TPU v7x, 256 devices: a whole 4x4x8 slice. The times are simulated.
256 devices in a mesh: blk: 16 (over y, x_hi, core), grp: 16 (over x_lo, z).
Axes of the slice: x: 4 (x_hi: 2, x_lo: 2; x = x_hi * 2 + x_lo), y: 4, z: 8, core: 2. Of those that a mesh axis runs over, the one named last changes fastest.
Arguments:
- points: bfloat16 [32768, 1536], P(('blk', 'grp')), may hold values from -6 to 6
- centroids: bfloat16 [16384, 1536], P(('blk', 'grp')), may hold values from -0.15625 to 0.15625
- pair_blocks: int32 [16, 2], P('blk'), may hold values from 0 to 15, as said below
- pair_valid: int32 [16, 2], P('blk'), may hold values from 0 to 1, as said below
- sizes: int32 [16384], replicated, may hold values from 64 to 1024
Outputs:
- new_centroids: float32 [16384, 1536], P(('blk', 'grp'))
Inputs may be any that keep to these rules, and one draw needn't show every extreme that they name: `pair_blocks`: column 0 is a permutation of the 16 centroid blocks; column 1 differs from column 0 in every row. `pair_valid`: column 0 is 1 in every row; column 1 is 0 in some rows.
All inputs are finite; a program needn't handle non-finite values.
Results may differ from a plain program's by a relative error of at most 0.0035.
Values may be sent and summed in bfloat16 or wider, within the bound.
No kernel may reach another device: no remote copies, remote signals or barrier semaphores. Data moves between devices by JAX's collectives and lax.ppermute only.
A program may use at most 128 MiB of HBM per device.

v0:
```python
import jax
import jax.numpy as jnp
from jax import lax
from jax.sharding import PartitionSpec as P

ITERS = 4


SCALE = 3.0


def shifted(block, axis, distance):
    devices = range(lax.axis_size(axis))
    route = [((i - distance) % len(devices), i) for i in devices]
    return lax.ppermute(block, axis, route)


def shards(points, centroids, pair_blocks, pair_valid, sizes):
    rows = points.shape[0]
    width = points.shape[1]
    part_rows = centroids.shape[0]
    n_blk = lax.axis_size("blk")
    n_grp = lax.axis_size("grp")
    block_len = part_rows * n_grp
    blk_index = lax.axis_index("blk")
    grp_index = lax.axis_index("grp")
    slots = pair_blocks[0]
    valid = pair_valid[0].astype(jnp.float32)
    size_f = sizes.astype(jnp.float32)
    total_points = rows * n_grp * n_blk
    targets = size_f * (jnp.float32(total_points) / jnp.sum(size_f))
    target_table = targets.reshape(n_blk, block_len)
    target_pair = jnp.take(target_table, slots, axis=0)
    onehot = (slots[:, None] == jnp.arange(n_blk, dtype=jnp.int32)[None, :]).astype(
        jnp.float32
    ) * valid[:, None]

    def check(step, visiting, kept):
        source = (blk_index - step) % n_blk
        match = (slots == source)[:, None, None]
        return jnp.where(match, visiting[None], kept)

    def turn(step, state):
        visiting, kept = state
        kept = check(step, visiting, kept)
        visiting = shifted(visiting, "blk", 1)
        return (visiting, kept)

    start_kept = jnp.zeros((2, part_rows, width), jnp.bfloat16)
    visiting, kept = lax.fori_loop(0, n_blk - 1, turn, (centroids, start_kept))
    kept = check(n_blk - 1, visiting, kept)
    dots = jnp.einsum(
        "rd,knd->rkn",
        points,
        lax.all_gather(kept, "grp", axis=1, tiled=True),
        preferred_element_type=jnp.float32,
    )
    kernel = jnp.exp(SCALE * dots) * valid[None, :, None]
    scale_v = jnp.ones((2, block_len), jnp.float32)
    scale_u = jnp.zeros((rows,), jnp.float32)
    for step in range(ITERS):
        rowsum = jnp.einsum("rkc,kc->r", kernel, scale_v, precision=lax.Precision.HIGHEST)
        scale_u = 1.0 / rowsum
        colpart = jnp.einsum("rkc,r->kc", kernel, scale_u, precision=lax.Precision.HIGHEST)
        table = jnp.einsum("kb,kc->bc", onehot, colpart, precision=lax.Precision.HIGHEST)
        totals = lax.psum(table, ("blk", "grp"))
        scale_v = target_pair / jnp.take(totals, slots, axis=0)
    weights = (scale_u[:, None, None] * kernel * scale_v[None]).astype(jnp.bfloat16)
    mine = lax.psum_scatter(
        jnp.einsum("rkc,rd->ckd", weights, points, preferred_element_type=jnp.float32),
        "grp",
        scatter_dimension=0,
        tiled=True,
    )
    spread = jnp.einsum("kb,ckd->bcd", onehot, mine, precision=lax.Precision.HIGHEST)
    owned = lax.psum_scatter(spread, "blk", scatter_dimension=0, tiled=True)
    own_targets = lax.dynamic_slice_in_dim(
        targets, blk_index * block_len + grp_index * part_rows, part_rows, 0
    )
    return owned[0] / own_targets[:, None]


def solution(mesh):
    placed = (P(("blk", "grp"), None), P(("blk", "grp"), None), P("blk", None), P("blk", None), P())
    return jax.shard_map(
        shards, mesh=mesh, in_specs=placed, out_specs=P(("blk", "grp"), None), check_vma=False
    )
```

profile of v0, /device:TPU:1, one launch (start us, length us, event | category | flops | bytes accessed | tf_op | source)
XLA Modules:
  0.0 1614.1 jit_solution(13617436699770496386)
XLA Ops:
  6.5 1.0 copy.55
  7.6 0.7 compare_and_fusion
  8.2 127.5 %while.18 = (s32[]{:T(128)}, bf16[64,1536]{1,0:T(8,128)(2,1)S(1)}, bf16[2,64,1536]{2,1,0:T(8,128)(2,1)S(1)}, s32[]{:T(128)}, s32[2]{0:T(128)}, /*index=5*/s32[]{:T(128)}, s32[]{:T(128)}, s32[]{:T(128)}, s32[]{:T(128)}) while((s32[]{:T(128)}, bf16[64,1536]{1,0:T(8,128)(2,1)S(1)}, bf16[2,64,1536]{2,1,0:T(8,128)(2,1)S(1)}, s32[]{:T(128)}, ...), condition=%wide.region_1.2_spmd.clone, body=%wide.region_0.0_spmd.clone.sunk | while | flops 393233 | bytes 2162968 | solution.py:50
  8.2 4.2 collective-permute-start
  12.4 0.7 broadcast_compare_fusion.3
  13.2 1.8 collective-permute-done
  15.1 4.1 collective-permute-start
  19.1 0.7 broadcast_compare_fusion.3
  19.9 1.8 collective-permute-done
  21.8 4.1 collective-permute-start
  25.8 0.7 broadcast_compare_fusion.3
  26.6 3.5 collective-permute-done
  30.1 2.4 collective-permute-start
  32.5 0.7 broadcast_compare_fusion.3
  33.3 5.6 collective-permute-done
  39.2 0.7 broadcast_compare_fusion.3
  40.0 7.7 collective-permute-done
  47.8 0.7 broadcast_compare_fusion.3
  48.6 7.9 collective-permute-done
  56.6 0.7 broadcast_compare_fusion.3
  57.4 7.9 collective-permute-done
  65.5 0.7 broadcast_compare_fusion.3
  66.2 7.9 collective-permute-done
  74.3 0.7 broadcast_compare_fusion.3
  75.0 7.9 collective-permute-done
  83.1 0.7 broadcast_compare_fusion.3
  83.8 7.9 collective-permute-done
  91.9 0.7 broadcast_compare_fusion.3
  92.6 7.9 collective-permute-done
  100.7 0.7 broadcast_compare_fusion.3
  101.4 7.9 collective-permute-done
  109.5 0.7 broadcast_compare_fusion.3
  110.2 7.9 collective-permute-done
  118.3 0.7 broadcast_compare_fusion.3
  119.1 7.9 collective-permute-done
  127.1 0.7 broadcast_compare_fusion.3
  127.9 7.9 collective-permute-done
  135.8 0.8 broadcast_select_fusion
  138.0 0.7 compare_select_fusion
  138.7 80.9 %all-gather.2.cloned.1.call-done = bf16[2,1024,1536]{2,1,0:T(8,128)(2,1)} async-done(((bf16[2,64,1536]{2,1,0:T(8,128)(2,1)}), bf16[2,1024,1536]{2,1,0:T(8,128)(2,1)}) %all-gather.2.cloned.1.call-update) | async-done | bytes 6291472 | tf_op jit(solution)/shard_map/all_gather | solution.py:55
  219.5 4.6 fusion.2
  224.8 1.0 fusion.61
  225.8 1.0 fusion.23
  227.4 238.6 %all-reduce.7.cloned.1.call-done = f32[16,1024]{1,0:T(8,128)} async-done(((f32[16,1024]{1,0:T(8,128)}), f32[16,1024]{1,0:T(8,128)}) %all-reduce.7.cloned.1.call-update) | async-done | bytes 65552 | tf_op jit(solution)/shard_map/psum | solution.py:66
  466.1 1.4 gather_fusion.1
  468.2 1.0 fusion.62
  469.2 1.0 fusion.21
  470.3 235.4 %all-reduce.9.cloned.1.call-done = f32[16,1024]{1,0:T(8,128)} async-done(((f32[16,1024]{1,0:T(8,128)}), f32[16,1024]{1,0:T(8,128)}) %all-reduce.9.cloned.1.call-update) | async-done | bytes 65552 | tf_op jit(solution)/shard_map/psum | solution.py:66
  705.6 1.4 gather_fusion.2
  707.8 1.0 fusion.63
  708.8 1.0 fusion.19
  709.9 235.2 %all-reduce.11.cloned.1.call-done = f32[16,1024]{1,0:T(8,128)} async-done(((f32[16,1024]{1,0:T(8,128)}), f32[16,1024]{1,0:T(8,128)}) %all-reduce.11.cloned.1.call-update) | async-done | bytes 65552 | tf_op jit(solution)/shard_map/psum | solution.py:66
  945.0 1.4 gather_fusion.3
  947.2 1.0 fusion.38
  948.2 1.0 fusion.17
  949.4 235.0 %all-reduce.13.cloned.1.call-done = f32[16,1024]{1,0:T(8,128)} async-done(((f32[16,1024]{1,0:T(8,128)}), f32[16,1024]{1,0:T(8,128)}) %all-reduce.13.cloned.1.call-update) | async-done | bytes 65552 | tf_op jit(solution)/shard_map/psum | solution.py:66
  1184.4 1.4 gather_fusion.4
  1185.9 1.8 fusion.12
  1187.7 29.1 %copy.39 = f32[2,1024,1536]{2,0,1:T(2,128)} copy(f32[2,1024,1536]{2,1,0:T(8,128)S(1)} %fusion.12) | data formatting | bytes 25165824 | tf_op jit(solution)/shard_map/rkc,rd->ckd/dot_general | solution.py:70
  1218.8 279.5 %all-reduce.15.cloned.1.call-done = f32[1024,2,1536]{2,1,0:T(2,128)} async-done(((f32[1024,2,1536]{2,1,0:T(2,128)}), f32[1024,2,1536]{2,1,0:T(2,128)}) %all-reduce.15.cloned.1.call-update) | async-done | bytes 12582928
  1498.2 6.7 fusion.10
  1505.0 6.3 copy.6
  1511.4 94.0 %reduce-scatter.2.cloned.1.call-done = f32[1,64,1536]{2,1,0:T(8,128)} async-done(((f32[16,64,1536]{2,1,0:T(8,128)}), f32[1,64,1536]{2,1,0:T(8,128)}) %reduce-scatter.2.cloned.1.call-update) | async-done | bytes 393232 | tf_op jit(solution)/shard_map/reduce_scatter | solution.py:76
  1605.4 1.8 bitcast_divide_fusion
  (82 shorter events, 8.9 us)
Async XLA Ops:
  6.5 213.0 %copy-start = (bf16[128,1536]{1,0:T(8,128)(2,1)S(1)}, bf16[128,1536]{1,0:T(8,128)(2,1)}, u32[]{:S(2)}) copy-start(bf16[128,1536]{1,0:T(8,128)(2,1)} %param.9) | copy-start | bytes 1179652
  6.5 132.1 %copy-start.3 = (s32[1,2]{1,0:T(1,128)S(1)}, s32[1,2]{1,0:T(1,128)}, u32[]{:S(2)}) copy-start(s32[1,2]{1,0:T(1,128)} %param.12) | copy-start | bytes 28
  6.5 130.1 %copy-start.1 = (s32[16384]{0:T(1024)S(1)}, s32[16384]{0:T(1024)}, u32[]{:S(2)}) copy-start(s32[16384]{0:T(1024)} %param.13) | copy-start | bytes 196612
  6.5 213.0 %all-gather.2.cloned.1.call-start = ((), (), s32[]{:S(2)}) async-start(), calls=%async_computation.1 | async-start | bytes 6684672 | tf_op jit(solution)/shard_map/all_gather | solution.py:55
  8.2 6.8 collective-permute-start
  15.1 6.7 collective-permute-start
  21.8 8.3 collective-permute-start
  30.1 8.8 collective-permute-start
  38.9 8.8 collective-permute-start
  47.7 8.8 collective-permute-start
  56.5 8.8 collective-permute-start
  65.3 8.8 collective-permute-start
  74.1 8.8 collective-permute-start
  82.9 8.8 collective-permute-start
  91.7 8.8 collective-permute-start
  100.6 8.8 collective-permute-start
  109.4 8.8 collective-permute-start
  118.2 8.8 collective-permute-start
  127.0 8.8 collective-permute-start
  135.8 90.0 %copy-start.2 = (s32[2]{0:T(128)S(1)}, s32[2]{0:T(128)}, u32[]{:S(2)}) copy-start(s32[2]{0:T(128)} %get-tuple-element.259) | copy-start | bytes 28
  136.6 329.4 %all-reduce.7.cloned.1.call-start = ((), (), s32[]{:S(2)}) async-start(), calls=%async_computation.2 | async-start | bytes 131072 | tf_op jit(solution)/shard_map/psum | solution.py:66
  226.8 478.9 %all-reduce.9.cloned.1.call-start = ((), (), s32[]{:S(2)}) async-start(), calls=%async_computation.3 | async-start | bytes 131072 | tf_op jit(solution)/shard_map/psum | solution.py:66
  470.2 474.8 %all-reduce.11.cloned.1.call-start = ((), (), s32[]{:S(2)}) async-start(), calls=%async_computation.4 | async-start | bytes 131072 | tf_op jit(solution)/shard_map/psum | solution.py:66
  709.8 474.6 %all-reduce.13.cloned.1.call-start = ((), (), s32[]{:S(2)}) async-start(), calls=%async_computation.5 | async-start | bytes 131072 | tf_op jit(solution)/shard_map/psum | solution.py:66
  949.2 549.0 %all-reduce.15.cloned.1.call-start = ((), (), s32[]{:S(2)}) async-start(), calls=%async_computation.7 | async-start | bytes 25165824
  1216.8 0.7 copy-start.4
  1216.9 388.5 %reduce-scatter.2.cloned.1.call-start = ((), (), s32[]{:S(2)}) async-start(), calls=%async_computation.6 | async-start | bytes 6684672 | tf_op jit(solution)/shard_map/reduce_scatter | solution.py:76
Sparse Core Ops, SparseCore 0:
  136.7 82.7 all-gather.1
  226.9 239.1 all-reduce.6
  471.6 234.0 all-reduce.8
  711.0 233.9 all-reduce.10
  950.4 233.9 all-reduce.12
  1217.0 281.1 all-reduce.14
  1511.4 93.9 reduce-scatter.1
where the time goes:
time: 1620 us; the launch traced here: 1610 us
  waiting for transfers between devices  1500 us (93%)
  local copies, waits for them, and re-layouts  44.1 us (3%)
  matrix products  23.7 us (1%)
  other arithmetic  16.5 us (1%)
  starting transfers between devices  16.3 us (1%)
    psum x4, waiting for transfers between devices, shards(): totals = lax.psum(table, ('blk', 'grp'))  944 us
    unnamed x8, waiting for transfers between devices  280 us
    ppermute x15, waiting for transfers between devices, shifted(): return lax.ppermute(block, axis, route)  99.4 us
    reduce_scatter x1, waiting for transfers between devices, shards(): owned = lax.psum_scatter(spread, 'blk', scatter_dimension=0, tiled=True)  94 us
    all_gather x1, waiting for transfers between devices, shards(): lax.all_gather(kept, 'grp', axis=1, tiled=True)  80.9 us
  transfers between devices with their start and end apart: 22, of which 22 were waited for; matrix products, arithmetic and copies ran while one was open for 1% of the time, Pallas kernels for 0%

commit v1 on v0

v1 whole, which is shorter than its diff:
```python
import jax
import jax.numpy as jnp
from jax import lax
from jax.sharding import Mesh, PartitionSpec as P

ITERS = 4
SCALE = 3.0
NY, NXH, NC, NXL, NZ = 4, 2, 2, 2, 8
NB = NY * NXH * NC
PLANE = ("y", "xh", "c", "xl")
SWAP = [(0, 1), (1, 0)]


def ordered(first, mine, other):
    is0 = first == 0
    return jnp.stack([jnp.where(is0, mine, other), jnp.where(is0, other, mine)])


def exchange(row, axes, n):
    return lax.all_to_all(jnp.broadcast_to(row[None], (n,) + row.shape), axes, 0, 0)


def shards(points, centroids, pair_blocks, pair_valid, sizes):
    width = points.shape[1]
    c = lax.axis_index("c")
    xl = lax.axis_index("xl")
    z = lax.axis_index("z")
    slots = pair_blocks[0]
    valid = pair_valid[0].astype(jnp.float32)

    pts = lax.all_gather(points, "z", axis=0, tiled=True)

    slots_other = lax.ppermute(slots, "c", SWAP)
    halves = centroids.reshape(2, 32, width)
    mine = lax.dynamic_index_in_dim(halves, c, 0, keepdims=False)
    give = lax.dynamic_index_in_dim(halves, 1 - c, 0, keepdims=False)
    got = lax.ppermute(give, "c", SWAP)
    both = ordered(c, mine, got)
    allc = lax.all_to_all(
        jnp.broadcast_to(both[None], (NY * NXH,) + both.shape), ("y", "xh"), 0, 0
    ).reshape(NB, 32, width)
    sel_mine = jnp.take(allc, slots, axis=0)
    sel_give = jnp.take(allc, slots_other, axis=0)
    sel_got = lax.ppermute(sel_give, "c", SWAP)
    kept = jnp.swapaxes(ordered(c, sel_mine, sel_got), 0, 1).reshape(2, 64, width)
    kept_xl = lax.ppermute(kept, "xl", SWAP)
    cents = jnp.swapaxes(ordered(xl, kept, kept_xl), 0, 1).reshape(256, width)

    size_f = sizes.astype(jnp.float32)
    targets = size_f * (jnp.float32(points.shape[0] * 256) / jnp.sum(size_f))
    table = jnp.take(targets.reshape(NB, 2, NZ, 64), z, axis=2).reshape(NB, 128)
    target_pair = jnp.take(table, slots, axis=0)

    dots = lax.dot_general(
        cents, pts, (((1,), (1,)), ((), ())), preferred_element_type=jnp.float32
    )
    kt = (jnp.exp(SCALE * dots).reshape(2, 128, -1) * valid[:, None, None]).reshape(256, -1)

    ids = jnp.pad(slots.astype(jnp.float32), (0, 126))

    def totals_of(colpart):
        got = exchange(jnp.concatenate([colpart, ids]), PLANE, NB * NXL)
        got_ids = got[:, 256:258].astype(jnp.int32)
        match = (got_ids[None] == slots[:, None, None]).astype(jnp.float32)
        cols = got[:, :256].reshape(-1, 2, 128)
        return jnp.sum(match[..., None] * cols[None], axis=(1, 2))

    scale_v = jnp.ones((256,), jnp.float32)
    for step in range(ITERS):
        rowpart = jnp.sum(kt * scale_v[:, None], axis=0)
        scale_u = 1.0 / jnp.sum(exchange(rowpart, "z", NZ), axis=0)
        if step < ITERS - 1:
            colpart = jnp.sum(kt * scale_u[None, :], axis=1)
            scale_v = (target_pair / totals_of(colpart)).reshape(256)
    weights = scale_u[None, :] * kt * scale_v[:, None]
    tot = totals_of(jnp.sum(weights, axis=1))
    sums = lax.dot_general(
        weights.astype(jnp.bfloat16), pts, (((1,), (0,)), ((), ())), preferred_element_type=jnp.float32
    ).reshape(2, 2, 64, width)
    s_mine = lax.dynamic_index_in_dim(sums, xl, 1, keepdims=False)
    s_give = lax.dynamic_index_in_dim(sums, 1 - xl, 1, keepdims=False).astype(jnp.bfloat16)
    s_got = lax.ppermute(s_give, "xl", SWAP)
    tot_mine = lax.dynamic_index_in_dim(tot.reshape(2, 2, 64), xl, 1, keepdims=False)
    means = ((s_mine + s_got.astype(jnp.float32)) / tot_mine[:, :, None]).astype(jnp.bfloat16)
    means = means.reshape(2, 2, 32, width)
    m_mine = lax.dynamic_index_in_dim(means, c, 1, keepdims=False)
    m_give = lax.dynamic_index_in_dim(means, 1 - c, 1, keepdims=False)
    m_got = lax.ppermute(m_give, "c", SWAP)

    blocks = jnp.arange(NB, dtype=jnp.int32)
    spread = jnp.zeros((NB, 32, width), jnp.float32)
    for part, ids_of, k in ((m_mine, slots, 0), (m_mine, slots, 1), (m_got, slots_other, 0), (m_got, slots_other, 1)):
        hit = (blocks == ids_of[k])[:, None, None]
        spread = spread + jnp.where(hit, part[k][None].astype(jnp.float32), 0.0)
    spread = spread.astype(jnp.bfloat16).reshape(NY * NXH, 2, 32, width)
    landed = lax.all_to_all(spread, ("y", "xh"), 0, 0)
    owned = jnp.sum(landed.astype(jnp.float32), axis=0)
    o_mine = lax.dynamic_index_in_dim(owned, c, 0, keepdims=False)
    o_give = lax.dynamic_index_in_dim(owned, 1 - c, 0, keepdims=False)
    o_got = lax.ppermute(o_give, "c", SWAP)
    return ordered(c, o_mine, o_got).reshape(64, width)


def solution(mesh):
    fine = Mesh(mesh.devices.reshape(NY, NXH, NC, NXL, NZ), ("y", "xh", "c", "xl", "z"))
    rows = P(("y", "xh", "c", "xl", "z"), None)
    pair = P(("y", "xh", "c"), None)
    return jax.shard_map(
        shards, mesh=fine, in_specs=(rows, rows, pair, pair, P()), out_specs=rows, check_vma=False
    )
```

time: 1620 us -> 213 us (0.13)
  waiting for transfers between devices: 1500 us -> 82 us
  blocking collectives: 0 us -> 37.7 us
  starting transfers between devices: 16.3 us -> 51.3 us
  local copies, waits for them, and re-layouts: 44.1 us -> 10.8 us
  matrix products: 23.7 us -> 5.79 us
    psum x4 -> x0, waiting for transfers between devices: 944 us -> none  [shards(): totals = lax.psum(table, ('blk', 'grp'))]
    unnamed x8 -> x1, waiting for transfers between devices: 280 us -> 0.71 us
    reduce_scatter x1 -> x0, waiting for transfers between devices: 94 us -> none  [shards(): owned = lax.psum_scatter(spread, 'blk', scatter_dimension=0, tiled=True)]
    ppermute x15 -> x7, waiting for transfers between devices: 99.4 us -> 18.7 us  [the longest x1 10.1 us: shards(): kept_xl = lax.ppermute(kept, 'xl', SWAP)]
    all_gather x1, waiting for transfers between devices: 80.9 us -> 1.76 us  [shards(): pts = lax.all_gather(points, 'z', axis=0, tiled=True)]
    all_to_all x0 -> x8, waiting for transfers between devices: none -> 60.9 us  [the longest x7 40.1 us: exchange(): lax.all_to_all(jnp.broadcast_to(row[None], (n,) + row.shape), axes, 0, 0)]
    all_to_all x0 -> x8, starting transfers between devices: none -> 41.1 us  [the longest x7 36.2 us: exchange(): lax.all_to_all(jnp.broadcast_to(row[None], (n,) + row.shape), axes, 0, 0)]
    all_to_all x0 -> x2, blocking collectives: none -> 37.7 us  [the longest x1 28.5 us: shards(): landed = lax.all_to_all(spread, ('y', 'xh'), 0, 0)]
  transfers between devices with their start and end apart: 22 -> 16, of which waited for: 22 -> 15; matrix products, arithmetic and copies ran while one was open for 1% -> 6% of each run, Pallas kernels for 0% -> 0%
where the time goes in v1:
time: 213 us; the launch traced here: 212 us
  waiting for transfers between devices  82 us (38%)
  starting transfers between devices  51.3 us (24%)
  blocking collectives  37.7 us (18%)
  between operations  14.5 us (7%)
  local copies, waits for them, and re-layouts  10.8 us (5%)
  other arithmetic  9.89 us (5%)
  matrix products  5.79 us (3%)
    all_to_all x7, waiting for transfers between devices, exchange(): lax.all_to_all(jnp.broadcast_to(row[None], (n,) + row.shape), axes, 0, 0)  40.1 us
    all_to_all x7, starting transfers between devices, exchange(): lax.all_to_all(jnp.broadcast_to(row[None], (n,) + row.shape), axes, 0, 0)  36.2 us
    all_to_all x1, blocking collectives, shards(): landed = lax.all_to_all(spread, ('y', 'xh'), 0, 0)  28.5 us
    all_to_all x1, waiting for transfers between devices, shards(): lax.all_to_all(jnp.broadcast_to(both[None], (NY * NXH,) + both.shape), ('...  20.8 us
    ppermute x1, waiting for transfers between devices, shards(): kept_xl = lax.ppermute(kept, 'xl', SWAP)  10.1 us
    all_to_all x1, blocking collectives, exchange(): lax.all_to_all(jnp.broadcast_to(row[None], (n,) + row.shape), axes, 0, 0)  9.25 us
    ppermute x1, waiting for transfers between devices, shards(): s_got = lax.ppermute(s_give, 'xl', SWAP)  5.74 us
    all_to_all x1, starting transfers between devices, shards(): lax.all_to_all(jnp.broadcast_to(both[None], (NY * NXH,) + both.shape), ('...  4.91 us
  transfers between devices with their start and end apart: 16, of which 15 were waited for; matrix products, arithmetic and copies ran while one was open for 6% of the time, Pallas kernels for 0%

profile of v1, /device:TPU:1, one launch (start us, length us, event | category | flops | bytes accessed | tf_op | source)
XLA Modules:
  0.0 212.1 jit_solution(14467531014042210681)
XLA Ops:
  6.5 0.7 all-gather.2.cloned.1.call-update
  7.3 0.9 dynamic-slice_bitcast_fusion.4
  8.2 3.2 %collective-permute-start = (bf16[32,1536]{1,0:T(8,128)(2,1)S(1)}, bf16[32,1536]{1,0:T(8,128)(2,1)S(1)}, u32[]{:S(2)}, u32[]{:S(2)}) collective-permute-start(bf16[32,1536]{1,0:T(8,128)(2,1)S(1)} %dynamic-slice_bitcast_fusion.4), channel_id=1, source_target_pairs={{0,16},{16,0},{1,17},{17,1},{2,18},{18,2},{3,19},{19,3},{4,20},{20... | collective-permute-start | bytes 294920 | tf_op jit(solution)/shard_map/ppermute | solution.py:37
  11.5 0.7 compare_select_fusion.1
  12.2 0.2 collective-permute-done
  12.4 0.9 fusion.15
  13.3 1.3 broadcast_in_dim.167
  14.6 4.9 %all-to-all-start = ((bf16[8,2,32,1536]{3,2,1,0:T(8,128)(2,1)}), bf16[8,2,32,1536]{3,2,1,0:T(8,128)(2,1)S(1)}, u32[]{:S(2)}, u32[]{:S(2)}) async-start(bf16[8,2,32,1536]{3,2,1,0:T(8,128)(2,1)} %broadcast_in_dim.167), calls=%async_computation | async-start | bytes 3145728 | tf_op jit(solution)/shard_map/all_to_all | solution.py:39
  19.5 0.6 convert_reduce_fusion.1
  21.0 20.8 %all-to-all-done = bf16[8,2,32,1536]{3,2,1,0:T(8,128)(2,1)S(1)} async-done(((bf16[8,2,32,1536]{3,2,1,0:T(8,128)(2,1)}), bf16[8,2,32,1536]{3,2,1,0:T(8,128)(2,1)S(1)}, u32[]{:S(2)}, u32[]{:S(2)}) %all-to-all-start) | async-done | bytes 1572896 | tf_op jit(solution)/shard_map/all_to_all | solution.py:39
  41.8 0.6 gather_fusion.2
  42.4 1.6 collective-permute-start.2
  44.1 0.6 gather_fusion.1
  44.6 0.5 collective-permute-done.2
  45.3 0.4 collective-permute-start.3
  45.7 10.1 %collective-permute-done.3 = bf16[2,64,1536]{2,1,0:T(8,128)(2,1)S(1)} collective-permute-done((bf16[2,64,1536]{2,1,0:T(8,128)(2,1)S(1)}, bf16[2,64,1536]{2,1,0:T(8,128)(2,1)S(1)}, u32[]{:S(2)}, u32[]{:S(2)}) %collective-permute-start.3) | collective-permute-done | bytes 393248 | tf_op jit(solution)/shard_map/ppermute | solution.py:46
  56.0 1.8 all-gather.2.cloned.1.call-done
  57.7 2.9 %fusion.29 = (f32[1024]{0:T(1024)S(1)}, f32[256,1024]{1,0:T(8,128)S(1)}) fusion(f32[256]{0:T(256)S(1)} %broadcast_bitcast_fusion, bf16[256,1536]{1,0:T(8,128)(2,1)S(1)} %bitcast.127, bf16[1024,1536]{1,0:T(8,128)(2,1)} %all-gather.2.cloned.1.call-done), kind=kOutput, calls=%fused_computation.103 | convolution fusion | flops 806091776 | bytes 4985856 | tf_op jit(solution)/shard_map/dot_general | solution.py:54
  60.7 0.6 broadcast_in_dim.173
  61.3 6.3 %all-to-all-start.1 = ((f32[8,1,1024]{2,1,0:T(1,128)}), f32[8,1,1024]{2,1,0:T(1,128)S(1)}, u32[]{:S(2)}, u32[]{:S(2)}) async-start(f32[8,1,1024]{2,1,0:T(1,128)} %broadcast_in_dim.173), calls=%async_computation.1 | async-start | bytes 65536 | tf_op jit(solution)/shard_map/all_to_all | solution.py:20
  67.7 6.9 %all-to-all-done.1 = f32[8,1,1024]{2,1,0:T(1,128)S(1)} async-done(((f32[8,1,1024]{2,1,0:T(1,128)}), f32[8,1,1024]{2,1,0:T(1,128)S(1)}, u32[]{:S(2)}, u32[]{:S(2)}) %all-to-all-start.1) | async-done | bytes 32800 | tf_op jit(solution)/shard_map/all_to_all | solution.py:20
  74.6 0.2 multiply_reduce_fusion.5
  74.8 0.6 broadcast_in_dim.174
  75.4 6.9 %all-to-all-start.2 = ((f32[32,1,384]{2,1,0:T(1,128)}), f32[32,1,384]{2,1,0:T(1,128)S(1)}, u32[]{:S(2)}, u32[]{:S(2)}) async-start(f32[32,1,384]{2,1,0:T(1,128)} %broadcast_in_dim.174), calls=%async_computation.2 | async-start | bytes 98304 | tf_op jit(solution)/shard_map/all_to_all | solution.py:20
  82.6 0.6 gather_fusion
  83.1 6.2 %all-to-all-done.2 = f32[32,1,384]{2,1,0:T(1,128)S(1)} async-done(((f32[32,1,384]{2,1,0:T(1,128)}), f32[32,1,384]{2,1,0:T(1,128)S(1)}, u32[]{:S(2)}, u32[]{:S(2)}) %all-to-all-start.2) | async-done | bytes 49184 | tf_op jit(solution)/shard_map/all_to_all | solution.py:20
  89.3 0.1 copy.46
  89.8 0.2 multiply_reduce_fusion.4
  90.0 9.2 %all_to_all.70 = f32[8,1,1024]{2,1,0:T(1,128)S(1)} all-to-all(f32[8,1,1024]{2,1,0:T(1,128)S(1)} %broadcast_in_dim.175), channel_id=1, replica_groups=mesh['y'=4,'xh'=2,'c'=2,'xl'=2,'z'=8] {'z'}, dimensions={0} | all-to-all | bytes 65536 | tf_op jit(solution)/shard_map/all_to_all | solution.py:20
  99.3 0.2 multiply_reduce_fusion.3
  99.5 0.6 broadcast_in_dim.176
  100.1 5.4 %all-to-all-start.4 = ((f32[32,1,384]{2,1,0:T(1,128)}), f32[32,1,384]{2,1,0:T(1,128)S(1)}, u32[]{:S(2)}, u32[]{:S(2)}) async-start(f32[32,1,384]{2,1,0:T(1,128)} %broadcast_in_dim.176), calls=%async_computation.4 | async-start | bytes 98304 | tf_op jit(solution)/shard_map/all_to_all | solution.py:20
  105.6 0.6 fusion.27
  106.1 6.5 %all-to-all-done.4 = f32[32,1,384]{2,1,0:T(1,128)S(1)} async-done(((f32[32,1,384]{2,1,0:T(1,128)}), f32[32,1,384]{2,1,0:T(1,128)S(1)}, u32[]{:S(2)}, u32[]{:S(2)}) %all-to-all-start.4) | async-done | bytes 49184 | tf_op jit(solution)/shard_map/all_to_all | solution.py:20
  113.2 0.2 multiply_reduce_fusion.2
  113.3 0.6 broadcast_in_dim.177
  114.0 3.3 %all-to-all-start.5 = ((f32[8,1,1024]{2,1,0:T(1,128)}), f32[8,1,1024]{2,1,0:T(1,128)S(1)}, u32[]{:S(2)}, u32[]{:S(2)}) async-start(f32[8,1,1024]{2,1,0:T(1,128)} %broadcast_in_dim.177), calls=%async_computation.5 | async-start | bytes 65536 | tf_op jit(solution)/shard_map/all_to_all | solution.py:20
  117.3 1.2 fusion.20
  118.5 5.6 %all-to-all-done.5 = f32[8,1,1024]{2,1,0:T(1,128)S(1)} async-done(((f32[8,1,1024]{2,1,0:T(1,128)}), f32[8,1,1024]{2,1,0:T(1,128)S(1)}, u32[]{:S(2)}, u32[]{:S(2)}) %all-to-all-start.5) | async-done | bytes 32800 | tf_op jit(solution)/shard_map/all_to_all | solution.py:20
  124.1 0.2 multiply_reduce_fusion.1
  124.3 0.6 broadcast_in_dim.178
  125.0 5.4 %all-to-all-start.6 = ((f32[32,1,384]{2,1,0:T(1,128)}), f32[32,1,384]{2,1,0:T(1,128)S(1)}, u32[]{:S(2)}, u32[]{:S(2)}) async-start(f32[32,1,384]{2,1,0:T(1,128)} %broadcast_in_dim.178), calls=%async_computation.6 | async-start | bytes 98304 | tf_op jit(solution)/shard_map/all_to_all | solution.py:20
  130.4 0.6 fusion.28
  131.0 6.5 %all-to-all-done.6 = f32[32,1,384]{2,1,0:T(1,128)S(1)} async-done(((f32[32,1,384]{2,1,0:T(1,128)}), f32[32,1,384]{2,1,0:T(1,128)S(1)}, u32[]{:S(2)}, u32[]{:S(2)}) %all-to-all-start.6) | async-done | bytes 49184 | tf_op jit(solution)/shard_map/all_to_all | solution.py:20
  138.0 0.2 multiply_reduce_fusion
  138.2 0.6 broadcast_in_dim.179
  138.8 3.3 %all-to-all-start.7 = ((f32[8,1,1024]{2,1,0:T(1,128)}), f32[8,1,1024]{2,1,0:T(1,128)S(1)}, u32[]{:S(2)}, u32[]{:S(2)}) async-start(f32[8,1,1024]{2,1,0:T(1,128)} %broadcast_in_dim.179), calls=%async_computation.7 | async-start | bytes 65536 | tf_op jit(solution)/shard_map/all_to_all | solution.py:20
  142.2 1.2 fusion.18
  143.3 5.6 %all-to-all-done.7 = f32[8,1,1024]{2,1,0:T(1,128)S(1)} async-done(((f32[8,1,1024]{2,1,0:T(1,128)}), f32[8,1,1024]{2,1,0:T(1,128)S(1)}, u32[]{:S(2)}, u32[]{:S(2)}) %all-to-all-start.7) | async-done | bytes 32800 | tf_op jit(solution)/shard_map/all_to_all | solution.py:20
  149.0 0.2 fusion.4
  149.2 0.6 broadcast_in_dim.180
  149.9 5.4 %all-to-all-start.8 = ((f32[32,1,384]{2,1,0:T(1,128)}), f32[32,1,384]{2,1,0:T(1,128)S(1)}, u32[]{:S(2)}, u32[]{:S(2)}) async-start(f32[32,1,384]{2,1,0:T(1,128)} %broadcast_in_dim.180), calls=%async_computation.8 | async-start | bytes 98304 | tf_op jit(solution)/shard_map/all_to_all | solution.py:20
  155.3 2.9 %fusion = f32[2,2,64,1536]{3,2,1,0:T(8,128)S(1)} fusion(bf16[2,2,64,1024]{3,2,1,0:T(8,128)(2,1)S(1)} %bitcast.123, bf16[1024,1536]{1,0:T(8,128)(2,1)} %all-gather.2.cloned.1.call-done), kind=kOutput, calls=%fused_computation.3 | convolution fusion | flops 805306368 | bytes 5242880 | tf_op jit(solution)/shard_map/dot_general | solution.py:77
  158.3 1.5 collective-permute-start.4
  159.7 2.7 %all-to-all-done.8 = f32[32,1,384]{2,1,0:T(1,128)S(1)} async-done(((f32[32,1,384]{2,1,0:T(1,128)}), f32[32,1,384]{2,1,0:T(1,128)S(1)}, u32[]{:S(2)}, u32[]{:S(2)}) %all-to-all-start.8) | async-done | bytes 49184 | tf_op jit(solution)/shard_map/all_to_all | solution.py:20
  163.0 5.7 %collective-permute-done.4 = bf16[2,64,1536]{2,1,0:T(8,128)(2,1)S(1)} collective-permute-done((bf16[2,64,1536]{2,1,0:T(8,128)(2,1)S(1)}, bf16[2,64,1536]{2,1,0:T(8,128)(2,1)S(1)}, u32[]{:S(2)}, u32[]{:S(2)}) %collective-permute-start.4) | collective-permute-done | bytes 393248 | tf_op jit(solution)/shard_map/ppermute | solution.py:82
  168.9 1.4 collective-permute-start.5
  170.3 1.0 collective-permute-done.5
  171.4 1.3 add_convert_fusion
  172.8 28.5 %all_to_all.71 = bf16[8,2,32,1536]{3,2,1,0:T(8,128)(2,1)S(1)} all-to-all(bf16[8,2,32,1536]{3,2,1,0:T(8,128)(2,1)S(1)} %add_convert_fusion), channel_id=1, replica_groups=mesh['y'=4,'xh'=2,'c'=2,'xl'=2,'z'=8] {'y','xh'}, dimensions={0} | all-to-all | bytes 3145728 | tf_op jit(solution)/shard_map/all_to_all | solution.py:96
  201.2 0.2 convert_reduce_fusion
  201.5 1.9 collective-permute-start.6
  203.4 1.1 collective-permute-done.6
  204.5 0.8 pad_maximum_fusion.2
  (77 shorter events, 3.1 us)
Async XLA Ops:
  6.5 14.3 %copy-start.1 = (s32[1,2]{1,0:T(1,128)S(1)}, s32[1,2]{1,0:T(1,128)}, u32[]{:S(2)}) copy-start(s32[1,2]{1,0:T(1,128)} %param.9) | copy-start | bytes 28
  6.5 13.0 %copy-start = (s32[16384]{0:T(1024)S(1)}, s32[16384]{0:T(1024)}, u32[]{:S(2)}) copy-start(s32[16384]{0:T(1024)} %param.11) | copy-start | bytes 196612
  6.5 14.3 %copy-start.2 = (s32[1,2]{1,0:T(1,128)S(1)}, s32[1,2]{1,0:T(1,128)}, u32[]{:S(2)}) copy-start(s32[1,2]{1,0:T(1,128)} %param.10) | copy-start | bytes 28
  6.5 51.2 %all-gather.2.cloned.1.call-start = ((), (), s32[]{:S(2)}) async-start(), calls=%async_computation.10 | async-start | bytes 3538944 | tf_op jit(solution)/shard_map/all_gather | solution.py:31
  8.2 4.2 %collective-permute-start = (bf16[32,1536]{1,0:T(8,128)(2,1)S(1)}, bf16[32,1536]{1,0:T(8,128)(2,1)S(1)}, u32[]{:S(2)}, u32[]{:S(2)}) collective-permute-start(bf16[32,1536]{1,0:T(8,128)(2,1)S(1)} %dynamic-slice_bitcast_fusion.4), channel_id=1, source_target_pairs={{0,16},{16,0},{1,17},{17,1},{2,18},{18,2},{3,19},{19,3},{4,20},{20... | collective-permute-start | bytes 294920 | tf_op jit(solution)/shard_map/ppermute | solution.py:37
  11.4 9.5 %collective-permute-start.1 = (s32[2]{0:T(128)}, s32[2]{0:T(128)S(1)}, u32[]{:S(2)}, u32[]{:S(2)}) collective-permute-start(s32[2]{0:T(128)} %bitcast.142), channel_id=1, source_target_pairs={{0,16},{16,0},{1,17},{17,1},{2,18},{18,2},{3,19},{19,3},{4,20},{20... | collective-permute-start | bytes 32 | tf_op jit(solution)/shard_map/ppermute | solution.py:33
  14.6 27.2 %all-to-all-start = ((bf16[8,2,32,1536]{3,2,1,0:T(8,128)(2,1)}), bf16[8,2,32,1536]{3,2,1,0:T(8,128)(2,1)S(1)}, u32[]{:S(2)}, u32[]{:S(2)}) async-start(bf16[8,2,32,1536]{3,2,1,0:T(8,128)(2,1)} %broadcast_in_dim.167), calls=%async_computation | async-start | bytes 3145728 | tf_op jit(solution)/shard_map/all_to_all | solution.py:39
  42.4 2.7 %collective-permute-start.2 = (bf16[2,32,1536]{2,1,0:T(8,128)(2,1)S(1)}, bf16[2,32,1536]{2,1,0:T(8,128)(2,1)S(1)}, u32[]{:S(2)}, u32[]{:S(2)}) collective-permute-start(bf16[2,32,1536]{2,1,0:T(8,128)(2,1)S(1)} %broadcast_select_fusion), channel_id=1, source_target_pairs={{0,16},{16,0},{1,17},{17,1},{2,18},{18,2},{3,19},{19,3},{4,20},{20... | collective-permute-start | bytes 589832 | tf_op jit(solution)/shard_map/ppermute | solution.py:44
  45.3 10.5 %collective-permute-start.3 = (bf16[2,64,1536]{2,1,0:T(8,128)(2,1)S(1)}, bf16[2,64,1536]{2,1,0:T(8,128)(2,1)S(1)}, u32[]{:S(2)}, u32[]{:S(2)}) collective-permute-start(bf16[2,64,1536]{2,1,0:T(8,128)(2,1)S(1)} %bitcast.124), channel_id=1, source_target_pairs={{0,8},{8,0},{1,9},{9,1},{2,10},{10,2},{3,11},{11,3},{4,12},{12,4},... | collective-permute-start | bytes 1179656 | tf_op jit(solution)/shard_map/ppermute | solution.py:46
  61.3 13.2 %all-to-all-start.1 = ((f32[8,1,1024]{2,1,0:T(1,128)}), f32[8,1,1024]{2,1,0:T(1,128)S(1)}, u32[]{:S(2)}, u32[]{:S(2)}) async-start(f32[8,1,1024]{2,1,0:T(1,128)} %broadcast_in_dim.173), calls=%async_computation.1 | async-start | bytes 65536 | tf_op jit(solution)/shard_map/all_to_all | solution.py:20
  75.4 13.9 %all-to-all-start.2 = ((f32[32,1,384]{2,1,0:T(1,128)}), f32[32,1,384]{2,1,0:T(1,128)S(1)}, u32[]{:S(2)}, u32[]{:S(2)}) async-start(f32[32,1,384]{2,1,0:T(1,128)} %broadcast_in_dim.174), calls=%async_computation.2 | async-start | bytes 98304 | tf_op jit(solution)/shard_map/all_to_all | solution.py:20
  100.1 12.6 %all-to-all-start.4 = ((f32[32,1,384]{2,1,0:T(1,128)}), f32[32,1,384]{2,1,0:T(1,128)S(1)}, u32[]{:S(2)}, u32[]{:S(2)}) async-start(f32[32,1,384]{2,1,0:T(1,128)} %broadcast_in_dim.176), calls=%async_computation.4 | async-start | bytes 98304 | tf_op jit(solution)/shard_map/all_to_all | solution.py:20
  114.0 10.1 %all-to-all-start.5 = ((f32[8,1,1024]{2,1,0:T(1,128)}), f32[8,1,1024]{2,1,0:T(1,128)S(1)}, u32[]{:S(2)}, u32[]{:S(2)}) async-start(f32[8,1,1024]{2,1,0:T(1,128)} %broadcast_in_dim.177), calls=%async_computation.5 | async-start | bytes 65536 | tf_op jit(solution)/shard_map/all_to_all | solution.py:20
  125.0 12.6 %all-to-all-start.6 = ((f32[32,1,384]{2,1,0:T(1,128)}), f32[32,1,384]{2,1,0:T(1,128)S(1)}, u32[]{:S(2)}, u32[]{:S(2)}) async-start(f32[32,1,384]{2,1,0:T(1,128)} %broadcast_in_dim.178), calls=%async_computation.6 | async-start | bytes 98304 | tf_op jit(solution)/shard_map/all_to_all | solution.py:20
  138.8 10.1 %all-to-all-start.7 = ((f32[8,1,1024]{2,1,0:T(1,128)}), f32[8,1,1024]{2,1,0:T(1,128)S(1)}, u32[]{:S(2)}, u32[]{:S(2)}) async-start(f32[8,1,1024]{2,1,0:T(1,128)} %broadcast_in_dim.179), calls=%async_computation.7 | async-start | bytes 65536 | tf_op jit(solution)/shard_map/all_to_all | solution.py:20
  149.9 12.6 %all-to-all-start.8 = ((f32[32,1,384]{2,1,0:T(1,128)}), f32[32,1,384]{2,1,0:T(1,128)S(1)}, u32[]{:S(2)}, u32[]{:S(2)}) async-start(f32[32,1,384]{2,1,0:T(1,128)} %broadcast_in_dim.180), calls=%async_computation.8 | async-start | bytes 98304 | tf_op jit(solution)/shard_map/all_to_all | solution.py:20
  158.3 10.4 %collective-permute-start.4 = (bf16[2,64,1536]{2,1,0:T(8,128)(2,1)S(1)}, bf16[2,64,1536]{2,1,0:T(8,128)(2,1)S(1)}, u32[]{:S(2)}, u32[]{:S(2)}) collective-permute-start(bf16[2,64,1536]{2,1,0:T(8,128)(2,1)S(1)} %fusion.8), channel_id=1, source_target_pairs={{0,8},{8,0},{1,9},{9,1},{2,10},{10,2},{3,11},{11,3},{4,12},{12,4},... | collective-permute-start | bytes 1179656 | tf_op jit(solution)/shard_map/ppermute | solution.py:82
  168.9 2.5 %collective-permute-start.5 = (bf16[2,32,1536]{2,1,0:T(8,128)(2,1)S(1)}, bf16[2,32,1536]{2,1,0:T(8,128)(2,1)S(1)}, u32[]{:S(2)}, u32[]{:S(2)}) collective-permute-start(bf16[2,32,1536]{2,1,0:T(8,128)(2,1)S(1)} %dynamic-slice_bitcast_fusion.1), channel_id=1, source_target_pairs={{0,16},{16,0},{1,17},{17,1},{2,18},{18,2},{3,19},{19,3},{4,20},{20... | collective-permute-start | bytes 589832 | tf_op jit(solution)/shard_map/ppermute | solution.py:88
  201.5 3.0 %collective-permute-start.6 = (f32[32,1536]{1,0:T(8,128)S(1)}, f32[32,1536]{1,0:T(8,128)S(1)}, u32[]{:S(2)}, u32[]{:S(2)}) collective-permute-start(f32[32,1536]{1,0:T(8,128)S(1)} %dynamic-slice_bitcast_fusion), channel_id=1, source_target_pairs={{0,16},{16,0},{1,17},{17,1},{2,18},{18,2},{3,19},{19,3},{4,20},{20... | collective-permute-start | bytes 589832 | tf_op jit(solution)/shard_map/ppermute | solution.py:100
Sparse Core Ops, SparseCore 0:
  9.2 48.5 all-gather.1

commit v2 on v1

v2 whole, which is shorter than its diff:
```python
import jax
import jax.numpy as jnp
from jax import lax
from jax.sharding import Mesh, PartitionSpec as P

ITERS = 4
SCALE = 3.0
NY, NXH, NC, NXL, NZ = 4, 2, 2, 2, 8
NB = NY * NXH * NC
PLANE = ("y", "xh", "c", "xl")
SWAP = [(0, 1), (1, 0)]
UP = [(i, (i + 1) % NZ) for i in range(NZ)]
DOWN = [(i, (i - 1) % NZ) for i in range(NZ)]
after = lax.optimization_barrier


def ordered(first, mine, other):
    is0 = first == 0
    return jnp.stack([jnp.where(is0, mine, other), jnp.where(is0, other, mine)])


def exchange(row, axes, n):
    return lax.all_to_all(jnp.broadcast_to(row[None], (n,) + row.shape), axes, 0, 0)


def shards(points, centroids, pair_blocks, pair_valid, sizes):
    rows, width = points.shape
    c = lax.axis_index("c")
    xl = lax.axis_index("xl")
    z = lax.axis_index("z")
    me = lax.axis_index(("y", "xh", "c"))
    def put(buf, part, at):
        return lax.dynamic_update_slice(buf, part[None], (at % NZ, 0, 0))

    spread_cents = jnp.broadcast_to(centroids[None], (NY * NXH,) + centroids.shape)
    allc = lax.all_to_all(spread_cents, ("y", "xh"), 0, 0)
    up1 = lax.ppermute(points, "z", UP)
    down1 = lax.ppermute(points, "z", DOWN)
    pair_blocks, points, sizes, pair_valid, _ = after((pair_blocks, points, sizes, pair_valid, up1))
    slots = pair_blocks[0]
    valid = pair_valid[0].astype(jnp.float32)
    slots_other = lax.ppermute(slots, "c", SWAP)
    ids4 = jnp.concatenate([slots, slots_other])
    grid = lax.broadcasted_iota(jnp.int32, (4, NY * NXH, NC), 1) * NC + lax.broadcasted_iota(
        jnp.int32, (4, NY * NXH, NC), 2
    )
    hits = ids4[:, None, None] == grid
    up2 = lax.ppermute(up1, "z", UP)
    down2 = lax.ppermute(down1, "z", DOWN)
    pts = put(jnp.zeros((NZ, rows, width), points.dtype), points, z)
    pts = put(put(pts, up1, z - 1 + NZ), down1, z + 1)
    up3 = lax.ppermute(up2, "z", UP)
    down3 = lax.ppermute(down2, "z", DOWN)
    pts = put(put(pts, up2, z - 2 + NZ), down2, z + 2)

    allc, _ = after((allc, up2))
    sel_give = allc.at[slots_other // NC].get(mode="promise_in_bounds")
    sel_got = lax.ppermute(sel_give, "c", SWAP)
    sel_mine = allc.at[slots // NC].get(mode="promise_in_bounds")
    kept = jnp.where((slots % NC == c)[:, None, None], sel_mine, sel_got)
    kept_xl = lax.ppermute(kept, "xl", SWAP)
    far = lax.ppermute(up3, "z", UP)
    pts = put(put(pts, up3, z - 3 + NZ), down3, z + 3)
    pts = put(pts, far, z + 4).reshape(NZ * rows, width)
    cents = jnp.swapaxes(ordered(xl, kept, kept_xl), 0, 1).reshape(256, width)

    size_f = sizes.astype(jnp.float32)
    targets = size_f * (jnp.float32(points.shape[0] * 256) / jnp.sum(size_f))
    table = lax.dynamic_index_in_dim(targets.reshape(NB, 2, NZ, 64), z, 2, keepdims=False).reshape(NB, 128)
    target_pair = table.at[slots].get(mode="promise_in_bounds")

    dots = lax.dot_general(
        cents, pts, (((1,), (1,)), ((), ())), preferred_element_type=jnp.float32
    )
    kt = (jnp.exp(SCALE * dots).reshape(2, 128, -1) * valid[:, None, None]).reshape(256, -1)

    ids = jnp.pad(slots.astype(jnp.float32), (0, 126))
    kt, target_pair, ids, hits, slots, me = after((kt, target_pair, ids, hits, slots, me))

    def totals_of(match, got):
        return jnp.sum(match[..., None] * got[:, :256].reshape(1, -1, 2, 128), axis=(1, 2))

    scale_v = jnp.ones((256,), jnp.float32)
    for step in range(ITERS):
        rowpart = jnp.sum(kt * scale_v[:, None], axis=0)
        scale_u = 1.0 / jnp.sum(exchange(rowpart, "z", NZ), axis=0)
        if step < ITERS - 1:
            colpart = jnp.sum(kt * scale_u[None, :], axis=1)
            if step == 0:
                got = exchange(jnp.concatenate([colpart, ids]), PLANE, NB * NXL)
                got_ids = got[:, 256:258].astype(jnp.int32)
                match = (got_ids[None] == slots[:, None, None]).astype(jnp.float32)
                match_me = (got_ids[None] == me).astype(jnp.float32)
                got, match, match_me = after((got, match, match_me))
            else:
                got = exchange(colpart, PLANE, NB * NXL)
            scale_v = (target_pair / totals_of(match, got)).reshape(256)
    weights = scale_u[None, :] * kt * scale_v[:, None]
    weights = weights.astype(jnp.bfloat16)
    colpart = jnp.sum(weights.astype(jnp.float32), axis=1)

    parts = []
    tot = exchange(colpart, PLANE, NB * NXL)
    for k in (0, 1):
        sums = lax.dot_general(
            weights[128 * k : 128 * (k + 1)], pts, (((1,), (0,)), ((), ())), preferred_element_type=jnp.float32
        ).reshape(2, 64, width)
        mine = lax.dynamic_index_in_dim(sums, xl, 0, keepdims=False)
        give = lax.dynamic_index_in_dim(sums, 1 - xl, 0, keepdims=False).astype(jnp.bfloat16)
        got = lax.ppermute(give, "xl", SWAP)
        sums = (mine + got.astype(jnp.float32)).astype(jnp.bfloat16).reshape(2, 32, width)
        m_mine = lax.dynamic_index_in_dim(sums, c, 0, keepdims=False)
        m_give = lax.dynamic_index_in_dim(sums, 1 - c, 0, keepdims=False)
        m_got = lax.ppermute(m_give, "c", SWAP)
        parts += [m_mine, m_got]
    zero = jnp.zeros((), jnp.bfloat16)

    def placed(first, second, a, b):
        return jnp.where(first[:, :, None, None], a, jnp.where(second[:, :, None, None], b, zero))

    parts, tot = after((parts, tot))
    spread = placed(hits[0], hits[1], parts[0], parts[2]) + placed(hits[2], hits[3], parts[1], parts[3])
    landed = lax.all_to_all(spread, ("y", "xh"), 0, 0)
    owned = jnp.sum(landed.astype(jnp.float32), axis=0)
    o_mine = lax.dynamic_index_in_dim(owned, c, 0, keepdims=False)
    o_give = lax.dynamic_index_in_dim(owned, 1 - c, 0, keepdims=False)
    o_got = lax.ppermute(o_give, "c", SWAP)
    tot = totals_of(match_me, tot).reshape(2, 64)
    tot = lax.dynamic_index_in_dim(tot, xl, 0, keepdims=False)
    return ordered(c, o_mine, o_got).reshape(64, width) / tot[:, None]


def solution(mesh):
    fine = Mesh(mesh.devices.reshape(NY, NXH, NC, NXL, NZ), ("y", "xh", "c", "xl", "z"))
    rows = P(("y", "xh", "c", "xl", "z"), None)
    pair = P(("y", "xh", "c"), None)
    return jax.shard_map(
        shards, mesh=fine, in_specs=(rows, rows, pair, pair, P()), out_specs=rows, check_vma=False
    )
```

time: 213 us -> 204 us (0.958)
  blocking collectives: 37.7 us -> 71.5 us
  waiting for transfers between devices: 82 us -> 57.7 us
  between operations: 14.5 us -> 1.24 us
  starting transfers between devices: 51.3 us -> 41.6 us
  local copies, waits for them, and re-layouts: 10.8 us -> 16.8 us
  other arithmetic: 9.89 us -> 7.68 us
    all_to_all x1 -> x6, blocking collectives: 9.25 us -> 71.5 us  [exchange(): lax.all_to_all(jnp.broadcast_to(row[None], (n,) + row.shape), axes, 0, 0)]
    all_to_all x7 -> x2, waiting for transfers between devices: 40.1 us -> 10.5 us  [exchange(): lax.all_to_all(jnp.broadcast_to(row[None], (n,) + row.shape), axes, 0, 0)]
    all_to_all x1 -> x0, blocking collectives: 28.5 us -> none  [shards(): landed = lax.all_to_all(spread, ('y', 'xh'), 0, 0)]
    all_to_all x7 -> x2, starting transfers between devices: 36.2 us -> 9.28 us  [exchange(): lax.all_to_all(jnp.broadcast_to(row[None], (n,) + row.shape), axes, 0, 0)]
    ppermute x2 -> x9, waiting for transfers between devices: 5.93 us -> 15.5 us  [the longest x1 8.43 us: shards(): up3 = lax.ppermute(up2, 'z', UP)]
    ppermute x2 -> x9, starting transfers between devices: 4.71 us -> 13.7 us  [the longest x1 4.03 us: shards(): down1 = lax.ppermute(points, 'z', DOWN)]
    all_to_all x1 -> x2, starting transfers between devices: 4.91 us -> 10.4 us  [the longest x1 6.78 us: shards(): allc = lax.all_to_all(spread_cents, ('y', 'xh'), 0, 0)]
    dynamic_update_slice x0 -> x8, local copies, waits for them, and re-layouts: none -> 5.25 us  [put(): return lax.dynamic_update_slice(buf, part[None], (at % NZ, 0, 0))]
  transfers between devices with their start and end apart: 16 -> 19, of which waited for: 15 -> 8; matrix products, arithmetic and copies ran while one was open for 6% -> 10% of each run, Pallas kernels for 0% -> 0%
where the time goes in v2:
time: 204 us; the launch traced here: 203 us
  blocking collectives  71.5 us (35%)
  waiting for transfers between devices  57.7 us (28%)
  starting transfers between devices  41.6 us (20%)
  local copies, waits for them, and re-layouts  16.8 us (8%)
  other arithmetic  7.68 us (4%)
  matrix products  6.12 us (3%)
    all_to_all x6, blocking collectives, exchange(): lax.all_to_all(jnp.broadcast_to(row[None], (n,) + row.shape), axes, 0, 0)  71.5 us
    all_to_all x1, waiting for transfers between devices, shards(): landed = lax.all_to_all(spread, ('y', 'xh'), 0, 0)  21.9 us
    all_to_all x2, waiting for transfers between devices, exchange(): lax.all_to_all(jnp.broadcast_to(row[None], (n,) + row.shape), axes, 0, 0)  10.5 us
    all_to_all x2, starting transfers between devices, exchange(): lax.all_to_all(jnp.broadcast_to(row[None], (n,) + row.shape), axes, 0, 0)  9.28 us
    ppermute x1, waiting for transfers between devices, shards(): kept_xl = lax.ppermute(kept, 'xl', SWAP)  8.77 us
    ppermute x1, waiting for transfers between devices, shards(): up3 = lax.ppermute(up2, 'z', UP)  8.43 us
    ppermute x1, waiting for transfers between devices, shards(): up2 = lax.ppermute(up1, 'z', UP)  6.92 us
    all_to_all x1, starting transfers between devices, shards(): allc = lax.all_to_all(spread_cents, ('y', 'xh'), 0, 0)  6.78 us
  transfers between devices with their start and end apart: 19, of which 8 were waited for; matrix products, arithmetic and copies ran while one was open for 10% of the time, Pallas kernels for 0%

profile of v2, /device:TPU:1, one launch (start us, length us, event | category | flops | bytes accessed | tf_op | source)
XLA Modules:
  0.0 202.7 jit_solution(16599754485865091942)
XLA Ops:
  0.0 2.5 %collective-permute-start = (bf16[128,1536]{1,0:T(8,128)(2,1)}, bf16[128,1536]{1,0:T(8,128)(2,1)}, u32[]{:S(2)}, u32[]{:S(2)}) collective-permute-start(bf16[128,1536]{1,0:T(8,128)(2,1)} %param.5), channel_id=1, source_target_pairs={{0,1},{1,2},{2,3},{3,4},{4,5},{5,6},{6,7},{7,0},{8,9},{9,10},{10,1... | collective-permute-start | bytes 1179656 | tf_op jit(solution)/shard_map/ppermute | solution.py:37
  2.6 4.0 %collective-permute-start.5 = (bf16[128,1536]{1,0:T(8,128)(2,1)}, bf16[128,1536]{1,0:T(8,128)(2,1)}, u32[]{:S(2)}, u32[]{:S(2)}) collective-permute-start(bf16[128,1536]{1,0:T(8,128)(2,1)} %param.5), channel_id=1, source_target_pairs={{0,7},{1,0},{2,1},{3,2},{4,3},{5,4},{6,5},{7,6},{8,15},{9,8},{10,9... | collective-permute-start | bytes 1179656 | tf_op jit(solution)/shard_map/ppermute | solution.py:38
  6.6 2.2 %broadcast_in_dim.163 = bf16[8,64,1536]{2,1,0:T(8,128)(2,1)} broadcast(bf16[64,1536]{1,0:T(8,128)(2,1)} %param.6), dimensions={1,2} | broadcast | bytes 1769472 | tf_op jit(solution)/shard_map/broadcast_in_dim | solution.py:35
  8.8 6.8 %all-to-all-start = ((bf16[8,64,1536]{2,1,0:T(8,128)(2,1)}), bf16[8,64,1536]{2,1,0:T(8,128)(2,1)}, u32[]{:S(2)}, u32[]{:S(2)}) async-start(bf16[8,64,1536]{2,1,0:T(8,128)(2,1)} %broadcast_in_dim.163), calls=%async_computation | async-start | bytes 3145728 | tf_op jit(solution)/shard_map/all_to_all | solution.py:36
  15.6 0.5 iota_multiply_fusion
  16.1 0.5 fusion.11
  16.6 1.3 collective-permute-start.2
  18.0 0.6 broadcast_bitcast_fusion
  18.6 0.6 convert_reduce_fusion.2
  20.1 0.6 gather_fusion.2
  20.7 0.5 pad.4
  21.2 0.3 broadcast_in_dim.165
  21.6 2.7 %collective-permute-start.6 = (bf16[128,1536]{1,0:T(8,128)(2,1)}, bf16[128,1536]{1,0:T(8,128)(2,1)S(1)}, u32[]{:S(2)}, u32[]{:S(2)}) collective-permute-start(bf16[128,1536]{1,0:T(8,128)(2,1)} %collective-permute-done.5), channel_id=1, source_target_pairs={{0,7},{1,0},{2,1},{3,2},{4,3},{5,4},{6,5},{7,6},{8,15},{9,8},{10,9... | collective-permute-start | bytes 1179656 | tf_op jit(solution)/shard_map/ppermute | solution.py:49
  24.3 1.0 bitcast_dynamic-update-slice_fusion.6
  25.3 1.0 bitcast_dynamic-update-slice_fusion.5
  26.6 6.9 %collective-permute-done.1 = bf16[128,1536]{1,0:T(8,128)(2,1)S(1)} collective-permute-done((bf16[128,1536]{1,0:T(8,128)(2,1)}, bf16[128,1536]{1,0:T(8,128)(2,1)S(1)}, u32[]{:S(2)}, u32[]{:S(2)}) %collective-permute-start.1) | collective-permute-done | bytes 393248 | tf_op jit(solution)/shard_map/ppermute | solution.py:48
  33.5 2.8 %collective-permute-start.8 = (bf16[128,1536]{1,0:T(8,128)(2,1)S(1)}, bf16[128,1536]{1,0:T(8,128)(2,1)}, u32[]{:S(2)}, u32[]{:S(2)}) collective-permute-start(bf16[128,1536]{1,0:T(8,128)(2,1)S(1)} %collective-permute-done.6), channel_id=1, source_target_pairs={{0,7},{1,0},{2,1},{3,2},{4,3},{5,4},{6,5},{7,6},{8,15},{9,8},{10,9... | collective-permute-start | bytes 1179656 | tf_op jit(solution)/shard_map/ppermute | solution.py:53
  36.3 8.4 %collective-permute-done.7 = bf16[128,1536]{1,0:T(8,128)(2,1)} collective-permute-done((bf16[128,1536]{1,0:T(8,128)(2,1)S(1)}, bf16[128,1536]{1,0:T(8,128)(2,1)}, u32[]{:S(2)}, u32[]{:S(2)}) %collective-permute-start.7) | collective-permute-done | bytes 393248 | tf_op jit(solution)/shard_map/ppermute | solution.py:52
  44.7 1.1 bitcast_dynamic-update-slice_fusion.2
  45.8 2.7 %gather_fusion.1 = bf16[2,64,1536]{2,1,0:T(8,128)(2,1)} fusion(bf16[8,64,1536]{2,1,0:T(8,128)(2,1)} %all-to-all-done, s32[1024]{0:T(1024)S(1)} %pad_clamp_fusion.1), kind=kCustom, calls=%fused_computation.1 | custom fusion | bytes 786440 | tf_op jit(solution)/shard_map/gather | solution.py:57
  48.5 1.6 collective-permute-start.3
  50.1 1.0 bitcast_dynamic-update-slice_fusion.1
  51.2 2.0 gather_fusion
  53.2 1.1 broadcast_select_fusion
  54.3 0.9 collective-permute-start.4
  55.1 0.2 collective-permute-done.9
  55.3 1.0 bitcast_dynamic-update-slice_fusion
  56.3 8.8 %collective-permute-done.4 = bf16[2,64,1536]{2,1,0:T(8,128)(2,1)S(1)} collective-permute-done((bf16[2,64,1536]{2,1,0:T(8,128)(2,1)S(1)}, bf16[2,64,1536]{2,1,0:T(8,128)(2,1)S(1)}, u32[]{:S(2)}, u32[]{:S(2)}) %collective-permute-start.4) | collective-permute-done | bytes 393248 | tf_op jit(solution)/shard_map/ppermute | solution.py:61
  65.3 2.9 %fusion.1 = f32[256,1024]{1,0:T(8,128)S(1)} fusion(bf16[256,1536]{1,0:T(8,128)(2,1)S(1)} %bitcast.133, bf16[1024,1536]{1,0:T(8,128)(2,1)} %bitcast.128, f32[256]{0:T(256)S(1)} %copy-done.9), kind=kOutput, calls=%fused_computation.7 | convolution fusion | flops 805830656 | bytes 4981760 | tf_op jit(solution)/shard_map/dot_general | solution.py:72
  68.3 12.7 %all_to_all.64 = f32[8,1,1024]{2,1,0:T(1,128)S(1)} all-to-all(f32[8,1,1024]{2,1,0:T(1,128)S(1)} %broadcast_in_dim.176), channel_id=1, replica_groups=mesh['y'=4,'xh'=2,'c'=2,'xl'=2,'z'=8] {'z'}, dimensions={0} | all-to-all | bytes 65536 | tf_op jit(solution)/shard_map/all_to_all | solution.py:23
  81.1 0.2 multiply_reduce_fusion.5
  81.3 16.3 %all_to_all.65 = f32[32,1,384]{2,1,0:T(1,128)S(1)} all-to-all(f32[32,1,384]{2,1,0:T(1,128)S(1)} %broadcast_in_dim.177), channel_id=1, replica_groups=mesh['y'=4,'xh'=2,'c'=2,'xl'=2,'z'=8] {'y','xh','c','xl'}, dimensions={0} | all-to-all | bytes 98304 | tf_op jit(solution)/shard_map/all_to_all | solution.py:23
  97.6 0.1 copy.57
  97.9 0.1 multiply_reduce_fusion.8
  98.0 0.2 multiply_reduce_fusion.4
  98.2 9.2 %all_to_all.66 = f32[8,1,1024]{2,1,0:T(1,128)S(1)} all-to-all(f32[8,1,1024]{2,1,0:T(1,128)S(1)} %broadcast_in_dim.178), channel_id=1, replica_groups=mesh['y'=4,'xh'=2,'c'=2,'xl'=2,'z'=8] {'z'}, dimensions={0} | all-to-all | bytes 65536 | tf_op jit(solution)/shard_map/all_to_all | solution.py:23
  107.5 0.2 multiply_reduce_fusion.3
  107.7 12.0 %all_to_all.67 = f32[32,1,256]{2,1,0:T(1,128)S(1)} all-to-all(f32[32,1,256]{2,1,0:T(1,128)S(1)} %broadcast_in_dim.179), channel_id=1, replica_groups=mesh['y'=4,'xh'=2,'c'=2,'xl'=2,'z'=8] {'y','xh','c','xl'}, dimensions={0} | all-to-all | bytes 65536 | tf_op jit(solution)/shard_map/all_to_all | solution.py:23
  119.8 0.2 multiply_reduce_fusion.2
  120.0 9.3 %all_to_all.68 = f32[8,1,1024]{2,1,0:T(1,128)S(1)} all-to-all(f32[8,1,1024]{2,1,0:T(1,128)S(1)} %broadcast_in_dim.180), channel_id=1, replica_groups=mesh['y'=4,'xh'=2,'c'=2,'xl'=2,'z'=8] {'z'}, dimensions={0} | all-to-all | bytes 65536 | tf_op jit(solution)/shard_map/all_to_all | solution.py:23
  129.3 0.2 multiply_reduce_fusion.1
  129.5 12.0 %all_to_all.69 = f32[32,1,256]{2,1,0:T(1,128)S(1)} all-to-all(f32[32,1,256]{2,1,0:T(1,128)S(1)} %broadcast_in_dim.181), channel_id=1, replica_groups=mesh['y'=4,'xh'=2,'c'=2,'xl'=2,'z'=8] {'y','xh','c','xl'}, dimensions={0} | all-to-all | bytes 65536 | tf_op jit(solution)/shard_map/all_to_all | solution.py:23
  141.5 0.2 multiply_reduce_fusion
  141.7 0.6 broadcast_in_dim.182
  142.3 3.3 %all-to-all-start.7 = ((f32[8,1,1024]{2,1,0:T(1,128)}), f32[8,1,1024]{2,1,0:T(1,128)S(1)}, u32[]{:S(2)}, u32[]{:S(2)}) async-start(f32[8,1,1024]{2,1,0:T(1,128)} %broadcast_in_dim.182), calls=%async_computation.7 | async-start | bytes 65536 | tf_op jit(solution)/shard_map/all_to_all | solution.py:23
  145.7 6.8 %all-to-all-done.7 = f32[8,1,1024]{2,1,0:T(1,128)S(1)} async-done(((f32[8,1,1024]{2,1,0:T(1,128)}), f32[8,1,1024]{2,1,0:T(1,128)S(1)}, u32[]{:S(2)}, u32[]{:S(2)}) %all-to-all-start.7) | async-done | bytes 32800 | tf_op jit(solution)/shard_map/all_to_all | solution.py:23
  152.5 0.2 convert_reduce_fusion.1
  152.8 2.6 %fusion.17 = f32[2,64,1536]{2,1,0:T(8,128)S(1)} fusion(bf16[2,64,1024]{2,1,0:T(8,128)(2,1)S(1)} %bitcast.132, bf16[1024,1536,1]{1,0,2:T(8,128)(2,1)} %bitcast.129), kind=kOutput, calls=%fused_computation.105 | convolution fusion | flops 402653184 | bytes 4194304 | tf_op jit(solution)/shard_map/dot_general | solution.py:105
  155.5 0.4 collective-permute-start.12
  155.9 0.6 fusion.16
  156.6 1.2 collective-permute-start.10
  157.8 0.6 broadcast_in_dim.183
  158.4 5.9 %all-to-all-start.8 = ((f32[32,1,256]{2,1,0:T(1,128)}), f32[32,1,256]{2,1,0:T(1,128)S(1)}, u32[]{:S(2)}, u32[]{:S(2)}) async-start(f32[32,1,256]{2,1,0:T(1,128)} %broadcast_in_dim.183), calls=%async_computation.8 | async-start | bytes 65536 | tf_op jit(solution)/shard_map/all_to_all | solution.py:23
  164.4 0.7 collective-permute-start.13
  165.2 2.0 %collective-permute-start.11 = (bf16[32,1536]{1,0:T(8,128)(2,1)S(1)}, bf16[32,1536]{1,0:T(8,128)(2,1)S(1)}, u32[]{:S(2)}, u32[]{:S(2)}) collective-permute-start(bf16[32,1536]{1,0:T(8,128)(2,1)S(1)} %get-tuple-element.53), channel_id=1, source_target_pairs={{0,16},{16,0},{1,17},{17,1},{2,18},{18,2},{3,19},{19,3},{4,20},{20... | collective-permute-start | bytes 294920 | tf_op jit(solution)/shard_map/ppermute | solution.py:114
  167.3 0.1 copy.55
  167.7 3.8 %all-to-all-done.8 = f32[32,1,256]{2,1,0:T(1,128)S(1)} async-done(((f32[32,1,256]{2,1,0:T(1,128)}), f32[32,1,256]{2,1,0:T(1,128)S(1)}, u32[]{:S(2)}, u32[]{:S(2)}) %all-to-all-start.8) | async-done | bytes 32800 | tf_op jit(solution)/shard_map/all_to_all | solution.py:23
  171.4 1.6 select_add_fusion
  173.0 3.6 %all-to-all-start.9 = ((bf16[8,2,32,1536]{3,2,1,0:T(8,128)(2,1)}), bf16[8,2,32,1536]{3,2,1,0:T(8,128)(2,1)S(1)}, u32[]{:S(2)}, u32[]{:S(2)}) async-start(bf16[8,2,32,1536]{3,2,1,0:T(8,128)(2,1)} %select_add_fusion), calls=%async_computation.9 | async-start | bytes 3145728 | tf_op jit(solution)/shard_map/all_to_all | solution.py:123
  176.8 21.9 %all-to-all-done.9 = bf16[8,2,32,1536]{3,2,1,0:T(8,128)(2,1)S(1)} async-done(((bf16[8,2,32,1536]{3,2,1,0:T(8,128)(2,1)}), bf16[8,2,32,1536]{3,2,1,0:T(8,128)(2,1)S(1)}, u32[]{:S(2)}, u32[]{:S(2)}) %all-to-all-start.9) | async-done | bytes 1572896 | tf_op jit(solution)/shard_map/all_to_all | solution.py:123
  198.7 0.2 convert_reduce_fusion
  198.9 1.8 collective-permute-start.14
  200.8 1.0 collective-permute-done.14
  201.8 0.8 bitcast_divide_fusion
  (101 shorter events, 2.4 us)
Async XLA Ops:
  0.0 16.1 %copy-start.4 = (s32[1,2]{1,0:T(1,128)S(1)}, s32[1,2]{1,0:T(1,128)}, u32[]{:S(2)}) copy-start(s32[1,2]{1,0:T(1,128)} %param.7) | copy-start | bytes 28
  0.0 18.0 %copy-start.8 = (s32[1,2]{1,0:T(1,128)S(1)}, s32[1,2]{1,0:T(1,128)}, u32[]{:S(2)}) copy-start(s32[1,2]{1,0:T(1,128)} %param.8) | copy-start | bytes 28
  0.0 18.6 %copy-start.3 = (s32[16384]{0:T(1024)S(1)}, s32[16384]{0:T(1024)}, u32[]{:S(2)}) copy-start(s32[16384]{0:T(1024)} %param.9) | copy-start | bytes 196612
  0.0 16.1 %collective-permute-start = (bf16[128,1536]{1,0:T(8,128)(2,1)}, bf16[128,1536]{1,0:T(8,128)(2,1)}, u32[]{:S(2)}, u32[]{:S(2)}) collective-permute-start(bf16[128,1536]{1,0:T(8,128)(2,1)} %param.5), channel_id=1, source_target_pairs={{0,1},{1,2},{2,3},{3,4},{4,5},{5,6},{6,7},{7,0},{8,9},{9,10},{10,1... | collective-permute-start | bytes 1179656 | tf_op jit(solution)/shard_map/ppermute | solution.py:37
  2.6 19.0 %collective-permute-start.5 = (bf16[128,1536]{1,0:T(8,128)(2,1)}, bf16[128,1536]{1,0:T(8,128)(2,1)}, u32[]{:S(2)}, u32[]{:S(2)}) collective-permute-start(bf16[128,1536]{1,0:T(8,128)(2,1)} %param.5), channel_id=1, source_target_pairs={{0,7},{1,0},{2,1},{3,2},{4,3},{5,4},{6,5},{7,6},{8,15},{9,8},{10,9... | collective-permute-start | bytes 1179656 | tf_op jit(solution)/shard_map/ppermute | solution.py:38
  8.8 12.7 %copy-start.2 = (bf16[128,1536]{1,0:T(8,128)(2,1)S(1)}, bf16[128,1536]{1,0:T(8,128)(2,1)}, u32[]{:S(2)}) copy-start(bf16[128,1536]{1,0:T(8,128)(2,1)} %param.5) | copy-start | bytes 1179652
  8.8 37.0 %all-to-all-start = ((bf16[8,64,1536]{2,1,0:T(8,128)(2,1)}), bf16[8,64,1536]{2,1,0:T(8,128)(2,1)}, u32[]{:S(2)}, u32[]{:S(2)}) async-start(bf16[8,64,1536]{2,1,0:T(8,128)(2,1)} %broadcast_in_dim.163), calls=%async_computation | async-start | bytes 3145728 | tf_op jit(solution)/shard_map/all_to_all | solution.py:36
  16.6 9.7 %collective-permute-start.2 = (s32[2]{0:T(128)S(1)}, s32[2]{0:T(128)S(1)}, u32[]{:S(2)}, u32[]{:S(2)}) collective-permute-start(s32[2]{0:T(128)S(1)} %bitcast.145), channel_id=1, source_target_pairs={{0,16},{16,0},{1,17},{17,1},{2,18},{18,2},{3,19},{19,3},{4,20},{20... | collective-permute-start | bytes 32 | tf_op jit(solution)/shard_map/ppermute | solution.py:42
  20.7 5.8 %copy-start.7 = (s32[8]{0:T(128)S(1)}, s32[8]{0:T(128)}, u32[]{:S(2)}) copy-start(s32[8]{0:T(128)} %iota_multiply_fusion) | copy-start | bytes 100
  21.2 12.2 %collective-permute-start.1 = (bf16[128,1536]{1,0:T(8,128)(2,1)}, bf16[128,1536]{1,0:T(8,128)(2,1)S(1)}, u32[]{:S(2)}, u32[]{:S(2)}) collective-permute-start(bf16[128,1536]{1,0:T(8,128)(2,1)} %collective-permute-done), channel_id=1, source_target_pairs={{0,1},{1,2},{2,3},{3,4},{4,5},{5,6},{6,7},{7,0},{8,9},{9,10},{10,1... | collective-permute-start | bytes 1179656 | tf_op jit(solution)/shard_map/ppermute | solution.py:48
  21.6 11.9 %collective-permute-start.6 = (bf16[128,1536]{1,0:T(8,128)(2,1)}, bf16[128,1536]{1,0:T(8,128)(2,1)S(1)}, u32[]{:S(2)}, u32[]{:S(2)}) collective-permute-start(bf16[128,1536]{1,0:T(8,128)(2,1)} %collective-permute-done.5), channel_id=1, source_target_pairs={{0,7},{1,0},{2,1},{3,2},{4,3},{5,4},{6,5},{7,6},{8,15},{9,8},{10,9... | collective-permute-start | bytes 1179656 | tf_op jit(solution)/shard_map/ppermute | solution.py:49
  33.5 11.3 %collective-permute-start.7 = (bf16[128,1536]{1,0:T(8,128)(2,1)S(1)}, bf16[128,1536]{1,0:T(8,128)(2,1)}, u32[]{:S(2)}, u32[]{:S(2)}) collective-permute-start(bf16[128,1536]{1,0:T(8,128)(2,1)S(1)} %collective-permute-done.1), channel_id=1, source_target_pairs={{0,1},{1,2},{2,3},{3,4},{4,5},{5,6},{6,7},{7,0},{8,9},{9,10},{10,1... | collective-permute-start | bytes 1179656 | tf_op jit(solution)/shard_map/ppermute | solution.py:52
  33.5 16.6 %collective-permute-start.8 = (bf16[128,1536]{1,0:T(8,128)(2,1)S(1)}, bf16[128,1536]{1,0:T(8,128)(2,1)}, u32[]{:S(2)}, u32[]{:S(2)}) collective-permute-start(bf16[128,1536]{1,0:T(8,128)(2,1)S(1)} %collective-permute-done.6), channel_id=1, source_target_pairs={{0,7},{1,0},{2,1},{3,2},{4,3},{5,4},{6,5},{7,6},{8,15},{9,8},{10,9... | collective-permute-start | bytes 1179656 | tf_op jit(solution)/shard_map/ppermute | solution.py:53
  44.7 10.6 %collective-permute-start.9 = (bf16[128,1536]{1,0:T(8,128)(2,1)}, bf16[128,1536]{1,0:T(8,128)(2,1)}, u32[]{:S(2)}, u32[]{:S(2)}) collective-permute-start(bf16[128,1536]{1,0:T(8,128)(2,1)} %collective-permute-done.7), channel_id=1, source_target_pairs={{0,1},{1,2},{2,3},{3,4},{4,5},{5,6},{6,7},{7,0},{8,9},{9,10},{10,1... | collective-permute-start | bytes 1179656 | tf_op jit(solution)/shard_map/ppermute | solution.py:62
  48.5 4.6 %collective-permute-start.3 = (bf16[2,64,1536]{2,1,0:T(8,128)(2,1)}, bf16[2,64,1536]{2,1,0:T(8,128)(2,1)}, u32[]{:S(2)}, u32[]{:S(2)}) collective-permute-start(bf16[2,64,1536]{2,1,0:T(8,128)(2,1)} %gather_fusion.1), channel_id=1, source_target_pairs={{0,16},{16,0},{1,17},{17,1},{2,18},{18,2},{3,19},{19,3},{4,20},{20... | collective-permute-start | bytes 1179656 | tf_op jit(solution)/shard_map/ppermute | solution.py:58
  51.2 14.1 %copy-start.9 = (f32[256]{0:T(256)S(1)}, f32[256]{0:T(256)}, u32[]{:S(2)}) copy-start(f32[256]{0:T(256)} %broadcast_bitcast_fusion) | copy-start | bytes 3076
  54.3 10.8 %collective-permute-start.4 = (bf16[2,64,1536]{2,1,0:T(8,128)(2,1)S(1)}, bf16[2,64,1536]{2,1,0:T(8,128)(2,1)S(1)}, u32[]{:S(2)}, u32[]{:S(2)}) collective-permute-start(bf16[2,64,1536]{2,1,0:T(8,128)(2,1)S(1)} %broadcast_select_fusion), channel_id=1, source_target_pairs={{0,8},{8,0},{1,9},{9,1},{2,10},{10,2},{3,11},{11,3},{4,12},{12,4},... | collective-permute-start | bytes 1179656 | tf_op jit(solution)/shard_map/ppermute | solution.py:61
  56.3 8.9 %copy-start = (bf16[8,128,1536]{2,1,0:T(8,128)(2,1)}, bf16[8,128,1536]{2,1,0:T(8,128)(2,1)S(1)}, u32[]{:S(2)}) copy-start(bf16[8,128,1536]{2,1,0:T(8,128)(2,1)S(1)} %bitcast_dynamic-update-slice_fusion) | copy-start | bytes 9437188
  65.3 16.0 %copy-start.6 = (f32[128]{0:T(128)S(1)}, f32[128]{0:T(128)}, u32[]{:S(2)}) copy-start(f32[128]{0:T(128)} %pad.4) | copy-start | bytes 1540
  65.3 32.5 %copy-start.5 = (s32[1,2]{1,0:T(1,128)S(1)}, s32[1,2]{1,0:T(1,128)}, u32[]{:S(2)}) copy-start(s32[1,2]{1,0:T(1,128)} %param.7) | copy-start | bytes 28
  142.3 10.1 %all-to-all-start.7 = ((f32[8,1,1024]{2,1,0:T(1,128)}), f32[8,1,1024]{2,1,0:T(1,128)S(1)}, u32[]{:S(2)}, u32[]{:S(2)}) async-start(f32[8,1,1024]{2,1,0:T(1,128)} %broadcast_in_dim.182), calls=%async_computation.7 | async-start | bytes 65536 | tf_op jit(solution)/shard_map/all_to_all | solution.py:23
  152.8 3.1 %copy-start.1 = (bf16[8,128,1536]{2,1,0:T(8,128)(2,1)S(1)}, bf16[8,128,1536]{2,1,0:T(8,128)(2,1)}, u32[]{:S(2)}) copy-start(bf16[8,128,1536]{2,1,0:T(8,128)(2,1)} %copy-done) | copy-start | bytes 9437188
  155.5 8.8 %collective-permute-start.12 = (bf16[64,1536]{1,0:T(8,128)(2,1)S(1)}, bf16[64,1536]{1,0:T(8,128)(2,1)S(1)}, u32[]{:S(2)}, u32[]{:S(2)}) collective-permute-start(bf16[64,1536]{1,0:T(8,128)(2,1)S(1)} %fusion.5), channel_id=1, source_target_pairs={{0,8},{8,0},{1,9},{9,1},{2,10},{10,2},{3,11},{11,3},{4,12},{12,4},... | collective-permute-start | bytes 589832 | tf_op jit(solution)/shard_map/ppermute | solution.py:110
  156.6 8.6 %collective-permute-start.10 = (bf16[64,1536]{1,0:T(8,128)(2,1)S(1)}, bf16[64,1536]{1,0:T(8,128)(2,1)S(1)}, u32[]{:S(2)}, u32[]{:S(2)}) collective-permute-start(bf16[64,1536]{1,0:T(8,128)(2,1)S(1)} %fusion.4), channel_id=1, source_target_pairs={{0,8},{8,0},{1,9},{9,1},{2,10},{10,2},{3,11},{11,3},{4,12},{12,4},... | collective-permute-start | bytes 589832 | tf_op jit(solution)/shard_map/ppermute | solution.py:110
  158.4 13.0 %all-to-all-start.8 = ((f32[32,1,256]{2,1,0:T(1,128)}), f32[32,1,256]{2,1,0:T(1,128)S(1)}, u32[]{:S(2)}, u32[]{:S(2)}) async-start(f32[32,1,256]{2,1,0:T(1,128)} %broadcast_in_dim.183), calls=%async_computation.8 | async-start | bytes 65536 | tf_op jit(solution)/shard_map/all_to_all | solution.py:23
  164.4 7.0 %collective-permute-start.13 = (bf16[32,1536]{1,0:T(8,128)(2,1)S(1)}, bf16[32,1536]{1,0:T(8,128)(2,1)S(1)}, u32[]{:S(2)}, u32[]{:S(2)}) collective-permute-start(bf16[32,1536]{1,0:T(8,128)(2,1)S(1)} %get-tuple-element.51), channel_id=1, source_target_pairs={{0,16},{16,0},{1,17},{17,1},{2,18},{18,2},{3,19},{19,3},{4,20},{20... | collective-permute-start | bytes 294920 | tf_op jit(solution)/shard_map/ppermute | solution.py:114
  165.2 6.2 %collective-permute-start.11 = (bf16[32,1536]{1,0:T(8,128)(2,1)S(1)}, bf16[32,1536]{1,0:T(8,128)(2,1)S(1)}, u32[]{:S(2)}, u32[]{:S(2)}) collective-permute-start(bf16[32,1536]{1,0:T(8,128)(2,1)S(1)} %get-tuple-element.53), channel_id=1, source_target_pairs={{0,16},{16,0},{1,17},{17,1},{2,18},{18,2},{3,19},{19,3},{4,20},{20... | collective-permute-start | bytes 294920 | tf_op jit(solution)/shard_map/ppermute | solution.py:114
  173.0 25.7 %all-to-all-start.9 = ((bf16[8,2,32,1536]{3,2,1,0:T(8,128)(2,1)}), bf16[8,2,32,1536]{3,2,1,0:T(8,128)(2,1)S(1)}, u32[]{:S(2)}, u32[]{:S(2)}) async-start(bf16[8,2,32,1536]{3,2,1,0:T(8,128)(2,1)} %select_add_fusion), calls=%async_computation.9 | async-start | bytes 3145728 | tf_op jit(solution)/shard_map/all_to_all | solution.py:123
  198.9 2.8 %collective-permute-start.14 = (f32[32,1536]{1,0:T(8,128)S(1)}, f32[32,1536]{1,0:T(8,128)S(1)}, u32[]{:S(2)}, u32[]{:S(2)}) collective-permute-start(f32[32,1536]{1,0:T(8,128)S(1)} %dynamic-slice_bitcast_fusion), channel_id=1, source_target_pairs={{0,16},{16,0},{1,17},{17,1},{2,18},{18,2},{3,19},{19,3},{4,20},{20... | collective-permute-start | bytes 589832 | tf_op jit(solution)/shard_map/ppermute | solution.py:127

commit v3 on v2

v3 whole, which is shorter than its diff:
```python
import jax
import jax.numpy as jnp
import numpy as np
from jax import lax
from jax.sharding import Mesh, PartitionSpec as P

ITERS = 4
SCALE = 3.0
NY, NXH, NC, NXL, NZ = 4, 2, 2, 2, 8
NB = NY * NXH * NC
PLANE = ("y", "xh", "c", "xl")
SWAP = [(0, 1), (1, 0)]
UP = [(i, (i + 1) % NZ) for i in range(NZ)]
DOWN = [(i, (i - 1) % NZ) for i in range(NZ)]
after = lax.optimization_barrier


def ordered(first, mine, other):
    is0 = first == 0
    return jnp.stack([jnp.where(is0, mine, other), jnp.where(is0, other, mine)])


def exchange(row, axes, n):
    return lax.all_to_all(jnp.broadcast_to(row[None], (n,) + row.shape), axes, 0, 0)


def shards(points, centroids, pair_blocks, pair_valid, sizes):
    rows, width = points.shape
    c = lax.axis_index("c")
    xl = lax.axis_index("xl")
    z = lax.axis_index("z")
    def put(buf, part, at):
        return lax.dynamic_update_slice(buf, part[None], (at % NZ, 0, 0))

    spread_cents = jnp.broadcast_to(centroids[None], (NY * NXH,) + centroids.shape)
    allc = lax.all_to_all(spread_cents, ("y", "xh"), 0, 0)
    up1 = lax.ppermute(points, "z", UP)
    down1 = lax.ppermute(points, "z", DOWN)
    pair_blocks, points, _ = after((pair_blocks, points, up1))
    slots = pair_blocks[0]
    slots_other = lax.ppermute(slots, "c", SWAP)
    up2 = lax.ppermute(up1, "z", UP)
    down2 = lax.ppermute(down1, "z", DOWN)
    pts = put(jnp.zeros((NZ, rows, width), points.dtype), points, z)
    pts = put(put(pts, up1, z - 1 + NZ), down1, z + 1)
    up3 = lax.ppermute(up2, "z", UP)
    down3 = lax.ppermute(down2, "z", DOWN)
    pts = put(put(pts, up2, z - 2 + NZ), down2, z + 2)

    allc, _ = after((allc, up2))
    sel_give = allc.at[slots_other // NC].get(mode="promise_in_bounds")
    sel_got = lax.ppermute(sel_give, "c", SWAP)
    sel_mine = allc.at[slots // NC].get(mode="promise_in_bounds")
    kept = jnp.where((slots % NC == c)[:, None, None], sel_mine, sel_got)
    kept_xl = lax.ppermute(kept, "xl", SWAP)
    far, _ = after((up3, kept))
    far = lax.ppermute(far, "z", UP)
    pts = put(put(pts, up3, z - 3 + NZ), down3, z + 3)
    cents = jnp.swapaxes(ordered(xl, kept, kept_xl), 0, 1).reshape(256, width)

    valid = pair_valid[0].astype(jnp.float32)

    def kernel_of(part):
        dots = lax.dot_general(
            cents, part, (((1,), (1,)), ((), ())), preferred_element_type=jnp.float32
        )
        return (jnp.exp(SCALE * dots).reshape(2, 128, -1) * valid[:, None, None]).reshape(256, -1)

    kt = kernel_of(pts.reshape(NZ * rows, width))
    kt = lax.dynamic_update_slice(kt, kernel_of(far), (0, ((z + 4) % NZ) * rows))
    pts = put(pts, far, z + 4).reshape(NZ * rows, width)

    def totals_of(match, got):
        return jnp.sum(match[..., None] * got[:, :256].reshape(1, -1, 2, 128), axis=(1, 2))

    rowpart = jnp.sum(kt, axis=0)
    rowpart, sizes, slots, slots_other = after((rowpart, sizes, slots, slots_other))
    got = exchange(rowpart, "z", NZ)
    ids = jnp.pad(slots.astype(jnp.float32), (0, 126))
    per_row = NB * 8
    pick = (8 * slots[:, None] + 4 * jnp.arange(2, dtype=jnp.int32)[None, :] + z // 2).reshape(4)
    own = sizes.reshape(per_row, 128).at[pick].get(mode="promise_in_bounds")
    own = lax.dynamic_slice(own, (0, (z % 2) * 64), (4, 64)).reshape(2, 128)
    factor = jnp.float32(rows * 256) / jnp.sum(sizes.astype(jnp.float32))
    target_pair = own.astype(jnp.float32) * factor
    grid = lax.broadcasted_iota(jnp.int32, (4, NY * NXH, NC), 1) * NC + lax.broadcasted_iota(
        jnp.int32, (4, NY * NXH, NC), 2
    )
    hits = jnp.concatenate([slots, slots_other])[:, None, None] == grid
    hits = [hits[i] for i in range(4)]
    got, ids, target_pair, hits, slots, pts = after((got, ids, target_pair, hits, slots, pts))

    for step in range(ITERS):
        if step > 0:
            got = exchange(jnp.sum(kt * scale_v[:, None], axis=0), "z", NZ)
        scale_u = 1.0 / jnp.sum(got, axis=0)
        if step < ITERS - 1:
            colpart = jnp.sum(kt * scale_u[None, :], axis=1)
            if step == 0:
                got = exchange(jnp.concatenate([colpart, ids]), PLANE, NB * NXL)
                got_ids = got[:, 256:258].astype(jnp.int32)
                match = (got_ids[None] == slots[:, None, None]).astype(jnp.float32)
                got, match = after((got, match))
            else:
                got = exchange(colpart, PLANE, NB * NXL)
            scale_v = (target_pair / totals_of(match, got)).reshape(256)
    weights = (scale_u[None, :] * kt * scale_v[:, None]).astype(jnp.bfloat16)

    def halved(part, at, axis_name):
        mine = lax.dynamic_index_in_dim(part, at, 0, keepdims=False)
        give = lax.dynamic_index_in_dim(part, 1 - at, 0, keepdims=False)
        return mine, lax.ppermute(give, axis_name, SWAP)

    ones = jnp.ones((NZ * rows, 128), jnp.bfloat16)
    tots = lax.dot_general(weights, ones, (((1,), (0,)), ((), ())), preferred_element_type=jnp.float32)
    tots = tots.reshape(2, 2, 64, 128)
    tots = jnp.swapaxes(tots, 0, 1)
    t_mine, t_got = halved(tots, xl, "xl")
    tots = jnp.swapaxes((t_mine + t_got).reshape(2, 2, 32, 128), 0, 1)
    tots = halved(tots, c, "c")

    def in_thirds(value, first):
        at = np.eye(128, dtype=np.float32)[first : first + 3]
        high = lax.reduce_precision(value, 8, 7)
        rest = value - high
        middle = lax.reduce_precision(rest, 8, 7)
        low = rest - middle
        return (high * at[:1] + middle * at[1:2] + low * at[2:]).astype(jnp.bfloat16)

    parts = []
    for k in (0, 1):
        sums = lax.dot_general(
            weights[128 * k : 128 * (k + 1)], pts, (((1,), (0,)), ((), ())), preferred_element_type=jnp.float32
        ).reshape(2, 64, width)
        mine = lax.dynamic_index_in_dim(sums, xl, 0, keepdims=False)
        give = lax.dynamic_index_in_dim(sums, 1 - xl, 0, keepdims=False).astype(jnp.bfloat16)
        got = lax.ppermute(give, "xl", SWAP)
        sums = (mine + got.astype(jnp.float32)).astype(jnp.bfloat16).reshape(2, 32, width)
        pair = halved(sums, c, "c")
        parts.append([jnp.concatenate([pair[i], in_thirds(tots[i][k], 4 * i)], axis=1) for i in (0, 1)])
    zero = jnp.zeros((), jnp.bfloat16)

    def placed(first, second, a, b):
        return jnp.where(first[:, :, None, None], a, jnp.where(second[:, :, None, None], b, zero))

    spread = placed(hits[0], hits[1], parts[0][0], parts[1][0]) + placed(hits[2], hits[3], parts[0][1], parts[1][1])
    landed = lax.all_to_all(spread, ("y", "xh"), 0, 0)
    owned = jnp.sum(landed.astype(jnp.float32), axis=0)
    owned = owned[:, :, :width] / jnp.sum(owned[:, :, width:], axis=2, keepdims=True)
    o_mine, o_got = halved(owned, c, "c")
    return ordered(c, o_mine, o_got).reshape(64, width)


def solution(mesh):
    fine = Mesh(mesh.devices.reshape(NY, NXH, NC, NXL, NZ), ("y", "xh", "c", "xl", "z"))
    rows = P(("y", "xh", "c", "xl", "z"), None)
    pair = P(("y", "xh", "c"), None)
    return jax.shard_map(
        shards, mesh=fine, in_specs=(rows, rows, pair, pair, P()), out_specs=rows, check_vma=False
    )
```

time: 204 us -> 195 us (0.956)
  waiting for transfers between devices: 57.7 us -> 31 us
  blocking collectives: 71.5 us -> 87.2 us
  starting transfers between devices: 41.6 us -> 44.1 us
    all_to_all x0 -> x1, blocking collectives: none -> 26.6 us  [shards(): landed = lax.all_to_all(spread, ('y', 'xh'), 0, 0)]
    all_to_all x1 -> x0, waiting for transfers between devices: 21.9 us -> none  [shards(): landed = lax.all_to_all(spread, ('y', 'xh'), 0, 0)]
    all_to_all x6 -> x5, blocking collectives: 71.5 us -> 60.7 us  [exchange(): lax.all_to_all(jnp.broadcast_to(row[None], (n,) + row.shape), axes, 0, 0)]
    ppermute x1, waiting for transfers between devices: 8.43 us -> 0.01 us  [shards(): up3 = lax.ppermute(up2, 'z', UP)]
    ppermute x4 -> x6, starting transfers between devices: 4.52 us -> 11.4 us  [the longest x5 11.3 us: halved(): return (mine, lax.ppermute(give, axis_name, SWAP))]
    all_to_all x1 -> x0, starting transfers between devices: 3.58 us -> none  [shards(): landed = lax.all_to_all(spread, ('y', 'xh'), 0, 0)]
    ppermute x4 -> x6, waiting for transfers between devices: 1.14 us -> 3.87 us  [the longest x5 3.87 us: halved(): return (mine, lax.ppermute(give, axis_name, SWAP))]
    all_to_all x1, waiting for transfers between devices: 0.01 us -> 2.06 us  [shards(): allc = lax.all_to_all(spread_cents, ('y', 'xh'), 0, 0)]
  transfers between devices with their start and end apart: 19 -> 20, of which waited for: 8 -> 9; matrix products, arithmetic and copies ran while one was open for 10% -> 11% of each run, Pallas kernels for 0% -> 0%
where the time goes in v3:
time: 195 us; the launch traced here: 194 us
  blocking collectives  87.2 us (45%)
  starting transfers between devices  44.1 us (23%)
  waiting for transfers between devices  31 us (16%)
  local copies, waits for them, and re-layouts  17.2 us (9%)
  other arithmetic  6.91 us (4%)
  matrix products  6.79 us (3%)
    all_to_all x5, blocking collectives, exchange(): lax.all_to_all(jnp.broadcast_to(row[None], (n,) + row.shape), axes, 0, 0)  60.7 us
    all_to_all x1, blocking collectives, shards(): landed = lax.all_to_all(spread, ('y', 'xh'), 0, 0)  26.6 us
    ppermute x5, starting transfers between devices, halved(): return (mine, lax.ppermute(give, axis_name, SWAP))  11.3 us
    all_to_all x2, waiting for transfers between devices, exchange(): lax.all_to_all(jnp.broadcast_to(row[None], (n,) + row.shape), axes, 0, 0)  10.1 us
    all_to_all x2, starting transfers between devices, exchange(): lax.all_to_all(jnp.broadcast_to(row[None], (n,) + row.shape), axes, 0, 0)  8.26 us
    ppermute x1, waiting for transfers between devices, shards(): kept_xl = lax.ppermute(kept, 'xl', SWAP)  7.93 us
    ppermute x1, waiting for transfers between devices, shards(): up2 = lax.ppermute(up1, 'z', UP)  7.05 us
    dynamic_update_slice x8, local copies, waits for them, and re-layouts, put(): return lax.dynamic_update_slice(buf, part[None], (at % NZ, 0, 0))  6.95 us
  transfers between devices with their start and end apart: 20, of which 9 were waited for; matrix products, arithmetic and copies ran while one was open for 11% of the time, Pallas kernels for 0%

profile of v3, /device:TPU:1, one launch (start us, length us, event | category | flops | bytes accessed | tf_op | source)
XLA Modules:
  0.0 194.5 jit_solution(12775140151864493429)
XLA Ops:
  0.0 2.5 %collective-permute-start = (bf16[128,1536]{1,0:T(8,128)(2,1)}, bf16[128,1536]{1,0:T(8,128)(2,1)}, u32[]{:S(2)}, u32[]{:S(2)}) collective-permute-start(bf16[128,1536]{1,0:T(8,128)(2,1)} %param.17), channel_id=1, source_target_pairs={{0,1},{1,2},{2,3},{3,4},{4,5},{5,6},{6,7},{7,0},{8,9},{9,10},{10,1... | collective-permute-start | bytes 1179656 | tf_op jit(solution)/shard_map/ppermute | solution.py:37
  2.5 4.0 %collective-permute-start.5 = (bf16[128,1536]{1,0:T(8,128)(2,1)}, bf16[128,1536]{1,0:T(8,128)(2,1)}, u32[]{:S(2)}, u32[]{:S(2)}) collective-permute-start(bf16[128,1536]{1,0:T(8,128)(2,1)} %param.17), channel_id=1, source_target_pairs={{0,7},{1,0},{2,1},{3,2},{4,3},{5,4},{6,5},{7,6},{8,15},{9,8},{10,9... | collective-permute-start | bytes 1179656 | tf_op jit(solution)/shard_map/ppermute | solution.py:38
  6.5 2.2 %broadcast_in_dim.157 = bf16[8,64,1536]{2,1,0:T(8,128)(2,1)} broadcast(bf16[64,1536]{1,0:T(8,128)(2,1)} %param.18), dimensions={1,2} | broadcast | bytes 1769472 | tf_op jit(solution)/shard_map/broadcast_in_dim | solution.py:35
  8.7 6.8 %all-to-all-start = ((bf16[8,64,1536]{2,1,0:T(8,128)(2,1)}), bf16[8,64,1536]{2,1,0:T(8,128)(2,1)}, u32[]{:S(2)}, u32[]{:S(2)}) async-start(bf16[8,64,1536]{2,1,0:T(8,128)(2,1)} %broadcast_in_dim.157), calls=%async_computation | async-start | bytes 3145728 | tf_op jit(solution)/shard_map/all_to_all | solution.py:36
  15.5 0.6 iota_multiply_fusion.1
  16.1 0.5 iota_multiply_fusion
  16.6 1.3 collective-permute-start.2
  18.1 0.3 broadcast_in_dim.159
  18.4 2.7 %collective-permute-start.6 = (bf16[128,1536]{1,0:T(8,128)(2,1)}, bf16[128,1536]{1,0:T(8,128)(2,1)}, u32[]{:S(2)}, u32[]{:S(2)}) collective-permute-start(bf16[128,1536]{1,0:T(8,128)(2,1)} %collective-permute-done.5), channel_id=1, source_target_pairs={{0,7},{1,0},{2,1},{3,2},{4,3},{5,4},{6,5},{7,6},{8,15},{9,8},{10,9... | collective-permute-start | bytes 1179656 | tf_op jit(solution)/shard_map/ppermute | solution.py:43
  21.1 1.0 bitcast_dynamic-update-slice_fusion.6
  22.2 1.0 bitcast_dynamic-update-slice_fusion.5
  23.3 7.0 %collective-permute-done.1 = bf16[128,1536]{1,0:T(8,128)(2,1)} collective-permute-done((bf16[128,1536]{1,0:T(8,128)(2,1)}, bf16[128,1536]{1,0:T(8,128)(2,1)}, u32[]{:S(2)}, u32[]{:S(2)}) %collective-permute-start.1) | collective-permute-done | bytes 393248 | tf_op jit(solution)/shard_map/ppermute | solution.py:42
  30.3 2.8 %collective-permute-start.8 = (bf16[128,1536]{1,0:T(8,128)(2,1)}, bf16[128,1536]{1,0:T(8,128)(2,1)}, u32[]{:S(2)}, u32[]{:S(2)}) collective-permute-start(bf16[128,1536]{1,0:T(8,128)(2,1)} %collective-permute-done.6), channel_id=1, source_target_pairs={{0,7},{1,0},{2,1},{3,2},{4,3},{5,4},{6,5},{7,6},{8,15},{9,8},{10,9... | collective-permute-start | bytes 1179656 | tf_op jit(solution)/shard_map/ppermute | solution.py:47
  33.1 1.0 bitcast_dynamic-update-slice_fusion.4
  34.1 1.0 bitcast_dynamic-update-slice_fusion.3
  35.1 2.1 %all-to-all-done = bf16[8,64,1536]{2,1,0:T(8,128)(2,1)} async-done(((bf16[8,64,1536]{2,1,0:T(8,128)(2,1)}), bf16[8,64,1536]{2,1,0:T(8,128)(2,1)}, u32[]{:S(2)}, u32[]{:S(2)}) %all-to-all-start) | async-done | bytes 1572896 | tf_op jit(solution)/shard_map/all_to_all | solution.py:36
  37.2 2.7 %gather_fusion.1 = bf16[2,64,1536]{2,1,0:T(8,128)(2,1)} fusion(bf16[8,64,1536]{2,1,0:T(8,128)(2,1)} %all-to-all-done, s32[1024]{0:T(1024)S(1)} %pad_clamp_fusion.1), kind=kCustom, calls=%fused_computation.1 | custom fusion | bytes 786440 | tf_op jit(solution)/shard_map/gather | solution.py:51
  39.9 2.2 %collective-permute-start.3 = (bf16[2,64,1536]{2,1,0:T(8,128)(2,1)}, bf16[2,64,1536]{2,1,0:T(8,128)(2,1)}, u32[]{:S(2)}, u32[]{:S(2)}) collective-permute-start(bf16[2,64,1536]{2,1,0:T(8,128)(2,1)} %gather_fusion.1), channel_id=1, source_target_pairs={{0,16},{16,0},{1,17},{17,1},{2,18},{18,2},{3,19},{19,3},{4,20},{20... | collective-permute-start | bytes 1179656 | tf_op jit(solution)/shard_map/ppermute | solution.py:52
  42.1 1.0 bitcast_dynamic-update-slice_fusion.2
  43.2 2.0 %gather_fusion = bf16[2,64,1536]{2,1,0:T(8,128)(2,1)S(1)} fusion(bf16[8,64,1536]{2,1,0:T(8,128)(2,1)} %all-to-all-done, s32[1024]{0:T(1024)S(1)} %pad_clamp_fusion.2), kind=kCustom, calls=%fused_computation | custom fusion | bytes 786440 | tf_op jit(solution)/shard_map/gather | solution.py:53
  45.2 1.1 broadcast_select_fusion
  46.3 0.4 collective-permute-start.4
  46.7 1.0 bitcast_dynamic-update-slice_fusion.1
  47.8 7.9 %collective-permute-done.4 = bf16[2,64,1536]{2,1,0:T(8,128)(2,1)S(1)} collective-permute-done((bf16[2,64,1536]{2,1,0:T(8,128)(2,1)S(1)}, bf16[2,64,1536]{2,1,0:T(8,128)(2,1)S(1)}, u32[]{:S(2)}, u32[]{:S(2)}) %collective-permute-start.4) | collective-permute-done | bytes 393248 | tf_op jit(solution)/shard_map/ppermute | solution.py:55
  55.9 2.9 %fusion.1 = f32[256,1024]{1,0:T(8,128)S(1)} fusion(bf16[256,1536]{1,0:T(8,128)(2,1)S(1)} %bitcast.145, bf16[1024,1536]{1,0:T(8,128)(2,1)} %bitcast.141, f32[256]{0:T(256)S(1)} %broadcast_bitcast_fusion), kind=kOutput, calls=%fused_computation.7 | convolution fusion | flops 805830656 | bytes 4981760 | tf_op jit(solution)/shard_map/dot_general | solution.py:64
  58.9 0.4 fusion.4
  59.3 0.6 broadcast_in_dim.167
  60.0 4.9 %all-to-all-start.1 = ((f32[8,1,1024]{2,1,0:T(1,128)}), f32[8,1,1024]{2,1,0:T(1,128)S(1)}, u32[]{:S(2)}, u32[]{:S(2)}) async-start(f32[8,1,1024]{2,1,0:T(1,128)} %broadcast_in_dim.167), calls=%async_computation.1 | async-start | bytes 65536 | tf_op jit(solution)/shard_map/all_to_all | solution.py:24
  65.1 0.7 convert_reduce_fusion.1
  65.9 0.6 gather_fusion.2
  67.2 0.8 bitcast_dynamic-update-slice_fusion
  68.1 3.7 %all-to-all-done.1 = f32[8,1,1024]{2,1,0:T(1,128)S(1)} async-done(((f32[8,1,1024]{2,1,0:T(1,128)}), f32[8,1,1024]{2,1,0:T(1,128)S(1)}, u32[]{:S(2)}, u32[]{:S(2)}) %all-to-all-start.1) | async-done | bytes 32800 | tf_op jit(solution)/shard_map/all_to_all | solution.py:24
  71.8 0.2 multiply_reduce_fusion.5
  72.0 18.2 %all_to_all.58 = f32[32,1,384]{2,1,0:T(1,128)S(1)} all-to-all(f32[32,1,384]{2,1,0:T(1,128)S(1)} %broadcast_in_dim.170), channel_id=1, replica_groups=mesh['y'=4,'xh'=2,'c'=2,'xl'=2,'z'=8] {'y','xh','c','xl'}, dimensions={0} | all-to-all | bytes 98304 | tf_op jit(solution)/shard_map/all_to_all | solution.py:24
  90.6 0.2 multiply_reduce_fusion.4
  90.8 9.2 %all_to_all.59 = f32[8,1,1024]{2,1,0:T(1,128)S(1)} all-to-all(f32[8,1,1024]{2,1,0:T(1,128)S(1)} %broadcast_in_dim.171), channel_id=1, replica_groups=mesh['y'=4,'xh'=2,'c'=2,'xl'=2,'z'=8] {'z'}, dimensions={0} | all-to-all | bytes 65536 | tf_op jit(solution)/shard_map/all_to_all | solution.py:24
  100.1 0.2 multiply_reduce_fusion.3
  100.3 12.0 %all_to_all.60 = f32[32,1,256]{2,1,0:T(1,128)S(1)} all-to-all(f32[32,1,256]{2,1,0:T(1,128)S(1)} %broadcast_in_dim.172), channel_id=1, replica_groups=mesh['y'=4,'xh'=2,'c'=2,'xl'=2,'z'=8] {'y','xh','c','xl'}, dimensions={0} | all-to-all | bytes 65536 | tf_op jit(solution)/shard_map/all_to_all | solution.py:24
  112.4 0.2 multiply_reduce_fusion.2
  112.6 9.3 %all_to_all.61 = f32[8,1,1024]{2,1,0:T(1,128)S(1)} all-to-all(f32[8,1,1024]{2,1,0:T(1,128)S(1)} %broadcast_in_dim.173), channel_id=1, replica_groups=mesh['y'=4,'xh'=2,'c'=2,'xl'=2,'z'=8] {'z'}, dimensions={0} | all-to-all | bytes 65536 | tf_op jit(solution)/shard_map/all_to_all | solution.py:24
  121.9 0.2 multiply_reduce_fusion.1
  122.1 12.0 %all_to_all.62 = f32[32,1,256]{2,1,0:T(1,128)S(1)} all-to-all(f32[32,1,256]{2,1,0:T(1,128)S(1)} %broadcast_in_dim.174), channel_id=1, replica_groups=mesh['y'=4,'xh'=2,'c'=2,'xl'=2,'z'=8] {'y','xh','c','xl'}, dimensions={0} | all-to-all | bytes 65536 | tf_op jit(solution)/shard_map/all_to_all | solution.py:24
  134.1 0.2 multiply_reduce_fusion
  134.3 0.6 broadcast_in_dim.175
  134.9 3.3 %all-to-all-start.7 = ((f32[8,1,1024]{2,1,0:T(1,128)}), f32[8,1,1024]{2,1,0:T(1,128)S(1)}, u32[]{:S(2)}, u32[]{:S(2)}) async-start(f32[8,1,1024]{2,1,0:T(1,128)} %broadcast_in_dim.175), calls=%async_computation.7 | async-start | bytes 65536 | tf_op jit(solution)/shard_map/all_to_all | solution.py:24
  138.7 6.4 %all-to-all-done.7 = f32[8,1,1024]{2,1,0:T(1,128)S(1)} async-done(((f32[8,1,1024]{2,1,0:T(1,128)}), f32[8,1,1024]{2,1,0:T(1,128)S(1)}, u32[]{:S(2)}, u32[]{:S(2)}) %all-to-all-start.7) | async-done | bytes 32800 | tf_op jit(solution)/shard_map/all_to_all | solution.py:24
  145.3 2.6 %fusion.7 = f32[128,1536]{1,0:T(8,128)S(1)} fusion(bf16[1024,1536]{1,0:T(8,128)(2,1)} %bitcast.142, bf16[256,1024]{1,0:T(8,128)(2,1)S(1)} %multiply_convert_fusion), kind=kOutput, calls=%fused_computation.39 | convolution fusion | flops 402653184 | bytes 4194304 | tf_op jit(solution)/shard_map/dot_general | solution.py:132
  148.0 0.6 fusion.9
  148.6 0.3 fusion.15
  148.9 0.4 collective-permute-start.11
  149.3 1.2 collective-permute-start.12
  150.6 0.4 collective-permute-start.10
  151.0 1.1 collective-permute-done.11
  152.1 3.9 %collective-permute-start.14 = (f32[2,32,128]{2,1,0:T(8,128)S(1)}, f32[2,32,128]{2,1,0:T(8,128)S(1)}, u32[]{:S(2)}, u32[]{:S(2)}) collective-permute-start(f32[2,32,128]{2,1,0:T(8,128)S(1)} %get-tuple-element.52), channel_id=1, source_target_pairs={{0,16},{16,0},{1,17},{17,1},{2,18},{18,2},{3,19},{19,3},{4,20},{20... | collective-permute-start | bytes 98312 | tf_op jit(solution)/shard_map/ppermute | solution.py:112
  156.0 0.8 collective-permute-done.14
  157.0 3.0 %collective-permute-start.15 = (bf16[32,1536]{1,0:T(8,128)(2,1)S(1)}, bf16[32,1536]{1,0:T(8,128)(2,1)S(1)}, u32[]{:S(2)}, u32[]{:S(2)}) collective-permute-start(bf16[32,1536]{1,0:T(8,128)(2,1)S(1)} %get-tuple-element.50), channel_id=1, source_target_pairs={{0,16},{16,0},{1,17},{17,1},{2,18},{18,2},{3,19},{19,3},{4,20},{20... | collective-permute-start | bytes 294920 | tf_op jit(solution)/shard_map/ppermute | solution.py:112
  160.0 2.0 %collective-permute-start.13 = (bf16[32,1536]{1,0:T(8,128)(2,1)S(1)}, bf16[32,1536]{1,0:T(8,128)(2,1)S(1)}, u32[]{:S(2)}, u32[]{:S(2)}) collective-permute-start(bf16[32,1536]{1,0:T(8,128)(2,1)S(1)} %get-tuple-element.48), channel_id=1, source_target_pairs={{0,16},{16,0},{1,17},{17,1},{2,18},{18,2},{3,19},{19,3},{4,20},{20... | collective-permute-start | bytes 294920 | tf_op jit(solution)/shard_map/ppermute | solution.py:112
  162.1 0.9 collective-permute-done.13
  163.0 0.5 select_add_fusion
  163.6 26.6 %all_to_all.63 = bf16[8,2,32,1664]{3,2,1,0:T(8,128)(2,1)S(1)} all-to-all(bf16[8,2,32,1664]{3,2,1,0:T(8,128)(2,1)S(1)} %select_add_fusion), channel_id=1, replica_groups=mesh['y'=4,'xh'=2,'c'=2,'xl'=2,'z'=8] {'y','xh'}, dimensions={0} | all-to-all | bytes 3407872 | tf_op jit(solution)/shard_map/all_to_all | solution.py:147
  190.1 0.2 convert_reduce_fusion
  190.6 2.0 %collective-permute-start.16 = (f32[32,1536]{1,0:T(8,128)S(1)}, f32[32,1536]{1,0:T(8,128)S(1)}, u32[]{:S(2)}, u32[]{:S(2)}) collective-permute-start(f32[32,1536]{1,0:T(8,128)S(1)} %dynamic-slice_bitcast_fusion), channel_id=1, source_target_pairs={{0,16},{16,0},{1,17},{17,1},{2,18},{18,2},{3,19},{19,3},{4,20},{20... | collective-permute-start | bytes 589832 | tf_op jit(solution)/shard_map/ppermute | solution.py:112
  192.6 1.1 collective-permute-done.16
  193.7 0.8 pad_maximum_fusion.1
  (119 shorter events, 3.1 us)
Async XLA Ops:
  0.0 16.5 %copy-start.13 = (s32[1,2]{1,0:T(1,128)S(1)}, s32[1,2]{1,0:T(1,128)}, u32[]{:S(2)}) copy-start(s32[1,2]{1,0:T(1,128)} %param.20) | copy-start | bytes 28
  0.0 16.6 %copy-start.10 = (s32[1,2]{1,0:T(1,128)S(1)}, s32[1,2]{1,0:T(1,128)}, u32[]{:S(2)}) copy-start(s32[1,2]{1,0:T(1,128)} %param.19) | copy-start | bytes 28
  0.0 16.6 %collective-permute-start = (bf16[128,1536]{1,0:T(8,128)(2,1)}, bf16[128,1536]{1,0:T(8,128)(2,1)}, u32[]{:S(2)}, u32[]{:S(2)}) collective-permute-start(bf16[128,1536]{1,0:T(8,128)(2,1)} %param.17), channel_id=1, source_target_pairs={{0,1},{1,2},{2,3},{3,4},{4,5},{5,6},{6,7},{7,0},{8,9},{9,10},{10,1... | collective-permute-start | bytes 1179656 | tf_op jit(solution)/shard_map/ppermute | solution.py:37
  2.5 15.9 %collective-permute-start.5 = (bf16[128,1536]{1,0:T(8,128)(2,1)}, bf16[128,1536]{1,0:T(8,128)(2,1)}, u32[]{:S(2)}, u32[]{:S(2)}) collective-permute-start(bf16[128,1536]{1,0:T(8,128)(2,1)} %param.17), channel_id=1, source_target_pairs={{0,7},{1,0},{2,1},{3,2},{4,3},{5,4},{6,5},{7,6},{8,15},{9,8},{10,9... | collective-permute-start | bytes 1179656 | tf_op jit(solution)/shard_map/ppermute | solution.py:38
  8.7 9.6 %copy-start.2 = (bf16[128,1536]{1,0:T(8,128)(2,1)S(1)}, bf16[128,1536]{1,0:T(8,128)(2,1)}, u32[]{:S(2)}) copy-start(bf16[128,1536]{1,0:T(8,128)(2,1)} %param.17) | copy-start | bytes 1179652
  8.7 28.5 %all-to-all-start = ((bf16[8,64,1536]{2,1,0:T(8,128)(2,1)}), bf16[8,64,1536]{2,1,0:T(8,128)(2,1)}, u32[]{:S(2)}, u32[]{:S(2)}) async-start(bf16[8,64,1536]{2,1,0:T(8,128)(2,1)} %broadcast_in_dim.157), calls=%async_computation | async-start | bytes 3145728 | tf_op jit(solution)/shard_map/all_to_all | solution.py:36
  16.6 6.6 %collective-permute-start.2 = (s32[2]{0:T(128)S(1)}, s32[2]{0:T(128)S(1)}, u32[]{:S(2)}, u32[]{:S(2)}) collective-permute-start(s32[2]{0:T(128)S(1)} %bitcast.161), channel_id=1, source_target_pairs={{0,16},{16,0},{1,17},{17,1},{2,18},{18,2},{3,19},{19,3},{4,20},{20... | collective-permute-start | bytes 32 | tf_op jit(solution)/shard_map/ppermute | solution.py:41
  18.0 12.3 %collective-permute-start.1 = (bf16[128,1536]{1,0:T(8,128)(2,1)}, bf16[128,1536]{1,0:T(8,128)(2,1)}, u32[]{:S(2)}, u32[]{:S(2)}) collective-permute-start(bf16[128,1536]{1,0:T(8,128)(2,1)} %collective-permute-done), channel_id=1, source_target_pairs={{0,1},{1,2},{2,3},{3,4},{4,5},{5,6},{6,7},{7,0},{8,9},{9,10},{10,1... | collective-permute-start | bytes 1179656 | tf_op jit(solution)/shard_map/ppermute | solution.py:42
  18.4 11.9 %collective-permute-start.6 = (bf16[128,1536]{1,0:T(8,128)(2,1)}, bf16[128,1536]{1,0:T(8,128)(2,1)}, u32[]{:S(2)}, u32[]{:S(2)}) collective-permute-start(bf16[128,1536]{1,0:T(8,128)(2,1)} %collective-permute-done.5), channel_id=1, source_target_pairs={{0,7},{1,0},{2,1},{3,2},{4,3},{5,4},{6,5},{7,6},{8,15},{9,8},{10,9... | collective-permute-start | bytes 1179656 | tf_op jit(solution)/shard_map/ppermute | solution.py:43
  23.2 10.9 %copy-start.14 = (s32[2]{0:T(128)}, s32[2]{0:T(128)S(1)}, u32[]{:S(2)}) copy-start(s32[2]{0:T(128)S(1)} %collective-permute-done.2) | copy-start | bytes 28
  30.3 11.8 %collective-permute-start.7 = (bf16[128,1536]{1,0:T(8,128)(2,1)}, bf16[128,1536]{1,0:T(8,128)(2,1)}, u32[]{:S(2)}, u32[]{:S(2)}) collective-permute-start(bf16[128,1536]{1,0:T(8,128)(2,1)} %collective-permute-done.1), channel_id=1, source_target_pairs={{0,1},{1,2},{2,3},{3,4},{4,5},{5,6},{6,7},{7,0},{8,9},{9,10},{10,1... | collective-permute-start | bytes 1179656 | tf_op jit(solution)/shard_map/ppermute | solution.py:46
  30.3 16.3 %collective-permute-start.8 = (bf16[128,1536]{1,0:T(8,128)(2,1)}, bf16[128,1536]{1,0:T(8,128)(2,1)}, u32[]{:S(2)}, u32[]{:S(2)}) collective-permute-start(bf16[128,1536]{1,0:T(8,128)(2,1)} %collective-permute-done.6), channel_id=1, source_target_pairs={{0,7},{1,0},{2,1},{3,2},{4,3},{5,4},{6,5},{7,6},{8,15},{9,8},{10,9... | collective-permute-start | bytes 1179656 | tf_op jit(solution)/shard_map/ppermute | solution.py:47
  39.9 5.2 %collective-permute-start.3 = (bf16[2,64,1536]{2,1,0:T(8,128)(2,1)}, bf16[2,64,1536]{2,1,0:T(8,128)(2,1)}, u32[]{:S(2)}, u32[]{:S(2)}) collective-permute-start(bf16[2,64,1536]{2,1,0:T(8,128)(2,1)} %gather_fusion.1), channel_id=1, source_target_pairs={{0,16},{16,0},{1,17},{17,1},{2,18},{18,2},{3,19},{19,3},{4,20},{20... | collective-permute-start | bytes 1179656 | tf_op jit(solution)/shard_map/ppermute | solution.py:52
  46.3 9.5 %collective-permute-start.4 = (bf16[2,64,1536]{2,1,0:T(8,128)(2,1)S(1)}, bf16[2,64,1536]{2,1,0:T(8,128)(2,1)S(1)}, u32[]{:S(2)}, u32[]{:S(2)}) collective-permute-start(bf16[2,64,1536]{2,1,0:T(8,128)(2,1)S(1)} %broadcast_select_fusion), channel_id=1, source_target_pairs={{0,8},{8,0},{1,9},{9,1},{2,10},{10,2},{3,11},{11,3},{4,12},{12,4},... | collective-permute-start | bytes 1179656 | tf_op jit(solution)/shard_map/ppermute | solution.py:55
  47.7 8.2 %copy-start = (bf16[8,128,1536]{2,1,0:T(8,128)(2,1)}, bf16[8,128,1536]{2,1,0:T(8,128)(2,1)S(1)}, u32[]{:S(2)}) copy-start(bf16[8,128,1536]{2,1,0:T(8,128)(2,1)S(1)} %bitcast_dynamic-update-slice_fusion.1) | copy-start | bytes 9437188
  47.7 11.2 %collective-permute-start.9 = (bf16[128,1536]{1,0:T(8,128)(2,1)}, bf16[128,1536]{1,0:T(8,128)(2,1)S(1)}, u32[]{:S(2)}, u32[]{:S(2)}) collective-permute-start(bf16[128,1536]{1,0:T(8,128)(2,1)} %collective-permute-done.7), channel_id=1, source_target_pairs={{0,1},{1,2},{2,3},{3,4},{4,5},{5,6},{6,7},{7,0},{8,9},{9,10},{10,1... | collective-permute-start | bytes 1179656 | tf_op jit(solution)/shard_map/ppermute | solution.py:57
  55.9 9.0 %copy-start.11 = (s32[2]{0:T(128)S(1)}, s32[2]{0:T(128)}, u32[]{:S(2)}) copy-start(s32[2]{0:T(128)} %iota_multiply_fusion.1) | copy-start | bytes 28
  55.9 9.2 %copy-start.3 = (s32[16384]{0:T(1024)S(1)}, s32[16384]{0:T(1024)}, u32[]{:S(2)}) copy-start(s32[16384]{0:T(1024)} %param.21) | copy-start | bytes 196612
  55.9 9.9 %copy-start.15 = (s32[2]{0:T(128)S(1)}, s32[2]{0:T(128)}, u32[]{:S(2)}) copy-start(s32[2]{0:T(128)} %copy-done.14) | copy-start | bytes 28
  55.9 9.9 %copy-start.12 = (s32[8]{0:T(128)S(1)}, s32[8]{0:T(128)}, u32[]{:S(2)}) copy-start(s32[8]{0:T(128)} %iota_multiply_fusion) | copy-start | bytes 100
  60.0 11.8 %all-to-all-start.1 = ((f32[8,1,1024]{2,1,0:T(1,128)}), f32[8,1,1024]{2,1,0:T(1,128)S(1)}, u32[]{:S(2)}, u32[]{:S(2)}) async-start(f32[8,1,1024]{2,1,0:T(1,128)} %broadcast_in_dim.167), calls=%async_computation.1 | async-start | bytes 65536 | tf_op jit(solution)/shard_map/all_to_all | solution.py:24
  134.9 10.1 %all-to-all-start.7 = ((f32[8,1,1024]{2,1,0:T(1,128)}), f32[8,1,1024]{2,1,0:T(1,128)S(1)}, u32[]{:S(2)}, u32[]{:S(2)}) async-start(f32[8,1,1024]{2,1,0:T(1,128)} %broadcast_in_dim.175), calls=%async_computation.7 | async-start | bytes 65536 | tf_op jit(solution)/shard_map/all_to_all | solution.py:24
  145.1 2.8 %copy-start.1 = (bf16[8,128,1536]{2,1,0:T(8,128)(2,1)S(1)}, bf16[8,128,1536]{2,1,0:T(8,128)(2,1)}, u32[]{:S(2)}) copy-start(bf16[8,128,1536]{2,1,0:T(8,128)(2,1)} %bitcast_dynamic-update-slice_fusion) | copy-start | bytes 9437188
  147.9 8.0 %copy-start.7 = (f32[128]{0:T(128)S(1)}, f32[128]{0:T(128)}, u32[]{:S(2)}) copy-start(f32[128]{0:T(128)} %constant.209) | copy-start | bytes 1540
  147.9 8.0 %copy-start.8 = (f32[128]{0:T(128)S(1)}, f32[128]{0:T(128)}, u32[]{:S(2)}) copy-start(f32[128]{0:T(128)} %constant.208) | copy-start | bytes 1540
  147.9 8.0 %copy-start.9 = (f32[128]{0:T(128)S(1)}, f32[128]{0:T(128)}, u32[]{:S(2)}) copy-start(f32[128]{0:T(128)} %constant.207) | copy-start | bytes 1540
  147.9 8.9 %copy-start.4 = (f32[128]{0:T(128)S(1)}, f32[128]{0:T(128)}, u32[]{:S(2)}) copy-start(f32[128]{0:T(128)} %constant.212) | copy-start | bytes 1540
  148.0 8.9 %copy-start.5 = (f32[128]{0:T(128)S(1)}, f32[128]{0:T(128)}, u32[]{:S(2)}) copy-start(f32[128]{0:T(128)} %constant.211) | copy-start | bytes 1540
  148.0 8.9 %copy-start.6 = (f32[128]{0:T(128)S(1)}, f32[128]{0:T(128)}, u32[]{:S(2)}) copy-start(f32[128]{0:T(128)} %constant.210) | copy-start | bytes 1540
  148.9 3.2 %collective-permute-start.11 = (f32[2,64,128]{2,1,0:T(8,128)S(1)}, f32[2,64,128]{2,1,0:T(8,128)S(1)}, u32[]{:S(2)}, u32[]{:S(2)}) collective-permute-start(f32[2,64,128]{2,1,0:T(8,128)S(1)} %dynamic-slice_bitcast_fusion.5), channel_id=1, source_target_pairs={{0,8},{8,0},{1,9},{9,1},{2,10},{10,2},{3,11},{11,3},{4,12},{12,4},... | collective-permute-start | bytes 196616 | tf_op jit(solution)/shard_map/ppermute | solution.py:112
  149.3 7.5 %collective-permute-start.12 = (bf16[64,1536]{1,0:T(8,128)(2,1)S(1)}, bf16[64,1536]{1,0:T(8,128)(2,1)S(1)}, u32[]{:S(2)}, u32[]{:S(2)}) collective-permute-start(bf16[64,1536]{1,0:T(8,128)(2,1)S(1)} %fusion.12), channel_id=1, source_target_pairs={{0,8},{8,0},{1,9},{9,1},{2,10},{10,2},{3,11},{11,3},{4,12},{12,4},... | collective-permute-start | bytes 589832 | tf_op jit(solution)/shard_map/ppermute | solution.py:137
  150.6 9.4 %collective-permute-start.10 = (bf16[64,1536]{1,0:T(8,128)(2,1)S(1)}, bf16[64,1536]{1,0:T(8,128)(2,1)S(1)}, u32[]{:S(2)}, u32[]{:S(2)}) collective-permute-start(bf16[64,1536]{1,0:T(8,128)(2,1)S(1)} %fusion.11), channel_id=1, source_target_pairs={{0,8},{8,0},{1,9},{9,1},{2,10},{10,2},{3,11},{11,3},{4,12},{12,4},... | collective-permute-start | bytes 589832 | tf_op jit(solution)/shard_map/ppermute | solution.py:137
  152.1 4.7 %collective-permute-start.14 = (f32[2,32,128]{2,1,0:T(8,128)S(1)}, f32[2,32,128]{2,1,0:T(8,128)S(1)}, u32[]{:S(2)}, u32[]{:S(2)}) collective-permute-start(f32[2,32,128]{2,1,0:T(8,128)S(1)} %get-tuple-element.52), channel_id=1, source_target_pairs={{0,16},{16,0},{1,17},{17,1},{2,18},{18,2},{3,19},{19,3},{4,20},{20... | collective-permute-start | bytes 98312 | tf_op jit(solution)/shard_map/ppermute | solution.py:112
  157.0 5.1 %collective-permute-start.15 = (bf16[32,1536]{1,0:T(8,128)(2,1)S(1)}, bf16[32,1536]{1,0:T(8,128)(2,1)S(1)}, u32[]{:S(2)}, u32[]{:S(2)}) collective-permute-start(bf16[32,1536]{1,0:T(8,128)(2,1)S(1)} %get-tuple-element.50), channel_id=1, source_target_pairs={{0,16},{16,0},{1,17},{17,1},{2,18},{18,2},{3,19},{19,3},{4,20},{20... | collective-permute-start | bytes 294920 | tf_op jit(solution)/shard_map/ppermute | solution.py:112
  160.0 3.0 %collective-permute-start.13 = (bf16[32,1536]{1,0:T(8,128)(2,1)S(1)}, bf16[32,1536]{1,0:T(8,128)(2,1)S(1)}, u32[]{:S(2)}, u32[]{:S(2)}) collective-permute-start(bf16[32,1536]{1,0:T(8,128)(2,1)S(1)} %get-tuple-element.48), channel_id=1, source_target_pairs={{0,16},{16,0},{1,17},{17,1},{2,18},{18,2},{3,19},{19,3},{4,20},{20... | collective-permute-start | bytes 294920 | tf_op jit(solution)/shard_map/ppermute | solution.py:112
  190.6 3.1 %collective-permute-start.16 = (f32[32,1536]{1,0:T(8,128)S(1)}, f32[32,1536]{1,0:T(8,128)S(1)}, u32[]{:S(2)}, u32[]{:S(2)}) collective-permute-start(f32[32,1536]{1,0:T(8,128)S(1)} %dynamic-slice_bitcast_fusion), channel_id=1, source_target_pairs={{0,16},{16,0},{1,17},{17,1},{2,18},{18,2},{3,19},{19,3},{4,20},{20... | collective-permute-start | bytes 589832 | tf_op jit(solution)/shard_map/ppermute | solution.py:112

commit v4 on v3

--- a/solution.py
+++ b/solution.py
@@ -41,7 +41,7 @@
     slots_other = lax.ppermute(slots, "c", SWAP)
     up2 = lax.ppermute(up1, "z", UP)
     down2 = lax.ppermute(down1, "z", DOWN)
-    pts = put(jnp.zeros((NZ, rows, width), points.dtype), points, z)
+    pts = jnp.broadcast_to(points[None], (NZ + 2, rows, width))
     pts = put(put(pts, up1, z - 1 + NZ), down1, z + 1)
     up3 = lax.ppermute(up2, "z", UP)
     down3 = lax.ppermute(down2, "z", DOWN)
@@ -53,8 +53,8 @@
     sel_mine = allc.at[slots // NC].get(mode="promise_in_bounds")
     kept = jnp.where((slots % NC == c)[:, None, None], sel_mine, sel_got)
     kept_xl = lax.ppermute(kept, "xl", SWAP)
-    far, _ = after((up3, kept))
-    far = lax.ppermute(far, "z", UP)
+    up3, down3, _ = after((up3, down3, kept))
+    far = lax.ppermute(up3, "z", UP)
     pts = put(put(pts, up3, z - 3 + NZ), down3, z + 3)
     cents = jnp.swapaxes(ordered(xl, kept, kept_xl), 0, 1).reshape(256, width)
 
@@ -66,9 +66,9 @@
         )
         return (jnp.exp(SCALE * dots).reshape(2, 128, -1) * valid[:, None, None]).reshape(256, -1)
 
-    kt = kernel_of(pts.reshape(NZ * rows, width))
+    kt = kernel_of(pts[:NZ].reshape(NZ * rows, width))
     kt = lax.dynamic_update_slice(kt, kernel_of(far), (0, ((z + 4) % NZ) * rows))
-    pts = put(pts, far, z + 4).reshape(NZ * rows, width)
+    pts = put(pts, far, z + 4)
 
     def totals_of(match, got):
         return jnp.sum(match[..., None] * got[:, :256].reshape(1, -1, 2, 128), axis=(1, 2))
@@ -89,6 +89,7 @@
     hits = jnp.concatenate([slots, slots_other])[:, None, None] == grid
     hits = [hits[i] for i in range(4)]
     got, ids, target_pair, hits, slots, pts = after((got, ids, target_pair, hits, slots, pts))
+    pts = pts[:NZ].reshape(NZ * rows, width)
 
     for step in range(ITERS):
         if step > 0:

time: 195 us -> 185 us (0.949)
  waiting for transfers between devices: 31 us -> 25.2 us
  local copies, waits for them, and re-layouts: 17.2 us -> 21.6 us
  blocking collectives: 87.2 us -> 83 us
  matrix products: 6.79 us -> 2.85 us
    slice x0 -> x3, local copies, waits for them, and re-layouts: none -> 5.9 us  [the longest x1 3.77 us: shards(): pts = pts[:NZ].reshape(NZ * rows, width)]
    all_to_all x2, waiting for transfers between devices: 10.1 us -> 6.24 us  [exchange(): lax.all_to_all(jnp.broadcast_to(row[None], (n,) + row.shape), axes, 0, 0)]
    all_to_all x5, blocking collectives: 60.7 us -> 57 us  [exchange(): lax.all_to_all(jnp.broadcast_to(row[None], (n,) + row.shape), axes, 0, 0)]
    dot_general x2, matrix products: 3.2 us -> 1.16 us  [shards(): lax.dot_general(weights[128 * k:128 * (k + 1)], pts, (((1,), (0,)), ((),...]
    broadcast_in_dim x1, local copies, waits for them, and re-layouts: 0.26 us -> 2.22 us  [shards(): pts = jnp.broadcast_to(points[None], (NZ + 2, rows, width))]
    dynamic_update_slice x8 -> x7, local copies, waits for them, and re-layouts: 6.95 us -> 5.46 us  [put(): return lax.dynamic_update_slice(buf, part[None], (at % NZ, 0, 0))]
  transfers between devices with their start and end apart: 20 -> 20, of which waited for: 9 -> 11; matrix products, arithmetic and copies ran while one was open for 11% -> 13% of each run, Pallas kernels for 0% -> 0%
where the time goes in v4:
time: 185 us
  blocking collectives  83 us (45%)
  starting transfers between devices  43.9 us (24%)
  waiting for transfers between devices  25.2 us (14%)
  local copies, waits for them, and re-layouts  21.6 us (12%)
  other arithmetic  6.89 us (4%)
  matrix products  2.85 us (2%)
    all_to_all x5, blocking collectives, exchange(): lax.all_to_all(jnp.broadcast_to(row[None], (n,) + row.shape), axes, 0, 0)  57 us
    all_to_all x1, blocking collectives, shards(): landed = lax.all_to_all(spread, ('y', 'xh'), 0, 0)  26 us
    ppermute x5, starting transfers between devices, halved(): return (mine, lax.ppermute(give, axis_name, SWAP))  11.1 us
    all_to_all x2, starting transfers between devices, exchange(): lax.all_to_all(jnp.broadcast_to(row[None], (n,) + row.shape), axes, 0, 0)  8.54 us
    all_to_all x1, starting transfers between devices, shards(): allc = lax.all_to_all(spread_cents, ('y', 'xh'), 0, 0)  6.65 us
    ppermute x1, waiting for transfers between devices, shards(): kept_xl = lax.ppermute(kept, 'xl', SWAP)  6.3 us
    all_to_all x2, waiting for transfers between devices, exchange(): lax.all_to_all(jnp.broadcast_to(row[None], (n,) + row.shape), axes, 0, 0)  6.24 us
    dynamic_update_slice x7, local copies, waits for them, and re-layouts, put(): return lax.dynamic_update_slice(buf, part[None], (at % NZ, 0, 0))  5.46 us
  transfers between devices with their start and end apart: 20, of which 11 were waited for; matrix products, arithmetic and copies ran while one was open for 13% of the time, Pallas kernels for 0%

profile of v4, /device:TPU:1, one launch (start us, length us, event | category | flops | bytes accessed | tf_op | source)
XLA Modules:
  0.0 184.7 jit_solution(13083606407009795734)
XLA Ops:
  0.0 2.5 %collective-permute-start = (bf16[128,1536]{1,0:T(8,128)(2,1)}, bf16[128,1536]{1,0:T(8,128)(2,1)S(1)}, u32[]{:S(2)}, u32[]{:S(2)}) collective-permute-start(bf16[128,1536]{1,0:T(8,128)(2,1)} %param.17), channel_id=1, source_target_pairs={{0,1},{1,2},{2,3},{3,4},{4,5},{5,6},{6,7},{7,0},{8,9},{9,10},{10,1... | collective-permute-start | bytes 1179656 | tf_op jit(solution)/shard_map/ppermute | solution.py:37
  2.6 4.0 %collective-permute-start.5 = (bf16[128,1536]{1,0:T(8,128)(2,1)}, bf16[128,1536]{1,0:T(8,128)(2,1)S(1)}, u32[]{:S(2)}, u32[]{:S(2)}) collective-permute-start(bf16[128,1536]{1,0:T(8,128)(2,1)} %param.17), channel_id=1, source_target_pairs={{0,7},{1,0},{2,1},{3,2},{4,3},{5,4},{6,5},{7,6},{8,15},{9,8},{10,9... | collective-permute-start | bytes 1179656 | tf_op jit(solution)/shard_map/ppermute | solution.py:38
  6.6 2.2 %broadcast_in_dim.90 = bf16[8,64,1536]{2,1,0:T(8,128)(2,1)} broadcast(bf16[64,1536]{1,0:T(8,128)(2,1)} %param.18), dimensions={1,2} | broadcast | bytes 1769472 | tf_op jit(solution)/shard_map/broadcast_in_dim | solution.py:35
  8.8 6.7 %all-to-all-start = ((bf16[8,64,1536]{2,1,0:T(8,128)(2,1)}), bf16[8,64,1536]{2,1,0:T(8,128)(2,1)S(1)}, u32[]{:S(2)}, u32[]{:S(2)}) async-start(bf16[8,64,1536]{2,1,0:T(8,128)(2,1)} %broadcast_in_dim.90), calls=%async_computation | async-start | bytes 3145728 | tf_op jit(solution)/shard_map/all_to_all | solution.py:36
  15.4 0.6 iota_multiply_fusion.1
  16.0 0.5 iota_multiply_fusion
  16.6 1.3 collective-permute-start.2
  17.9 2.8 %collective-permute-start.6 = (bf16[128,1536]{1,0:T(8,128)(2,1)S(1)}, bf16[128,1536]{1,0:T(8,128)(2,1)S(1)}, u32[]{:S(2)}, u32[]{:S(2)}) collective-permute-start(bf16[128,1536]{1,0:T(8,128)(2,1)S(1)} %collective-permute-done.5), channel_id=1, source_target_pairs={{0,7},{1,0},{2,1},{3,2},{4,3},{5,4},{6,5},{7,6},{8,15},{9,8},{10,9... | collective-permute-start | bytes 1179656 | tf_op jit(solution)/shard_map/ppermute | solution.py:43
  20.7 2.2 %broadcast_in_dim.159 = bf16[10,128,1536]{2,1,0:T(8,128)(2,1)} broadcast(bf16[128,1536]{1,0:T(8,128)(2,1)S(1)} %copy-done.1), dimensions={1,2} | broadcast | bytes 4325376 | tf_op jit(solution)/shard_map/broadcast_in_dim | solution.py:44
  22.9 0.8 bitcast_dynamic-update-slice_fusion.6
  23.7 0.8 bitcast_dynamic-update-slice_fusion.5
  24.5 5.3 %collective-permute-done.1 = bf16[128,1536]{1,0:T(8,128)(2,1)S(1)} collective-permute-done((bf16[128,1536]{1,0:T(8,128)(2,1)S(1)}, bf16[128,1536]{1,0:T(8,128)(2,1)S(1)}, u32[]{:S(2)}, u32[]{:S(2)}) %collective-permute-start.1) | collective-permute-done | bytes 393248 | tf_op jit(solution)/shard_map/ppermute | solution.py:42
  29.8 2.7 %collective-permute-start.8 = (bf16[128,1536]{1,0:T(8,128)(2,1)S(1)}, bf16[128,1536]{1,0:T(8,128)(2,1)S(1)}, u32[]{:S(2)}, u32[]{:S(2)}) collective-permute-start(bf16[128,1536]{1,0:T(8,128)(2,1)S(1)} %collective-permute-done.6), channel_id=1, source_target_pairs={{0,7},{1,0},{2,1},{3,2},{4,3},{5,4},{6,5},{7,6},{8,15},{9,8},{10,9... | collective-permute-start | bytes 1179656 | tf_op jit(solution)/shard_map/ppermute | solution.py:47
  32.4 0.8 bitcast_dynamic-update-slice_fusion.4
  33.2 3.9 %all-to-all-done = bf16[8,64,1536]{2,1,0:T(8,128)(2,1)S(1)} async-done(((bf16[8,64,1536]{2,1,0:T(8,128)(2,1)}), bf16[8,64,1536]{2,1,0:T(8,128)(2,1)S(1)}, u32[]{:S(2)}, u32[]{:S(2)}) %all-to-all-start) | async-done | bytes 1572896 | tf_op jit(solution)/shard_map/all_to_all | solution.py:36
  37.1 1.3 gather_fusion.1
  38.4 2.2 %collective-permute-start.3 = (bf16[2,64,1536]{2,1,0:T(8,128)(2,1)}, bf16[2,64,1536]{2,1,0:T(8,128)(2,1)}, u32[]{:S(2)}, u32[]{:S(2)}) collective-permute-start(bf16[2,64,1536]{2,1,0:T(8,128)(2,1)} %gather_fusion.1), channel_id=1, source_target_pairs={{0,16},{16,0},{1,17},{17,1},{2,18},{18,2},{3,19},{19,3},{4,20},{20... | collective-permute-start | bytes 1179656 | tf_op jit(solution)/shard_map/ppermute | solution.py:52
  40.6 0.8 bitcast_dynamic-update-slice_fusion.3
  41.4 0.6 gather_fusion
  41.9 0.3 collective-permute-done.3
  42.3 1.1 broadcast_select_fusion
  43.4 0.4 collective-permute-start.4
  43.8 0.8 bitcast_dynamic-update-slice_fusion.2
  44.6 0.8 bitcast_dynamic-update-slice_fusion.1
  45.4 2.1 %slice.72 = bf16[8,128,1536]{2,1,0:T(8,128)(2,1)S(1)} slice(bf16[10,128,1536]{2,1,0:T(8,128)(2,1)} %bitcast_dynamic-update-slice_fusion.1), slice={[0:8], [0:128], [0:1536]} | slice | bytes 6291456 | tf_op jit(solution)/shard_map/slice | solution.py:69
  47.5 6.3 %collective-permute-done.4 = bf16[2,64,1536]{2,1,0:T(8,128)(2,1)S(1)} collective-permute-done((bf16[2,64,1536]{2,1,0:T(8,128)(2,1)S(1)}, bf16[2,64,1536]{2,1,0:T(8,128)(2,1)S(1)}, u32[]{:S(2)}, u32[]{:S(2)}) %collective-permute-start.4) | collective-permute-done | bytes 393248 | tf_op jit(solution)/shard_map/ppermute | solution.py:55
  54.0 1.0 fusion.1
  55.0 0.4 fusion.4
  55.5 0.6 broadcast_in_dim.166
  56.1 5.2 %all-to-all-start.1 = ((f32[8,1,1024]{2,1,0:T(1,128)}), f32[8,1,1024]{2,1,0:T(1,128)S(1)}, u32[]{:S(2)}, u32[]{:S(2)}) async-start(f32[8,1,1024]{2,1,0:T(1,128)} %broadcast_in_dim.166), calls=%async_computation.1 | async-start | bytes 65536 | tf_op jit(solution)/shard_map/all_to_all | solution.py:24
  61.5 0.7 convert_reduce_fusion.1
  62.4 0.6 gather_fusion.2
  63.6 0.8 bitcast_dynamic-update-slice_fusion
  64.6 3.6 %all-to-all-done.1 = f32[8,1,1024]{2,1,0:T(1,128)S(1)} async-done(((f32[8,1,1024]{2,1,0:T(1,128)}), f32[8,1,1024]{2,1,0:T(1,128)S(1)}, u32[]{:S(2)}, u32[]{:S(2)}) %all-to-all-start.1) | async-done | bytes 32800 | tf_op jit(solution)/shard_map/all_to_all | solution.py:24
  68.4 14.3 %all_to_all.58 = f32[32,1,384]{2,1,0:T(1,128)S(1)} all-to-all(f32[32,1,384]{2,1,0:T(1,128)S(1)} %broadcast_in_dim.169), channel_id=1, replica_groups=mesh['y'=4,'xh'=2,'c'=2,'xl'=2,'z'=8] {'y','xh','c','xl'}, dimensions={0} | all-to-all | bytes 98304 | tf_op jit(solution)/shard_map/all_to_all | solution.py:24
  83.2 0.2 multiply_reduce_fusion.4
  83.4 9.2 %all_to_all.59 = f32[8,1,1024]{2,1,0:T(1,128)S(1)} all-to-all(f32[8,1,1024]{2,1,0:T(1,128)S(1)} %broadcast_in_dim.170), channel_id=1, replica_groups=mesh['y'=4,'xh'=2,'c'=2,'xl'=2,'z'=8] {'z'}, dimensions={0} | all-to-all | bytes 65536 | tf_op jit(solution)/shard_map/all_to_all | solution.py:24
  92.8 12.0 %all_to_all.60 = f32[32,1,256]{2,1,0:T(1,128)S(1)} all-to-all(f32[32,1,256]{2,1,0:T(1,128)S(1)} %broadcast_in_dim.171), channel_id=1, replica_groups=mesh['y'=4,'xh'=2,'c'=2,'xl'=2,'z'=8] {'y','xh','c','xl'}, dimensions={0} | all-to-all | bytes 65536 | tf_op jit(solution)/shard_map/all_to_all | solution.py:24
  105.0 0.2 multiply_reduce_fusion.2
  105.2 9.3 %all_to_all.61 = f32[8,1,1024]{2,1,0:T(1,128)S(1)} all-to-all(f32[8,1,1024]{2,1,0:T(1,128)S(1)} %broadcast_in_dim.172), channel_id=1, replica_groups=mesh['y'=4,'xh'=2,'c'=2,'xl'=2,'z'=8] {'z'}, dimensions={0} | all-to-all | bytes 65536 | tf_op jit(solution)/shard_map/all_to_all | solution.py:24
  114.6 12.1 %all_to_all.62 = f32[32,1,256]{2,1,0:T(1,128)S(1)} all-to-all(f32[32,1,256]{2,1,0:T(1,128)S(1)} %broadcast_in_dim.173), channel_id=1, replica_groups=mesh['y'=4,'xh'=2,'c'=2,'xl'=2,'z'=8] {'y','xh','c','xl'}, dimensions={0} | all-to-all | bytes 65536 | tf_op jit(solution)/shard_map/all_to_all | solution.py:24
  127.0 0.6 broadcast_in_dim.174
  127.7 3.3 %all-to-all-start.7 = ((f32[8,1,1024]{2,1,0:T(1,128)}), f32[8,1,1024]{2,1,0:T(1,128)S(1)}, u32[]{:S(2)}, u32[]{:S(2)}) async-start(f32[8,1,1024]{2,1,0:T(1,128)} %broadcast_in_dim.174), calls=%async_computation.7 | async-start | bytes 65536 | tf_op jit(solution)/shard_map/all_to_all | solution.py:24
  131.4 3.8 %slice.58 = bf16[8,128,1536]{2,1,0:T(8,128)(2,1)} slice(bf16[10,128,1536]{2,1,0:T(8,128)(2,1)} %bitcast_dynamic-update-slice_fusion), slice={[0:8], [0:128], [0:1536]} | slice | bytes 6291456 | tf_op jit(solution)/shard_map/slice | solution.py:92
  135.2 2.6 %all-to-all-done.7 = f32[8,1,1024]{2,1,0:T(1,128)S(1)} async-done(((f32[8,1,1024]{2,1,0:T(1,128)}), f32[8,1,1024]{2,1,0:T(1,128)S(1)}, u32[]{:S(2)}, u32[]{:S(2)}) %all-to-all-start.7) | async-done | bytes 32800 | tf_op jit(solution)/shard_map/all_to_all | solution.py:24
  138.1 0.3 fusion.11
  138.4 0.4 collective-permute-start.11
  138.8 1.0 copy-done
  139.8 0.6 fusion.38
  140.4 0.4 collective-permute-start.12
  140.8 0.6 fusion.37
  141.5 1.2 collective-permute-start.10
  142.7 2.7 %collective-permute-start.14 = (f32[2,32,128]{2,1,0:T(8,128)S(1)}, f32[2,32,128]{2,1,0:T(8,128)S(1)}, u32[]{:S(2)}, u32[]{:S(2)}) collective-permute-start(f32[2,32,128]{2,1,0:T(8,128)S(1)} %get-tuple-element.56), channel_id=1, source_target_pairs={{0,16},{16,0},{1,17},{17,1},{2,18},{18,2},{3,19},{19,3},{4,20},{20... | collective-permute-start | bytes 98312 | tf_op jit(solution)/shard_map/ppermute | solution.py:113
  145.4 0.8 collective-permute-done.14
  146.5 3.9 %collective-permute-start.15 = (bf16[32,1536]{1,0:T(8,128)(2,1)S(1)}, bf16[32,1536]{1,0:T(8,128)(2,1)S(1)}, u32[]{:S(2)}, u32[]{:S(2)}) collective-permute-start(bf16[32,1536]{1,0:T(8,128)(2,1)S(1)} %get-tuple-element.54), channel_id=1, source_target_pairs={{0,16},{16,0},{1,17},{17,1},{2,18},{18,2},{3,19},{19,3},{4,20},{20... | collective-permute-start | bytes 294920 | tf_op jit(solution)/shard_map/ppermute | solution.py:113
  150.3 0.3 collective-permute-done.10
  150.7 2.2 %collective-permute-start.13 = (bf16[32,1536]{1,0:T(8,128)(2,1)S(1)}, bf16[32,1536]{1,0:T(8,128)(2,1)S(1)}, u32[]{:S(2)}, u32[]{:S(2)}) collective-permute-start(bf16[32,1536]{1,0:T(8,128)(2,1)S(1)} %get-tuple-element.52), channel_id=1, source_target_pairs={{0,16},{16,0},{1,17},{17,1},{2,18},{18,2},{3,19},{19,3},{4,20},{20... | collective-permute-start | bytes 294920 | tf_op jit(solution)/shard_map/ppermute | solution.py:113
  152.9 0.9 collective-permute-done.13
  153.8 0.5 select_add_fusion
  154.4 26.0 %all_to_all.63 = bf16[8,2,32,1664]{3,2,1,0:T(8,128)(2,1)S(1)} all-to-all(bf16[8,2,32,1664]{3,2,1,0:T(8,128)(2,1)S(1)} %select_add_fusion), channel_id=1, replica_groups=mesh['y'=4,'xh'=2,'c'=2,'xl'=2,'z'=8] {'y','xh'}, dimensions={0} | all-to-all | bytes 3407872 | tf_op jit(solution)/shard_map/all_to_all | solution.py:148
  180.4 0.2 convert_reduce_fusion
  180.8 2.0 %collective-permute-start.16 = (f32[32,1536]{1,0:T(8,128)S(1)}, f32[32,1536]{1,0:T(8,128)S(1)}, u32[]{:S(2)}, u32[]{:S(2)}) collective-permute-start(f32[32,1536]{1,0:T(8,128)S(1)} %dynamic-slice_bitcast_fusion), channel_id=1, source_target_pairs={{0,16},{16,0},{1,17},{17,1},{2,18},{18,2},{3,19},{19,3},{4,20},{20... | collective-permute-start | bytes 589832 | tf_op jit(solution)/shard_map/ppermute | solution.py:113
  182.8 1.1 collective-permute-done.16
  183.9 0.8 pad_maximum_fusion.1
  (119 shorter events, 3.6 us)
Async XLA Ops:
  0.0 20.7 %copy-start.1 = (bf16[128,1536]{1,0:T(8,128)(2,1)S(1)}, bf16[128,1536]{1,0:T(8,128)(2,1)}, u32[]{:S(2)}) copy-start(bf16[128,1536]{1,0:T(8,128)(2,1)} %param.17) | copy-start | bytes 1179652
  0.0 16.5 %copy-start.12 = (s32[1,2]{1,0:T(1,128)S(1)}, s32[1,2]{1,0:T(1,128)}, u32[]{:S(2)}) copy-start(s32[1,2]{1,0:T(1,128)} %param.20) | copy-start | bytes 28
  0.0 16.6 %copy-start.9 = (s32[1,2]{1,0:T(1,128)S(1)}, s32[1,2]{1,0:T(1,128)}, u32[]{:S(2)}) copy-start(s32[1,2]{1,0:T(1,128)} %param.19) | copy-start | bytes 28
  0.0 16.6 %collective-permute-start = (bf16[128,1536]{1,0:T(8,128)(2,1)}, bf16[128,1536]{1,0:T(8,128)(2,1)S(1)}, u32[]{:S(2)}, u32[]{:S(2)}) collective-permute-start(bf16[128,1536]{1,0:T(8,128)(2,1)} %param.17), channel_id=1, source_target_pairs={{0,1},{1,2},{2,3},{3,4},{4,5},{5,6},{6,7},{7,0},{8,9},{9,10},{10,1... | collective-permute-start | bytes 1179656 | tf_op jit(solution)/shard_map/ppermute | solution.py:37
  2.6 15.3 %collective-permute-start.5 = (bf16[128,1536]{1,0:T(8,128)(2,1)}, bf16[128,1536]{1,0:T(8,128)(2,1)S(1)}, u32[]{:S(2)}, u32[]{:S(2)}) collective-permute-start(bf16[128,1536]{1,0:T(8,128)(2,1)} %param.17), channel_id=1, source_target_pairs={{0,7},{1,0},{2,1},{3,2},{4,3},{5,4},{6,5},{7,6},{8,15},{9,8},{10,9... | collective-permute-start | bytes 1179656 | tf_op jit(solution)/shard_map/ppermute | solution.py:38
  8.8 28.3 %all-to-all-start = ((bf16[8,64,1536]{2,1,0:T(8,128)(2,1)}), bf16[8,64,1536]{2,1,0:T(8,128)(2,1)S(1)}, u32[]{:S(2)}, u32[]{:S(2)}) async-start(bf16[8,64,1536]{2,1,0:T(8,128)(2,1)} %broadcast_in_dim.90), calls=%async_computation | async-start | bytes 3145728 | tf_op jit(solution)/shard_map/all_to_all | solution.py:36
  16.6 7.9 %collective-permute-start.2 = (s32[2]{0:T(128)S(1)}, s32[2]{0:T(128)S(1)}, u32[]{:S(2)}, u32[]{:S(2)}) collective-permute-start(s32[2]{0:T(128)S(1)} %bitcast.161), channel_id=1, source_target_pairs={{0,16},{16,0},{1,17},{17,1},{2,18},{18,2},{3,19},{19,3},{4,20},{20... | collective-permute-start | bytes 32 | tf_op jit(solution)/shard_map/ppermute | solution.py:41
  17.9 11.9 %collective-permute-start.1 = (bf16[128,1536]{1,0:T(8,128)(2,1)S(1)}, bf16[128,1536]{1,0:T(8,128)(2,1)S(1)}, u32[]{:S(2)}, u32[]{:S(2)}) collective-permute-start(bf16[128,1536]{1,0:T(8,128)(2,1)S(1)} %collective-permute-done), channel_id=1, source_target_pairs={{0,1},{1,2},{2,3},{3,4},{4,5},{5,6},{6,7},{7,0},{8,9},{9,10},{10,1... | collective-permute-start | bytes 1179656 | tf_op jit(solution)/shard_map/ppermute | solution.py:42
  17.9 11.9 %collective-permute-start.6 = (bf16[128,1536]{1,0:T(8,128)(2,1)S(1)}, bf16[128,1536]{1,0:T(8,128)(2,1)S(1)}, u32[]{:S(2)}, u32[]{:S(2)}) collective-permute-start(bf16[128,1536]{1,0:T(8,128)(2,1)S(1)} %collective-permute-done.5), channel_id=1, source_target_pairs={{0,7},{1,0},{2,1},{3,2},{4,3},{5,4},{6,5},{7,6},{8,15},{9,8},{10,9... | collective-permute-start | bytes 1179656 | tf_op jit(solution)/shard_map/ppermute | solution.py:43
  24.4 8.0 %copy-start.13 = (s32[2]{0:T(128)}, s32[2]{0:T(128)S(1)}, u32[]{:S(2)}) copy-start(s32[2]{0:T(128)S(1)} %collective-permute-done.2) | copy-start | bytes 28
  29.7 14.0 %collective-permute-start.7 = (bf16[128,1536]{1,0:T(8,128)(2,1)S(1)}, bf16[128,1536]{1,0:T(8,128)(2,1)S(1)}, u32[]{:S(2)}, u32[]{:S(2)}) collective-permute-start(bf16[128,1536]{1,0:T(8,128)(2,1)S(1)} %collective-permute-done.1), channel_id=1, source_target_pairs={{0,1},{1,2},{2,3},{3,4},{4,5},{5,6},{6,7},{7,0},{8,9},{9,10},{10,1... | collective-permute-start | bytes 1179656 | tf_op jit(solution)/shard_map/ppermute | solution.py:46
  29.8 14.0 %collective-permute-start.8 = (bf16[128,1536]{1,0:T(8,128)(2,1)S(1)}, bf16[128,1536]{1,0:T(8,128)(2,1)S(1)}, u32[]{:S(2)}, u32[]{:S(2)}) collective-permute-start(bf16[128,1536]{1,0:T(8,128)(2,1)S(1)} %collective-permute-done.6), channel_id=1, source_target_pairs={{0,7},{1,0},{2,1},{3,2},{4,3},{5,4},{6,5},{7,6},{8,15},{9,8},{10,9... | collective-permute-start | bytes 1179656 | tf_op jit(solution)/shard_map/ppermute | solution.py:47
  38.4 3.9 %collective-permute-start.3 = (bf16[2,64,1536]{2,1,0:T(8,128)(2,1)}, bf16[2,64,1536]{2,1,0:T(8,128)(2,1)}, u32[]{:S(2)}, u32[]{:S(2)}) collective-permute-start(bf16[2,64,1536]{2,1,0:T(8,128)(2,1)} %gather_fusion.1), channel_id=1, source_target_pairs={{0,16},{16,0},{1,17},{17,1},{2,18},{18,2},{3,19},{19,3},{4,20},{20... | collective-permute-start | bytes 1179656 | tf_op jit(solution)/shard_map/ppermute | solution.py:52
  43.4 10.4 %collective-permute-start.4 = (bf16[2,64,1536]{2,1,0:T(8,128)(2,1)S(1)}, bf16[2,64,1536]{2,1,0:T(8,128)(2,1)S(1)}, u32[]{:S(2)}, u32[]{:S(2)}) collective-permute-start(bf16[2,64,1536]{2,1,0:T(8,128)(2,1)S(1)} %broadcast_select_fusion), channel_id=1, source_target_pairs={{0,8},{8,0},{1,9},{9,1},{2,10},{10,2},{3,11},{11,3},{4,12},{12,4},... | collective-permute-start | bytes 1179656 | tf_op jit(solution)/shard_map/ppermute | solution.py:55
  43.8 11.2 %collective-permute-start.9 = (bf16[128,1536]{1,0:T(8,128)(2,1)S(1)}, bf16[128,1536]{1,0:T(8,128)(2,1)S(1)}, u32[]{:S(2)}, u32[]{:S(2)}) collective-permute-start(bf16[128,1536]{1,0:T(8,128)(2,1)S(1)} %collective-permute-done.7), channel_id=1, source_target_pairs={{0,1},{1,2},{2,3},{3,4},{4,5},{5,6},{6,7},{7,0},{8,9},{9,10},{10,1... | collective-permute-start | bytes 1179656 | tf_op jit(solution)/shard_map/ppermute | solution.py:57
  53.9 7.4 %copy-start.10 = (s32[2]{0:T(128)S(1)}, s32[2]{0:T(128)}, u32[]{:S(2)}) copy-start(s32[2]{0:T(128)} %iota_multiply_fusion.1) | copy-start | bytes 28
  53.9 7.6 %copy-start.2 = (s32[16384]{0:T(1024)S(1)}, s32[16384]{0:T(1024)}, u32[]{:S(2)}) copy-start(s32[16384]{0:T(1024)} %param.21) | copy-start | bytes 196612
  54.0 8.3 %copy-start.14 = (s32[2]{0:T(128)S(1)}, s32[2]{0:T(128)}, u32[]{:S(2)}) copy-start(s32[2]{0:T(128)} %copy-done.13) | copy-start | bytes 28
  54.0 8.3 %copy-start.11 = (s32[8]{0:T(128)S(1)}, s32[8]{0:T(128)}, u32[]{:S(2)}) copy-start(s32[8]{0:T(128)} %iota_multiply_fusion) | copy-start | bytes 100
  56.1 12.1 %all-to-all-start.1 = ((f32[8,1,1024]{2,1,0:T(1,128)}), f32[8,1,1024]{2,1,0:T(1,128)S(1)}, u32[]{:S(2)}, u32[]{:S(2)}) async-start(f32[8,1,1024]{2,1,0:T(1,128)} %broadcast_in_dim.166), calls=%async_computation.1 | async-start | bytes 65536 | tf_op jit(solution)/shard_map/all_to_all | solution.py:24
  127.7 10.1 %all-to-all-start.7 = ((f32[8,1,1024]{2,1,0:T(1,128)}), f32[8,1,1024]{2,1,0:T(1,128)S(1)}, u32[]{:S(2)}, u32[]{:S(2)}) async-start(f32[8,1,1024]{2,1,0:T(1,128)} %broadcast_in_dim.174), calls=%async_computation.7 | async-start | bytes 65536 | tf_op jit(solution)/shard_map/all_to_all | solution.py:24
  137.9 1.9 %copy-start = (bf16[8,128,1536]{2,1,0:T(8,128)(2,1)S(1)}, bf16[8,128,1536]{2,1,0:T(8,128)(2,1)}, u32[]{:S(2)}) copy-start(bf16[8,128,1536]{2,1,0:T(8,128)(2,1)} %slice.58) | copy-start | bytes 9437188
  138.4 4.3 %collective-permute-start.11 = (f32[2,64,128]{2,1,0:T(8,128)S(1)}, f32[2,64,128]{2,1,0:T(8,128)S(1)}, u32[]{:S(2)}, u32[]{:S(2)}) collective-permute-start(f32[2,64,128]{2,1,0:T(8,128)S(1)} %dynamic-slice_bitcast_fusion.5), channel_id=1, source_target_pairs={{0,8},{8,0},{1,9},{9,1},{2,10},{10,2},{3,11},{11,3},{4,12},{12,4},... | collective-permute-start | bytes 196616 | tf_op jit(solution)/shard_map/ppermute | solution.py:113
  140.4 6.0 %collective-permute-start.12 = (bf16[64,1536]{1,0:T(8,128)(2,1)S(1)}, bf16[64,1536]{1,0:T(8,128)(2,1)S(1)}, u32[]{:S(2)}, u32[]{:S(2)}) collective-permute-start(bf16[64,1536]{1,0:T(8,128)(2,1)S(1)} %fusion.8), channel_id=1, source_target_pairs={{0,8},{8,0},{1,9},{9,1},{2,10},{10,2},{3,11},{11,3},{4,12},{12,4},... | collective-permute-start | bytes 589832 | tf_op jit(solution)/shard_map/ppermute | solution.py:138
  140.8 4.6 %copy-start.6 = (f32[128]{0:T(128)S(1)}, f32[128]{0:T(128)}, u32[]{:S(2)}) copy-start(f32[128]{0:T(128)} %constant.206) | copy-start | bytes 1540
  140.8 4.6 %copy-start.7 = (f32[128]{0:T(128)S(1)}, f32[128]{0:T(128)}, u32[]{:S(2)}) copy-start(f32[128]{0:T(128)} %constant.205) | copy-start | bytes 1540
  140.8 4.6 %copy-start.8 = (f32[128]{0:T(128)S(1)}, f32[128]{0:T(128)}, u32[]{:S(2)}) copy-start(f32[128]{0:T(128)} %constant.204) | copy-start | bytes 1540
  140.8 5.4 %copy-start.3 = (f32[128]{0:T(128)S(1)}, f32[128]{0:T(128)}, u32[]{:S(2)}) copy-start(f32[128]{0:T(128)} %constant.209) | copy-start | bytes 1540
  140.8 5.4 %copy-start.4 = (f32[128]{0:T(128)S(1)}, f32[128]{0:T(128)}, u32[]{:S(2)}) copy-start(f32[128]{0:T(128)} %constant.208) | copy-start | bytes 1540
  140.8 5.4 %copy-start.5 = (f32[128]{0:T(128)S(1)}, f32[128]{0:T(128)}, u32[]{:S(2)}) copy-start(f32[128]{0:T(128)} %constant.207) | copy-start | bytes 1540
  141.5 9.1 %collective-permute-start.10 = (bf16[64,1536]{1,0:T(8,128)(2,1)S(1)}, bf16[64,1536]{1,0:T(8,128)(2,1)S(1)}, u32[]{:S(2)}, u32[]{:S(2)}) collective-permute-start(bf16[64,1536]{1,0:T(8,128)(2,1)S(1)} %fusion.7), channel_id=1, source_target_pairs={{0,8},{8,0},{1,9},{9,1},{2,10},{10,2},{3,11},{11,3},{4,12},{12,4},... | collective-permute-start | bytes 589832 | tf_op jit(solution)/shard_map/ppermute | solution.py:138
  142.7 3.5 %collective-permute-start.14 = (f32[2,32,128]{2,1,0:T(8,128)S(1)}, f32[2,32,128]{2,1,0:T(8,128)S(1)}, u32[]{:S(2)}, u32[]{:S(2)}) collective-permute-start(f32[2,32,128]{2,1,0:T(8,128)S(1)} %get-tuple-element.56), channel_id=1, source_target_pairs={{0,16},{16,0},{1,17},{17,1},{2,18},{18,2},{3,19},{19,3},{4,20},{20... | collective-permute-start | bytes 98312 | tf_op jit(solution)/shard_map/ppermute | solution.py:113
  146.5 6.4 %collective-permute-start.15 = (bf16[32,1536]{1,0:T(8,128)(2,1)S(1)}, bf16[32,1536]{1,0:T(8,128)(2,1)S(1)}, u32[]{:S(2)}, u32[]{:S(2)}) collective-permute-start(bf16[32,1536]{1,0:T(8,128)(2,1)S(1)} %get-tuple-element.54), channel_id=1, source_target_pairs={{0,16},{16,0},{1,17},{17,1},{2,18},{18,2},{3,19},{19,3},{4,20},{20... | collective-permute-start | bytes 294920 | tf_op jit(solution)/shard_map/ppermute | solution.py:113
  150.7 3.1 %collective-permute-start.13 = (bf16[32,1536]{1,0:T(8,128)(2,1)S(1)}, bf16[32,1536]{1,0:T(8,128)(2,1)S(1)}, u32[]{:S(2)}, u32[]{:S(2)}) collective-permute-start(bf16[32,1536]{1,0:T(8,128)(2,1)S(1)} %get-tuple-element.52), channel_id=1, source_target_pairs={{0,16},{16,0},{1,17},{17,1},{2,18},{18,2},{3,19},{19,3},{4,20},{20... | collective-permute-start | bytes 294920 | tf_op jit(solution)/shard_map/ppermute | solution.py:113
  180.8 3.1 %collective-permute-start.16 = (f32[32,1536]{1,0:T(8,128)S(1)}, f32[32,1536]{1,0:T(8,128)S(1)}, u32[]{:S(2)}, u32[]{:S(2)}) collective-permute-start(f32[32,1536]{1,0:T(8,128)S(1)} %dynamic-slice_bitcast_fusion), channel_id=1, source_target_pairs={{0,16},{16,0},{1,17},{17,1},{2,18},{18,2},{3,19},{19,3},{4,20},{20... | collective-permute-start | bytes 589832 | tf_op jit(solution)/shard_map/ppermute | solution.py:113

commit v5 on v4

--- a/solution.py
+++ b/solution.py
@@ -83,10 +83,8 @@
     own = lax.dynamic_slice(own, (0, (z % 2) * 64), (4, 64)).reshape(2, 128)
     factor = jnp.float32(rows * 256) / jnp.sum(sizes.astype(jnp.float32))
     target_pair = own.astype(jnp.float32) * factor
-    grid = lax.broadcasted_iota(jnp.int32, (4, NY * NXH, NC), 1) * NC + lax.broadcasted_iota(
-        jnp.int32, (4, NY * NXH, NC), 2
-    )
-    hits = jnp.concatenate([slots, slots_other])[:, None, None] == grid
+    grid = lax.broadcasted_iota(jnp.int32, (4, NY * NXH), 1) * NC + c
+    hits = jnp.concatenate([slots, slots_other])[:, None] == grid
     hits = [hits[i] for i in range(4)]
     got, ids, target_pair, hits, slots, pts = after((got, ids, target_pair, hits, slots, pts))
     pts = pts[:NZ].reshape(NZ * rows, width)
@@ -117,8 +115,8 @@
     tots = tots.reshape(2, 2, 64, 128)
     tots = jnp.swapaxes(tots, 0, 1)
     t_mine, t_got = halved(tots, xl, "xl")
-    tots = jnp.swapaxes((t_mine + t_got).reshape(2, 2, 32, 128), 0, 1)
-    tots = halved(tots, c, "c")
+    tots = t_mine + t_got
+    tots = (tots, lax.ppermute(tots, "c", SWAP))
 
     def in_thirds(value, first):
         at = np.eye(128, dtype=np.float32)[first : first + 3]
@@ -136,20 +134,18 @@
         mine = lax.dynamic_index_in_dim(sums, xl, 0, keepdims=False)
         give = lax.dynamic_index_in_dim(sums, 1 - xl, 0, keepdims=False).astype(jnp.bfloat16)
         got = lax.ppermute(give, "xl", SWAP)
-        sums = (mine + got.astype(jnp.float32)).astype(jnp.bfloat16).reshape(2, 32, width)
-        pair = halved(sums, c, "c")
+        sums = (mine + got.astype(jnp.float32)).astype(jnp.bfloat16)
+        pair = (sums, lax.ppermute(sums, "c", SWAP))
         parts.append([jnp.concatenate([pair[i], in_thirds(tots[i][k], 4 * i)], axis=1) for i in (0, 1)])
     zero = jnp.zeros((), jnp.bfloat16)
 
     def placed(first, second, a, b):
-        return jnp.where(first[:, :, None, None], a, jnp.where(second[:, :, None, None], b, zero))
+        return jnp.where(first[:, None, None], a, jnp.where(second[:, None, None], b, zero))
 
     spread = placed(hits[0], hits[1], parts[0][0], parts[1][0]) + placed(hits[2], hits[3], parts[0][1], parts[1][1])
     landed = lax.all_to_all(spread, ("y", "xh"), 0, 0)
     owned = jnp.sum(landed.astype(jnp.float32), axis=0)
-    owned = owned[:, :, :width] / jnp.sum(owned[:, :, width:], axis=2, keepdims=True)
-    o_mine, o_got = halved(owned, c, "c")
-    return ordered(c, o_mine, o_got).reshape(64, width)
+    return owned[:, :width] / jnp.sum(owned[:, width:], axis=1, keepdims=True)
 
 
 def solution(mesh):

time: 185 us -> 182 us (0.984)
  starting transfers between devices: 43.9 us -> 41.8 us
    ppermute x5 -> x1, starting transfers between devices: 11.1 us -> 0.43 us  [halved(): return (mine, lax.ppermute(give, axis_name, SWAP))]
    ppermute x0 -> x3, starting transfers between devices: none -> 8.67 us  [the longest x2 6.01 us: shards(): pair = (sums, lax.ppermute(sums, 'c', SWAP))]
    ppermute x5 -> x1, waiting for transfers between devices: 2.8 us -> 0.01 us  [halved(): return (mine, lax.ppermute(give, axis_name, SWAP))]
    ppermute x0 -> x3, waiting for transfers between devices: none -> 1.85 us  [the longest x2 0.99 us: shards(): pair = (sums, lax.ppermute(sums, 'c', SWAP))]
  transfers between devices with their start and end apart: 20 -> 19, of which waited for: 11 -> 10; matrix products, arithmetic and copies ran while one was open for 13% -> 13% of each run, Pallas kernels for 0% -> 0%
where the time goes in v5:
time: 182 us
  blocking collectives  83 us (46%)
  starting transfers between devices  41.8 us (23%)
  waiting for transfers between devices  24.7 us (14%)
  local copies, waits for them, and re-layouts  21.2 us (12%)
  other arithmetic  6.92 us (4%)
  matrix products  2.85 us (2%)
    all_to_all x5, blocking collectives, exchange(): lax.all_to_all(jnp.broadcast_to(row[None], (n,) + row.shape), axes, 0, 0)  57 us
    all_to_all x1, blocking collectives, shards(): landed = lax.all_to_all(spread, ('y', 'xh'), 0, 0)  26 us
    all_to_all x2, starting transfers between devices, exchange(): lax.all_to_all(jnp.broadcast_to(row[None], (n,) + row.shape), axes, 0, 0)  8.54 us
    all_to_all x1, starting transfers between devices, shards(): allc = lax.all_to_all(spread_cents, ('y', 'xh'), 0, 0)  6.65 us
    all_to_all x2, waiting for transfers between devices, exchange(): lax.all_to_all(jnp.broadcast_to(row[None], (n,) + row.shape), axes, 0, 0)  6.63 us
    ppermute x1, waiting for transfers between devices, shards(): kept_xl = lax.ppermute(kept, 'xl', SWAP)  6.3 us
    ppermute x2, starting transfers between devices, shards(): pair = (sums, lax.ppermute(sums, 'c', SWAP))  6.01 us
    dynamic_update_slice x7, local copies, waits for them, and re-layouts, put(): return lax.dynamic_update_slice(buf, part[None], (at % NZ, 0, 0))  5.46 us
  transfers between devices with their start and end apart: 19, of which 10 were waited for; matrix products, arithmetic and copies ran while one was open for 13% of the time, Pallas kernels for 0%

profile of v5, /device:TPU:1, one launch (start us, length us, event | category | flops | bytes accessed | tf_op | source)
XLA Modules:
  0.0 181.7 jit_solution(8785626972965390595)
XLA Ops:
  0.0 2.5 %collective-permute-start = (bf16[128,1536]{1,0:T(8,128)(2,1)}, bf16[128,1536]{1,0:T(8,128)(2,1)S(1)}, u32[]{:S(2)}, u32[]{:S(2)}) collective-permute-start(bf16[128,1536]{1,0:T(8,128)(2,1)} %param.17), channel_id=1, source_target_pairs={{0,1},{1,2},{2,3},{3,4},{4,5},{5,6},{6,7},{7,0},{8,9},{9,10},{10,1... | collective-permute-start | bytes 1179656 | tf_op jit(solution)/shard_map/ppermute | solution.py:37
  2.6 4.0 %collective-permute-start.5 = (bf16[128,1536]{1,0:T(8,128)(2,1)}, bf16[128,1536]{1,0:T(8,128)(2,1)S(1)}, u32[]{:S(2)}, u32[]{:S(2)}) collective-permute-start(bf16[128,1536]{1,0:T(8,128)(2,1)} %param.17), channel_id=1, source_target_pairs={{0,7},{1,0},{2,1},{3,2},{4,3},{5,4},{6,5},{7,6},{8,15},{9,8},{10,9... | collective-permute-start | bytes 1179656 | tf_op jit(solution)/shard_map/ppermute | solution.py:38
  6.6 2.2 %broadcast_in_dim.90 = bf16[8,64,1536]{2,1,0:T(8,128)(2,1)} broadcast(bf16[64,1536]{1,0:T(8,128)(2,1)} %param.18), dimensions={1,2} | broadcast | bytes 1769472 | tf_op jit(solution)/shard_map/broadcast_in_dim | solution.py:35
  8.8 6.7 %all-to-all-start = ((bf16[8,64,1536]{2,1,0:T(8,128)(2,1)}), bf16[8,64,1536]{2,1,0:T(8,128)(2,1)S(1)}, u32[]{:S(2)}, u32[]{:S(2)}) async-start(bf16[8,64,1536]{2,1,0:T(8,128)(2,1)} %broadcast_in_dim.90), calls=%async_computation | async-start | bytes 3145728 | tf_op jit(solution)/shard_map/all_to_all | solution.py:36
  15.4 0.6 iota_multiply_fusion
  16.0 0.5 multiply_add_fusion
  16.6 1.3 collective-permute-start.2
  17.9 2.8 %collective-permute-start.6 = (bf16[128,1536]{1,0:T(8,128)(2,1)S(1)}, bf16[128,1536]{1,0:T(8,128)(2,1)S(1)}, u32[]{:S(2)}, u32[]{:S(2)}) collective-permute-start(bf16[128,1536]{1,0:T(8,128)(2,1)S(1)} %collective-permute-done.5), channel_id=1, source_target_pairs={{0,7},{1,0},{2,1},{3,2},{4,3},{5,4},{6,5},{7,6},{8,15},{9,8},{10,9... | collective-permute-start | bytes 1179656 | tf_op jit(solution)/shard_map/ppermute | solution.py:43
  20.7 2.2 %broadcast_in_dim.159 = bf16[10,128,1536]{2,1,0:T(8,128)(2,1)} broadcast(bf16[128,1536]{1,0:T(8,128)(2,1)S(1)} %copy-done.1), dimensions={1,2} | broadcast | bytes 4325376 | tf_op jit(solution)/shard_map/broadcast_in_dim | solution.py:44
  22.9 0.8 bitcast_dynamic-update-slice_fusion.6
  23.7 0.8 bitcast_dynamic-update-slice_fusion.5
  24.5 5.3 %collective-permute-done.1 = bf16[128,1536]{1,0:T(8,128)(2,1)S(1)} collective-permute-done((bf16[128,1536]{1,0:T(8,128)(2,1)S(1)}, bf16[128,1536]{1,0:T(8,128)(2,1)S(1)}, u32[]{:S(2)}, u32[]{:S(2)}) %collective-permute-start.1) | collective-permute-done | bytes 393248 | tf_op jit(solution)/shard_map/ppermute | solution.py:42
  29.8 2.7 %collective-permute-start.8 = (bf16[128,1536]{1,0:T(8,128)(2,1)S(1)}, bf16[128,1536]{1,0:T(8,128)(2,1)S(1)}, u32[]{:S(2)}, u32[]{:S(2)}) collective-permute-start(bf16[128,1536]{1,0:T(8,128)(2,1)S(1)} %collective-permute-done.6), channel_id=1, source_target_pairs={{0,7},{1,0},{2,1},{3,2},{4,3},{5,4},{6,5},{7,6},{8,15},{9,8},{10,9... | collective-permute-start | bytes 1179656 | tf_op jit(solution)/shard_map/ppermute | solution.py:47
  32.4 0.8 bitcast_dynamic-update-slice_fusion.4
  33.2 3.9 %all-to-all-done = bf16[8,64,1536]{2,1,0:T(8,128)(2,1)S(1)} async-done(((bf16[8,64,1536]{2,1,0:T(8,128)(2,1)}), bf16[8,64,1536]{2,1,0:T(8,128)(2,1)S(1)}, u32[]{:S(2)}, u32[]{:S(2)}) %all-to-all-start) | async-done | bytes 1572896 | tf_op jit(solution)/shard_map/all_to_all | solution.py:36
  37.1 1.3 gather_fusion.1
  38.4 2.2 %collective-permute-start.3 = (bf16[2,64,1536]{2,1,0:T(8,128)(2,1)}, bf16[2,64,1536]{2,1,0:T(8,128)(2,1)}, u32[]{:S(2)}, u32[]{:S(2)}) collective-permute-start(bf16[2,64,1536]{2,1,0:T(8,128)(2,1)} %gather_fusion.1), channel_id=1, source_target_pairs={{0,16},{16,0},{1,17},{17,1},{2,18},{18,2},{3,19},{19,3},{4,20},{20... | collective-permute-start | bytes 1179656 | tf_op jit(solution)/shard_map/ppermute | solution.py:52
  40.6 0.8 bitcast_dynamic-update-slice_fusion.3
  41.4 0.6 gather_fusion
  41.9 0.3 collective-permute-done.3
  42.3 1.1 broadcast_select_fusion
  43.4 0.4 collective-permute-start.4
  43.8 0.8 bitcast_dynamic-update-slice_fusion.2
  44.6 0.8 bitcast_dynamic-update-slice_fusion.1
  45.4 2.1 %slice.70 = bf16[8,128,1536]{2,1,0:T(8,128)(2,1)S(1)} slice(bf16[10,128,1536]{2,1,0:T(8,128)(2,1)} %bitcast_dynamic-update-slice_fusion.1), slice={[0:8], [0:128], [0:1536]} | slice | bytes 6291456 | tf_op jit(solution)/shard_map/slice | solution.py:69
  47.5 6.3 %collective-permute-done.4 = bf16[2,64,1536]{2,1,0:T(8,128)(2,1)S(1)} collective-permute-done((bf16[2,64,1536]{2,1,0:T(8,128)(2,1)S(1)}, bf16[2,64,1536]{2,1,0:T(8,128)(2,1)S(1)}, u32[]{:S(2)}, u32[]{:S(2)}) %collective-permute-start.4) | collective-permute-done | bytes 393248 | tf_op jit(solution)/shard_map/ppermute | solution.py:55
  54.0 1.0 fusion.1
  55.0 0.4 fusion.4
  55.5 0.6 broadcast_in_dim.166
  56.1 5.2 %all-to-all-start.1 = ((f32[8,1,1024]{2,1,0:T(1,128)}), f32[8,1,1024]{2,1,0:T(1,128)S(1)}, u32[]{:S(2)}, u32[]{:S(2)}) async-start(f32[8,1,1024]{2,1,0:T(1,128)} %broadcast_in_dim.166), calls=%async_computation.1 | async-start | bytes 65536 | tf_op jit(solution)/shard_map/all_to_all | solution.py:24
  61.5 0.7 convert_reduce_fusion.1
  62.4 0.6 gather_fusion.2
  63.7 0.8 bitcast_dynamic-update-slice_fusion
  64.6 3.6 %all-to-all-done.1 = f32[8,1,1024]{2,1,0:T(1,128)S(1)} async-done(((f32[8,1,1024]{2,1,0:T(1,128)}), f32[8,1,1024]{2,1,0:T(1,128)S(1)}, u32[]{:S(2)}, u32[]{:S(2)}) %all-to-all-start.1) | async-done | bytes 32800 | tf_op jit(solution)/shard_map/all_to_all | solution.py:24
  68.4 14.3 %all_to_all.58 = f32[32,1,384]{2,1,0:T(1,128)S(1)} all-to-all(f32[32,1,384]{2,1,0:T(1,128)S(1)} %broadcast_in_dim.169), channel_id=1, replica_groups=mesh['y'=4,'xh'=2,'c'=2,'xl'=2,'z'=8] {'y','xh','c','xl'}, dimensions={0} | all-to-all | bytes 98304 | tf_op jit(solution)/shard_map/all_to_all | solution.py:24
  83.2 0.2 multiply_reduce_fusion.4
  83.4 9.2 %all_to_all.59 = f32[8,1,1024]{2,1,0:T(1,128)S(1)} all-to-all(f32[8,1,1024]{2,1,0:T(1,128)S(1)} %broadcast_in_dim.170), channel_id=1, replica_groups=mesh['y'=4,'xh'=2,'c'=2,'xl'=2,'z'=8] {'z'}, dimensions={0} | all-to-all | bytes 65536 | tf_op jit(solution)/shard_map/all_to_all | solution.py:24
  92.7 0.2 multiply_reduce_fusion.3
  92.8 12.0 %all_to_all.60 = f32[32,1,256]{2,1,0:T(1,128)S(1)} all-to-all(f32[32,1,256]{2,1,0:T(1,128)S(1)} %broadcast_in_dim.171), channel_id=1, replica_groups=mesh['y'=4,'xh'=2,'c'=2,'xl'=2,'z'=8] {'y','xh','c','xl'}, dimensions={0} | all-to-all | bytes 65536 | tf_op jit(solution)/shard_map/all_to_all | solution.py:24
  105.0 0.2 multiply_reduce_fusion.2
  105.2 9.3 %all_to_all.61 = f32[8,1,1024]{2,1,0:T(1,128)S(1)} all-to-all(f32[8,1,1024]{2,1,0:T(1,128)S(1)} %broadcast_in_dim.172), channel_id=1, replica_groups=mesh['y'=4,'xh'=2,'c'=2,'xl'=2,'z'=8] {'z'}, dimensions={0} | all-to-all | bytes 65536 | tf_op jit(solution)/shard_map/all_to_all | solution.py:24
  114.6 12.1 %all_to_all.62 = f32[32,1,256]{2,1,0:T(1,128)S(1)} all-to-all(f32[32,1,256]{2,1,0:T(1,128)S(1)} %broadcast_in_dim.173), channel_id=1, replica_groups=mesh['y'=4,'xh'=2,'c'=2,'xl'=2,'z'=8] {'y','xh','c','xl'}, dimensions={0} | all-to-all | bytes 65536 | tf_op jit(solution)/shard_map/all_to_all | solution.py:24
  126.9 0.2 multiply_reduce_fusion
  127.1 0.6 broadcast_in_dim.174
  127.7 3.3 %all-to-all-start.7 = ((f32[8,1,1024]{2,1,0:T(1,128)}), f32[8,1,1024]{2,1,0:T(1,128)S(1)}, u32[]{:S(2)}, u32[]{:S(2)}) async-start(f32[8,1,1024]{2,1,0:T(1,128)} %broadcast_in_dim.174), calls=%async_computation.7 | async-start | bytes 65536 | tf_op jit(solution)/shard_map/all_to_all | solution.py:24
  131.0 3.8 %slice.56 = bf16[8,128,1536]{2,1,0:T(8,128)(2,1)} slice(bf16[10,128,1536]{2,1,0:T(8,128)(2,1)} %bitcast_dynamic-update-slice_fusion), slice={[0:8], [0:128], [0:1536]} | slice | bytes 6291456 | tf_op jit(solution)/shard_map/slice | solution.py:90
  134.8 3.0 %all-to-all-done.7 = f32[8,1,1024]{2,1,0:T(1,128)S(1)} async-done(((f32[8,1,1024]{2,1,0:T(1,128)}), f32[8,1,1024]{2,1,0:T(1,128)S(1)}, u32[]{:S(2)}, u32[]{:S(2)}) %all-to-all-start.7) | async-done | bytes 32800 | tf_op jit(solution)/shard_map/all_to_all | solution.py:24
  138.1 0.3 fusion.9
  138.4 0.4 collective-permute-start.11
  138.8 1.0 copy-done
  139.8 0.6 fusion.36
  140.4 0.4 collective-permute-start.12
  140.9 0.6 fusion.35
  141.5 1.2 collective-permute-start.10
  142.7 2.7 %collective-permute-start.14 = (f32[2,64,128]{2,1,0:T(8,128)S(1)}, f32[2,64,128]{2,1,0:T(8,128)S(1)}, u32[]{:S(2)}, u32[]{:S(2)}) collective-permute-start(f32[2,64,128]{2,1,0:T(8,128)S(1)} %bitcast_add_fusion.2), channel_id=1, source_target_pairs={{0,16},{16,0},{1,17},{17,1},{2,18},{18,2},{3,19},{19,3},{4,20},{20... | collective-permute-start | bytes 196616 | tf_op jit(solution)/shard_map/ppermute | solution.py:119
  145.4 0.9 collective-permute-done.14
  146.5 3.8 %collective-permute-start.15 = (bf16[64,1536]{1,0:T(8,128)(2,1)S(1)}, bf16[64,1536]{1,0:T(8,128)(2,1)S(1)}, u32[]{:S(2)}, u32[]{:S(2)}) collective-permute-start(bf16[64,1536]{1,0:T(8,128)(2,1)S(1)} %fusion.5), channel_id=1, source_target_pairs={{0,16},{16,0},{1,17},{17,1},{2,18},{18,2},{3,19},{19,3},{4,20},{20... | collective-permute-start | bytes 589832 | tf_op jit(solution)/shard_map/ppermute | solution.py:138
  150.3 0.3 collective-permute-done.10
  150.7 2.2 %collective-permute-start.13 = (bf16[64,1536]{1,0:T(8,128)(2,1)S(1)}, bf16[64,1536]{1,0:T(8,128)(2,1)S(1)}, u32[]{:S(2)}, u32[]{:S(2)}) collective-permute-start(bf16[64,1536]{1,0:T(8,128)(2,1)S(1)} %fusion.6), channel_id=1, source_target_pairs={{0,16},{16,0},{1,17},{17,1},{2,18},{18,2},{3,19},{19,3},{4,20},{20... | collective-permute-start | bytes 589832 | tf_op jit(solution)/shard_map/ppermute | solution.py:138
  152.9 1.0 collective-permute-done.13
  153.9 0.5 select_add_fusion
  154.5 26.0 %all_to_all.63 = bf16[8,64,1664]{2,1,0:T(8,128)(2,1)S(1)} all-to-all(bf16[8,64,1664]{2,1,0:T(8,128)(2,1)S(1)} %select_add_fusion), channel_id=1, replica_groups=mesh['y'=4,'xh'=2,'c'=2,'xl'=2,'z'=8] {'y','xh'}, dimensions={0} | all-to-all | bytes 3407872 | tf_op jit(solution)/shard_map/all_to_all | solution.py:146
  180.5 0.2 convert_reduce_fusion
  180.8 0.9 slice_divide_fusion
  (108 shorter events, 2.7 us)
Async XLA Ops:
  0.0 20.7 %copy-start.1 = (bf16[128,1536]{1,0:T(8,128)(2,1)S(1)}, bf16[128,1536]{1,0:T(8,128)(2,1)}, u32[]{:S(2)}) copy-start(bf16[128,1536]{1,0:T(8,128)(2,1)} %param.17) | copy-start | bytes 1179652
  0.0 16.5 %copy-start.11 = (s32[1,2]{1,0:T(1,128)S(1)}, s32[1,2]{1,0:T(1,128)}, u32[]{:S(2)}) copy-start(s32[1,2]{1,0:T(1,128)} %param.20) | copy-start | bytes 28
  0.0 16.6 %copy-start.9 = (s32[1,2]{1,0:T(1,128)S(1)}, s32[1,2]{1,0:T(1,128)}, u32[]{:S(2)}) copy-start(s32[1,2]{1,0:T(1,128)} %param.19) | copy-start | bytes 28
  0.0 16.6 %collective-permute-start = (bf16[128,1536]{1,0:T(8,128)(2,1)}, bf16[128,1536]{1,0:T(8,128)(2,1)S(1)}, u32[]{:S(2)}, u32[]{:S(2)}) collective-permute-start(bf16[128,1536]{1,0:T(8,128)(2,1)} %param.17), channel_id=1, source_target_pairs={{0,1},{1,2},{2,3},{3,4},{4,5},{5,6},{6,7},{7,0},{8,9},{9,10},{10,1... | collective-permute-start | bytes 1179656 | tf_op jit(solution)/shard_map/ppermute | solution.py:37
  2.6 15.3 %collective-permute-start.5 = (bf16[128,1536]{1,0:T(8,128)(2,1)}, bf16[128,1536]{1,0:T(8,128)(2,1)S(1)}, u32[]{:S(2)}, u32[]{:S(2)}) collective-permute-start(bf16[128,1536]{1,0:T(8,128)(2,1)} %param.17), channel_id=1, source_target_pairs={{0,7},{1,0},{2,1},{3,2},{4,3},{5,4},{6,5},{7,6},{8,15},{9,8},{10,9... | collective-permute-start | bytes 1179656 | tf_op jit(solution)/shard_map/ppermute | solution.py:38
  8.8 28.3 %all-to-all-start = ((bf16[8,64,1536]{2,1,0:T(8,128)(2,1)}), bf16[8,64,1536]{2,1,0:T(8,128)(2,1)S(1)}, u32[]{:S(2)}, u32[]{:S(2)}) async-start(bf16[8,64,1536]{2,1,0:T(8,128)(2,1)} %broadcast_in_dim.90), calls=%async_computation | async-start | bytes 3145728 | tf_op jit(solution)/shard_map/all_to_all | solution.py:36
  16.6 7.9 %collective-permute-start.2 = (s32[2]{0:T(128)S(1)}, s32[2]{0:T(128)S(1)}, u32[]{:S(2)}, u32[]{:S(2)}) collective-permute-start(s32[2]{0:T(128)S(1)} %bitcast.129), channel_id=1, source_target_pairs={{0,16},{16,0},{1,17},{17,1},{2,18},{18,2},{3,19},{19,3},{4,20},{20... | collective-permute-start | bytes 32 | tf_op jit(solution)/shard_map/ppermute | solution.py:41
  17.9 11.9 %collective-permute-start.1 = (bf16[128,1536]{1,0:T(8,128)(2,1)S(1)}, bf16[128,1536]{1,0:T(8,128)(2,1)S(1)}, u32[]{:S(2)}, u32[]{:S(2)}) collective-permute-start(bf16[128,1536]{1,0:T(8,128)(2,1)S(1)} %collective-permute-done), channel_id=1, source_target_pairs={{0,1},{1,2},{2,3},{3,4},{4,5},{5,6},{6,7},{7,0},{8,9},{9,10},{10,1... | collective-permute-start | bytes 1179656 | tf_op jit(solution)/shard_map/ppermute | solution.py:42
  17.9 11.9 %collective-permute-start.6 = (bf16[128,1536]{1,0:T(8,128)(2,1)S(1)}, bf16[128,1536]{1,0:T(8,128)(2,1)S(1)}, u32[]{:S(2)}, u32[]{:S(2)}) collective-permute-start(bf16[128,1536]{1,0:T(8,128)(2,1)S(1)} %collective-permute-done.5), channel_id=1, source_target_pairs={{0,7},{1,0},{2,1},{3,2},{4,3},{5,4},{6,5},{7,6},{8,15},{9,8},{10,9... | collective-permute-start | bytes 1179656 | tf_op jit(solution)/shard_map/ppermute | solution.py:43
  24.5 8.0 %copy-start.12 = (s32[2]{0:T(128)}, s32[2]{0:T(128)S(1)}, u32[]{:S(2)}) copy-start(s32[2]{0:T(128)S(1)} %collective-permute-done.2) | copy-start | bytes 28
  29.7 14.0 %collective-permute-start.7 = (bf16[128,1536]{1,0:T(8,128)(2,1)S(1)}, bf16[128,1536]{1,0:T(8,128)(2,1)S(1)}, u32[]{:S(2)}, u32[]{:S(2)}) collective-permute-start(bf16[128,1536]{1,0:T(8,128)(2,1)S(1)} %collective-permute-done.1), channel_id=1, source_target_pairs={{0,1},{1,2},{2,3},{3,4},{4,5},{5,6},{6,7},{7,0},{8,9},{9,10},{10,1... | collective-permute-start | bytes 1179656 | tf_op jit(solution)/shard_map/ppermute | solution.py:46
  29.8 14.0 %collective-permute-start.8 = (bf16[128,1536]{1,0:T(8,128)(2,1)S(1)}, bf16[128,1536]{1,0:T(8,128)(2,1)S(1)}, u32[]{:S(2)}, u32[]{:S(2)}) collective-permute-start(bf16[128,1536]{1,0:T(8,128)(2,1)S(1)} %collective-permute-done.6), channel_id=1, source_target_pairs={{0,7},{1,0},{2,1},{3,2},{4,3},{5,4},{6,5},{7,6},{8,15},{9,8},{10,9... | collective-permute-start | bytes 1179656 | tf_op jit(solution)/shard_map/ppermute | solution.py:47
  38.4 3.9 %collective-permute-start.3 = (bf16[2,64,1536]{2,1,0:T(8,128)(2,1)}, bf16[2,64,1536]{2,1,0:T(8,128)(2,1)}, u32[]{:S(2)}, u32[]{:S(2)}) collective-permute-start(bf16[2,64,1536]{2,1,0:T(8,128)(2,1)} %gather_fusion.1), channel_id=1, source_target_pairs={{0,16},{16,0},{1,17},{17,1},{2,18},{18,2},{3,19},{19,3},{4,20},{20... | collective-permute-start | bytes 1179656 | tf_op jit(solution)/shard_map/ppermute | solution.py:52
  43.4 10.4 %collective-permute-start.4 = (bf16[2,64,1536]{2,1,0:T(8,128)(2,1)S(1)}, bf16[2,64,1536]{2,1,0:T(8,128)(2,1)S(1)}, u32[]{:S(2)}, u32[]{:S(2)}) collective-permute-start(bf16[2,64,1536]{2,1,0:T(8,128)(2,1)S(1)} %broadcast_select_fusion), channel_id=1, source_target_pairs={{0,8},{8,0},{1,9},{9,1},{2,10},{10,2},{3,11},{11,3},{4,12},{12,4},... | collective-permute-start | bytes 1179656 | tf_op jit(solution)/shard_map/ppermute | solution.py:55
  43.8 11.2 %collective-permute-start.9 = (bf16[128,1536]{1,0:T(8,128)(2,1)S(1)}, bf16[128,1536]{1,0:T(8,128)(2,1)S(1)}, u32[]{:S(2)}, u32[]{:S(2)}) collective-permute-start(bf16[128,1536]{1,0:T(8,128)(2,1)S(1)} %collective-permute-done.7), channel_id=1, source_target_pairs={{0,1},{1,2},{2,3},{3,4},{4,5},{5,6},{6,7},{7,0},{8,9},{9,10},{10,1... | collective-permute-start | bytes 1179656 | tf_op jit(solution)/shard_map/ppermute | solution.py:57
  53.9 7.4 %copy-start.10 = (s32[2]{0:T(128)S(1)}, s32[2]{0:T(128)}, u32[]{:S(2)}) copy-start(s32[2]{0:T(128)} %iota_multiply_fusion) | copy-start | bytes 28
  53.9 7.6 %copy-start.2 = (s32[16384]{0:T(1024)S(1)}, s32[16384]{0:T(1024)}, u32[]{:S(2)}) copy-start(s32[16384]{0:T(1024)} %param.21) | copy-start | bytes 196612
  54.0 8.3 %copy-start.13 = (s32[2]{0:T(128)S(1)}, s32[2]{0:T(128)}, u32[]{:S(2)}) copy-start(s32[2]{0:T(128)} %copy-done.12) | copy-start | bytes 28
  54.0 8.3 %copy-start.14 = (s32[8]{0:T(128)S(1)}, s32[8]{0:T(128)}, u32[]{:S(2)}) copy-start(s32[8]{0:T(128)} %multiply_add_fusion) | copy-start | bytes 100
  56.1 12.1 %all-to-all-start.1 = ((f32[8,1,1024]{2,1,0:T(1,128)}), f32[8,1,1024]{2,1,0:T(1,128)S(1)}, u32[]{:S(2)}, u32[]{:S(2)}) async-start(f32[8,1,1024]{2,1,0:T(1,128)} %broadcast_in_dim.166), calls=%async_computation.1 | async-start | bytes 65536 | tf_op jit(solution)/shard_map/all_to_all | solution.py:24
  127.7 10.1 %all-to-all-start.7 = ((f32[8,1,1024]{2,1,0:T(1,128)}), f32[8,1,1024]{2,1,0:T(1,128)S(1)}, u32[]{:S(2)}, u32[]{:S(2)}) async-start(f32[8,1,1024]{2,1,0:T(1,128)} %broadcast_in_dim.174), calls=%async_computation.7 | async-start | bytes 65536 | tf_op jit(solution)/shard_map/all_to_all | solution.py:24
  137.9 1.9 %copy-start = (bf16[8,128,1536]{2,1,0:T(8,128)(2,1)S(1)}, bf16[8,128,1536]{2,1,0:T(8,128)(2,1)}, u32[]{:S(2)}) copy-start(bf16[8,128,1536]{2,1,0:T(8,128)(2,1)} %slice.56) | copy-start | bytes 9437188
  138.4 4.3 %collective-permute-start.11 = (f32[2,64,128]{2,1,0:T(8,128)S(1)}, f32[2,64,128]{2,1,0:T(8,128)S(1)}, u32[]{:S(2)}, u32[]{:S(2)}) collective-permute-start(f32[2,64,128]{2,1,0:T(8,128)S(1)} %dynamic-slice_bitcast_fusion), channel_id=1, source_target_pairs={{0,8},{8,0},{1,9},{9,1},{2,10},{10,2},{3,11},{11,3},{4,12},{12,4},... | collective-permute-start | bytes 196616 | tf_op jit(solution)/shard_map/ppermute | solution.py:111
  140.4 6.0 %collective-permute-start.12 = (bf16[64,1536]{1,0:T(8,128)(2,1)S(1)}, bf16[64,1536]{1,0:T(8,128)(2,1)S(1)}, u32[]{:S(2)}, u32[]{:S(2)}) collective-permute-start(bf16[64,1536]{1,0:T(8,128)(2,1)S(1)} %fusion.8), channel_id=1, source_target_pairs={{0,8},{8,0},{1,9},{9,1},{2,10},{10,2},{3,11},{11,3},{4,12},{12,4},... | collective-permute-start | bytes 589832 | tf_op jit(solution)/shard_map/ppermute | solution.py:136
  140.8 4.6 %copy-start.6 = (f32[128]{0:T(128)S(1)}, f32[128]{0:T(128)}, u32[]{:S(2)}) copy-start(f32[128]{0:T(128)} %constant.183) | copy-start | bytes 1540
  140.8 4.6 %copy-start.7 = (f32[128]{0:T(128)S(1)}, f32[128]{0:T(128)}, u32[]{:S(2)}) copy-start(f32[128]{0:T(128)} %constant.182) | copy-start | bytes 1540
  140.8 4.6 %copy-start.8 = (f32[128]{0:T(128)S(1)}, f32[128]{0:T(128)}, u32[]{:S(2)}) copy-start(f32[128]{0:T(128)} %constant.181) | copy-start | bytes 1540
  140.8 5.5 %copy-start.3 = (f32[128]{0:T(128)S(1)}, f32[128]{0:T(128)}, u32[]{:S(2)}) copy-start(f32[128]{0:T(128)} %constant.186) | copy-start | bytes 1540
  140.8 5.5 %copy-start.4 = (f32[128]{0:T(128)S(1)}, f32[128]{0:T(128)}, u32[]{:S(2)}) copy-start(f32[128]{0:T(128)} %constant.185) | copy-start | bytes 1540
  140.8 5.4 %copy-start.5 = (f32[128]{0:T(128)S(1)}, f32[128]{0:T(128)}, u32[]{:S(2)}) copy-start(f32[128]{0:T(128)} %constant.184) | copy-start | bytes 1540
  141.5 9.1 %collective-permute-start.10 = (bf16[64,1536]{1,0:T(8,128)(2,1)S(1)}, bf16[64,1536]{1,0:T(8,128)(2,1)S(1)}, u32[]{:S(2)}, u32[]{:S(2)}) collective-permute-start(bf16[64,1536]{1,0:T(8,128)(2,1)S(1)} %fusion.7), channel_id=1, source_target_pairs={{0,8},{8,0},{1,9},{9,1},{2,10},{10,2},{3,11},{11,3},{4,12},{12,4},... | collective-permute-start | bytes 589832 | tf_op jit(solution)/shard_map/ppermute | solution.py:136
  142.7 3.6 %collective-permute-start.14 = (f32[2,64,128]{2,1,0:T(8,128)S(1)}, f32[2,64,128]{2,1,0:T(8,128)S(1)}, u32[]{:S(2)}, u32[]{:S(2)}) collective-permute-start(f32[2,64,128]{2,1,0:T(8,128)S(1)} %bitcast_add_fusion.2), channel_id=1, source_target_pairs={{0,16},{16,0},{1,17},{17,1},{2,18},{18,2},{3,19},{19,3},{4,20},{20... | collective-permute-start | bytes 196616 | tf_op jit(solution)/shard_map/ppermute | solution.py:119
  146.5 6.4 %collective-permute-start.15 = (bf16[64,1536]{1,0:T(8,128)(2,1)S(1)}, bf16[64,1536]{1,0:T(8,128)(2,1)S(1)}, u32[]{:S(2)}, u32[]{:S(2)}) collective-permute-start(bf16[64,1536]{1,0:T(8,128)(2,1)S(1)} %fusion.5), channel_id=1, source_target_pairs={{0,16},{16,0},{1,17},{17,1},{2,18},{18,2},{3,19},{19,3},{4,20},{20... | collective-permute-start | bytes 589832 | tf_op jit(solution)/shard_map/ppermute | solution.py:138
  150.7 3.2 %collective-permute-start.13 = (bf16[64,1536]{1,0:T(8,128)(2,1)S(1)}, bf16[64,1536]{1,0:T(8,128)(2,1)S(1)}, u32[]{:S(2)}, u32[]{:S(2)}) collective-permute-start(bf16[64,1536]{1,0:T(8,128)(2,1)S(1)} %fusion.6), channel_id=1, source_target_pairs={{0,16},{16,0},{1,17},{17,1},{2,18},{18,2},{3,19},{19,3},{4,20},{20... | collective-permute-start | bytes 589832 | tf_op jit(solution)/shard_map/ppermute | solution.py:138

commit v6 on v5

--- a/solution.py
+++ b/solution.py
@@ -126,17 +126,23 @@
         low = rest - middle
         return (high * at[:1] + middle * at[1:2] + low * at[2:]).astype(jnp.bfloat16)
 
-    parts = []
-    for k in (0, 1):
+    sides = []
+    for lo, hi in ((0, width // 2), (width // 2, width)):
         sums = lax.dot_general(
-            weights[128 * k : 128 * (k + 1)], pts, (((1,), (0,)), ((), ())), preferred_element_type=jnp.float32
-        ).reshape(2, 64, width)
-        mine = lax.dynamic_index_in_dim(sums, xl, 0, keepdims=False)
-        give = lax.dynamic_index_in_dim(sums, 1 - xl, 0, keepdims=False).astype(jnp.bfloat16)
+            weights, pts[:, lo:hi], (((1,), (0,)), ((), ())), preferred_element_type=jnp.float32
+        ).reshape(2, 2, 64, hi - lo)
+        mine = lax.dynamic_index_in_dim(sums, xl, 1, keepdims=False)
+        give = lax.dynamic_index_in_dim(sums, 1 - xl, 1, keepdims=False).astype(jnp.bfloat16)
         got = lax.ppermute(give, "xl", SWAP)
         sums = (mine + got.astype(jnp.float32)).astype(jnp.bfloat16)
-        pair = (sums, lax.ppermute(sums, "c", SWAP))
-        parts.append([jnp.concatenate([pair[i], in_thirds(tots[i][k], 4 * i)], axis=1) for i in (0, 1)])
+        sides.append((sums, lax.ppermute(sums, "c", SWAP)))
+    parts = [
+        [
+            jnp.concatenate([sides[0][i][k], sides[1][i][k], in_thirds(tots[i][k], 4 * i)], axis=1)
+            for i in (0, 1)
+        ]
+        for k in (0, 1)
+    ]
     zero = jnp.zeros((), jnp.bfloat16)
 
     def placed(first, second, a, b):

time: 182 us -> 184 us (1.011)
  transfers between devices with their start and end apart: 19 -> 19, of which waited for: 10 -> 9; matrix products, arithmetic and copies ran while one was open for 13% -> 13% of each run, Pallas kernels for 0% -> 0%
where the time goes in v6:
time: 184 us
  blocking collectives  83.6 us (45%)
  starting transfers between devices  42 us (23%)
  waiting for transfers between devices  25.3 us (14%)
  local copies, waits for them, and re-layouts  20.3 us (11%)
  other arithmetic  6.93 us (4%)
  matrix products  4.37 us (2%)
    all_to_all x5, blocking collectives, exchange(): lax.all_to_all(jnp.broadcast_to(row[None], (n,) + row.shape), axes, 0, 0)  57 us
    all_to_all x1, blocking collectives, shards(): landed = lax.all_to_all(spread, ('y', 'xh'), 0, 0)  26.6 us
    all_to_all x2, starting transfers between devices, exchange(): lax.all_to_all(jnp.broadcast_to(row[None], (n,) + row.shape), axes, 0, 0)  8.54 us
    all_to_all x1, starting transfers between devices, shards(): allc = lax.all_to_all(spread_cents, ('y', 'xh'), 0, 0)  6.65 us
    all_to_all x2, waiting for transfers between devices, exchange(): lax.all_to_all(jnp.broadcast_to(row[None], (n,) + row.shape), axes, 0, 0)  6.63 us
    ppermute x1, waiting for transfers between devices, shards(): kept_xl = lax.ppermute(kept, 'xl', SWAP)  6.3 us
    dynamic_update_slice x7, local copies, waits for them, and re-layouts, put(): return lax.dynamic_update_slice(buf, part[None], (at % NZ, 0, 0))  5.46 us
    ppermute x1, waiting for transfers between devices, shards(): up2 = lax.ppermute(up1, 'z', UP)  5.26 us
  transfers between devices with their start and end apart: 19, of which 9 were waited for; matrix products, arithmetic and copies ran while one was open for 13% of the time, Pallas kernels for 0%

profile of v6, /device:TPU:1, one launch (start us, length us, event | category | flops | bytes accessed | tf_op | source)
XLA Modules:
  0.0 183.7 jit_solution(1961267663434816084)
XLA Ops:
  0.0 2.5 %collective-permute-start = (bf16[128,1536]{1,0:T(8,128)(2,1)}, bf16[128,1536]{1,0:T(8,128)(2,1)S(1)}, u32[]{:S(2)}, u32[]{:S(2)}) collective-permute-start(bf16[128,1536]{1,0:T(8,128)(2,1)} %param.17), channel_id=1, source_target_pairs={{0,1},{1,2},{2,3},{3,4},{4,5},{5,6},{6,7},{7,0},{8,9},{9,10},{10,1... | collective-permute-start | bytes 1179656 | tf_op jit(solution)/shard_map/ppermute | solution.py:37
  2.6 4.0 %collective-permute-start.5 = (bf16[128,1536]{1,0:T(8,128)(2,1)}, bf16[128,1536]{1,0:T(8,128)(2,1)S(1)}, u32[]{:S(2)}, u32[]{:S(2)}) collective-permute-start(bf16[128,1536]{1,0:T(8,128)(2,1)} %param.17), channel_id=1, source_target_pairs={{0,7},{1,0},{2,1},{3,2},{4,3},{5,4},{6,5},{7,6},{8,15},{9,8},{10,9... | collective-permute-start | bytes 1179656 | tf_op jit(solution)/shard_map/ppermute | solution.py:38
  6.6 2.2 %broadcast_in_dim.90 = bf16[8,64,1536]{2,1,0:T(8,128)(2,1)} broadcast(bf16[64,1536]{1,0:T(8,128)(2,1)} %param.18), dimensions={1,2} | broadcast | bytes 1769472 | tf_op jit(solution)/shard_map/broadcast_in_dim | solution.py:35
  8.8 6.7 %all-to-all-start = ((bf16[8,64,1536]{2,1,0:T(8,128)(2,1)}), bf16[8,64,1536]{2,1,0:T(8,128)(2,1)S(1)}, u32[]{:S(2)}, u32[]{:S(2)}) async-start(bf16[8,64,1536]{2,1,0:T(8,128)(2,1)} %broadcast_in_dim.90), calls=%async_computation | async-start | bytes 3145728 | tf_op jit(solution)/shard_map/all_to_all | solution.py:36
  15.4 0.6 iota_multiply_fusion
  16.0 0.5 multiply_add_fusion
  16.6 1.3 collective-permute-start.2
  17.9 2.8 %collective-permute-start.6 = (bf16[128,1536]{1,0:T(8,128)(2,1)S(1)}, bf16[128,1536]{1,0:T(8,128)(2,1)S(1)}, u32[]{:S(2)}, u32[]{:S(2)}) collective-permute-start(bf16[128,1536]{1,0:T(8,128)(2,1)S(1)} %collective-permute-done.5), channel_id=1, source_target_pairs={{0,7},{1,0},{2,1},{3,2},{4,3},{5,4},{6,5},{7,6},{8,15},{9,8},{10,9... | collective-permute-start | bytes 1179656 | tf_op jit(solution)/shard_map/ppermute | solution.py:43
  20.7 2.2 %broadcast_in_dim.159 = bf16[10,128,1536]{2,1,0:T(8,128)(2,1)} broadcast(bf16[128,1536]{1,0:T(8,128)(2,1)S(1)} %copy-done.1), dimensions={1,2} | broadcast | bytes 4325376 | tf_op jit(solution)/shard_map/broadcast_in_dim | solution.py:44
  22.9 0.8 bitcast_dynamic-update-slice_fusion.6
  23.7 0.8 bitcast_dynamic-update-slice_fusion.5
  24.5 5.3 %collective-permute-done.1 = bf16[128,1536]{1,0:T(8,128)(2,1)S(1)} collective-permute-done((bf16[128,1536]{1,0:T(8,128)(2,1)S(1)}, bf16[128,1536]{1,0:T(8,128)(2,1)S(1)}, u32[]{:S(2)}, u32[]{:S(2)}) %collective-permute-start.1) | collective-permute-done | bytes 393248 | tf_op jit(solution)/shard_map/ppermute | solution.py:42
  29.8 2.7 %collective-permute-start.8 = (bf16[128,1536]{1,0:T(8,128)(2,1)S(1)}, bf16[128,1536]{1,0:T(8,128)(2,1)S(1)}, u32[]{:S(2)}, u32[]{:S(2)}) collective-permute-start(bf16[128,1536]{1,0:T(8,128)(2,1)S(1)} %collective-permute-done.6), channel_id=1, source_target_pairs={{0,7},{1,0},{2,1},{3,2},{4,3},{5,4},{6,5},{7,6},{8,15},{9,8},{10,9... | collective-permute-start | bytes 1179656 | tf_op jit(solution)/shard_map/ppermute | solution.py:47
  32.4 0.8 bitcast_dynamic-update-slice_fusion.4
  33.2 3.9 %all-to-all-done = bf16[8,64,1536]{2,1,0:T(8,128)(2,1)S(1)} async-done(((bf16[8,64,1536]{2,1,0:T(8,128)(2,1)}), bf16[8,64,1536]{2,1,0:T(8,128)(2,1)S(1)}, u32[]{:S(2)}, u32[]{:S(2)}) %all-to-all-start) | async-done | bytes 1572896 | tf_op jit(solution)/shard_map/all_to_all | solution.py:36
  37.1 1.3 gather_fusion.1
  38.4 2.2 %collective-permute-start.3 = (bf16[2,64,1536]{2,1,0:T(8,128)(2,1)}, bf16[2,64,1536]{2,1,0:T(8,128)(2,1)}, u32[]{:S(2)}, u32[]{:S(2)}) collective-permute-start(bf16[2,64,1536]{2,1,0:T(8,128)(2,1)} %gather_fusion.1), channel_id=1, source_target_pairs={{0,16},{16,0},{1,17},{17,1},{2,18},{18,2},{3,19},{19,3},{4,20},{20... | collective-permute-start | bytes 1179656 | tf_op jit(solution)/shard_map/ppermute | solution.py:52
  40.6 0.8 bitcast_dynamic-update-slice_fusion.3
  41.4 0.6 gather_fusion
  41.9 0.3 collective-permute-done.3
  42.3 1.1 broadcast_select_fusion
  43.4 0.4 collective-permute-start.4
  43.8 0.8 bitcast_dynamic-update-slice_fusion.2
  44.6 0.8 bitcast_dynamic-update-slice_fusion.1
  45.4 2.1 %slice.102 = bf16[8,128,1536]{2,1,0:T(8,128)(2,1)S(1)} slice(bf16[10,128,1536]{2,1,0:T(8,128)(2,1)} %bitcast_dynamic-update-slice_fusion.1), slice={[0:8], [0:128], [0:1536]} | slice | bytes 6291456 | tf_op jit(solution)/shard_map/slice | solution.py:69
  47.5 6.3 %collective-permute-done.4 = bf16[2,64,1536]{2,1,0:T(8,128)(2,1)S(1)} collective-permute-done((bf16[2,64,1536]{2,1,0:T(8,128)(2,1)S(1)}, bf16[2,64,1536]{2,1,0:T(8,128)(2,1)S(1)}, u32[]{:S(2)}, u32[]{:S(2)}) %collective-permute-start.4) | collective-permute-done | bytes 393248 | tf_op jit(solution)/shard_map/ppermute | solution.py:55
  54.0 1.0 fusion.5
  55.0 0.4 fusion.8
  55.5 0.6 broadcast_in_dim.166
  56.1 5.2 %all-to-all-start.1 = ((f32[8,1,1024]{2,1,0:T(1,128)}), f32[8,1,1024]{2,1,0:T(1,128)S(1)}, u32[]{:S(2)}, u32[]{:S(2)}) async-start(f32[8,1,1024]{2,1,0:T(1,128)} %broadcast_in_dim.166), calls=%async_computation.1 | async-start | bytes 65536 | tf_op jit(solution)/shard_map/all_to_all | solution.py:24
  61.5 0.7 convert_reduce_fusion.1
  62.4 0.6 gather_fusion.2
  63.7 0.8 bitcast_dynamic-update-slice_fusion
  64.6 3.6 %all-to-all-done.1 = f32[8,1,1024]{2,1,0:T(1,128)S(1)} async-done(((f32[8,1,1024]{2,1,0:T(1,128)}), f32[8,1,1024]{2,1,0:T(1,128)S(1)}, u32[]{:S(2)}, u32[]{:S(2)}) %all-to-all-start.1) | async-done | bytes 32800 | tf_op jit(solution)/shard_map/all_to_all | solution.py:24
  68.2 0.2 multiply_reduce_fusion.5
  68.4 14.3 %all_to_all.58 = f32[32,1,384]{2,1,0:T(1,128)S(1)} all-to-all(f32[32,1,384]{2,1,0:T(1,128)S(1)} %broadcast_in_dim.169), channel_id=1, replica_groups=mesh['y'=4,'xh'=2,'c'=2,'xl'=2,'z'=8] {'y','xh','c','xl'}, dimensions={0} | all-to-all | bytes 98304 | tf_op jit(solution)/shard_map/all_to_all | solution.py:24
  83.2 0.2 multiply_reduce_fusion.4
  83.4 9.2 %all_to_all.59 = f32[8,1,1024]{2,1,0:T(1,128)S(1)} all-to-all(f32[8,1,1024]{2,1,0:T(1,128)S(1)} %broadcast_in_dim.170), channel_id=1, replica_groups=mesh['y'=4,'xh'=2,'c'=2,'xl'=2,'z'=8] {'z'}, dimensions={0} | all-to-all | bytes 65536 | tf_op jit(solution)/shard_map/all_to_all | solution.py:24
  92.7 0.2 multiply_reduce_fusion.3
  92.8 12.0 %all_to_all.60 = f32[32,1,256]{2,1,0:T(1,128)S(1)} all-to-all(f32[32,1,256]{2,1,0:T(1,128)S(1)} %broadcast_in_dim.171), channel_id=1, replica_groups=mesh['y'=4,'xh'=2,'c'=2,'xl'=2,'z'=8] {'y','xh','c','xl'}, dimensions={0} | all-to-all | bytes 65536 | tf_op jit(solution)/shard_map/all_to_all | solution.py:24
  105.0 0.2 multiply_reduce_fusion.2
  105.2 9.3 %all_to_all.61 = f32[8,1,1024]{2,1,0:T(1,128)S(1)} all-to-all(f32[8,1,1024]{2,1,0:T(1,128)S(1)} %broadcast_in_dim.172), channel_id=1, replica_groups=mesh['y'=4,'xh'=2,'c'=2,'xl'=2,'z'=8] {'z'}, dimensions={0} | all-to-all | bytes 65536 | tf_op jit(solution)/shard_map/all_to_all | solution.py:24
  114.6 12.1 %all_to_all.62 = f32[32,1,256]{2,1,0:T(1,128)S(1)} all-to-all(f32[32,1,256]{2,1,0:T(1,128)S(1)} %broadcast_in_dim.173), channel_id=1, replica_groups=mesh['y'=4,'xh'=2,'c'=2,'xl'=2,'z'=8] {'y','xh','c','xl'}, dimensions={0} | all-to-all | bytes 65536 | tf_op jit(solution)/shard_map/all_to_all | solution.py:24
  126.9 0.2 multiply_reduce_fusion
  127.1 0.6 broadcast_in_dim.174
  127.7 3.3 %all-to-all-start.7 = ((f32[8,1,1024]{2,1,0:T(1,128)}), f32[8,1,1024]{2,1,0:T(1,128)S(1)}, u32[]{:S(2)}, u32[]{:S(2)}) async-start(f32[8,1,1024]{2,1,0:T(1,128)} %broadcast_in_dim.174), calls=%async_computation.7 | async-start | bytes 65536 | tf_op jit(solution)/shard_map/all_to_all | solution.py:24
  131.0 3.8 %slice.79 = bf16[8,128,1536]{2,1,0:T(8,128)(2,1)} slice(bf16[10,128,1536]{2,1,0:T(8,128)(2,1)} %bitcast_dynamic-update-slice_fusion), slice={[0:8], [0:128], [0:1536]} | slice | bytes 6291456 | tf_op jit(solution)/shard_map/slice | solution.py:90
  134.8 3.0 %all-to-all-done.7 = f32[8,1,1024]{2,1,0:T(1,128)S(1)} async-done(((f32[8,1,1024]{2,1,0:T(1,128)}), f32[8,1,1024]{2,1,0:T(1,128)S(1)}, u32[]{:S(2)}, u32[]{:S(2)}) %all-to-all-start.7) | async-done | bytes 32800 | tf_op jit(solution)/shard_map/all_to_all | solution.py:24
  138.0 2.1 %fusion = f32[256,768]{1,0:T(8,128)S(1)} fusion(bf16[256,1024]{1,0:T(8,128)(2,1)S(1)} %multiply_convert_fusion, bf16[1024,1536]{1,0:T(8,128)(2,1)} %bitcast.130), kind=kOutput, calls=%fused_computation.5 | convolution fusion | flops 402653184 | bytes 2883584 | tf_op jit(solution)/shard_map/dot_general | solution.py:131
  140.3 0.6 fusion.2
  140.8 0.3 fusion.13
  141.1 0.4 collective-permute-start.12
  141.6 1.2 collective-permute-start.11
  142.8 0.5 collective-permute-start.10
  143.3 1.1 collective-permute-done.12
  144.4 3.9 %collective-permute-start.15 = (f32[2,64,128]{2,1,0:T(8,128)S(1)}, f32[2,64,128]{2,1,0:T(8,128)S(1)}, u32[]{:S(2)}, u32[]{:S(2)}) collective-permute-start(f32[2,64,128]{2,1,0:T(8,128)S(1)} %bitcast_add_fusion.2), channel_id=1, source_target_pairs={{0,16},{16,0},{1,17},{17,1},{2,18},{18,2},{3,19},{19,3},{4,20},{20... | collective-permute-start | bytes 196616 | tf_op jit(solution)/shard_map/ppermute | solution.py:119
  148.3 0.9 collective-permute-done.15
  149.2 3.0 %collective-permute-start.14 = (bf16[2,64,768]{2,1,0:T(8,128)(2,1)S(1)}, bf16[2,64,768]{2,1,0:T(8,128)(2,1)S(1)}, u32[]{:S(2)}, u32[]{:S(2)}) collective-permute-start(bf16[2,64,768]{2,1,0:T(8,128)(2,1)S(1)} %fusion.9), channel_id=1, source_target_pairs={{0,16},{16,0},{1,17},{17,1},{2,18},{18,2},{3,19},{19,3},{4,20},{20... | collective-permute-start | bytes 589832 | tf_op jit(solution)/shard_map/ppermute | solution.py:138
  152.3 2.0 %collective-permute-start.13 = (bf16[2,64,768]{2,1,0:T(8,128)(2,1)S(1)}, bf16[2,64,768]{2,1,0:T(8,128)(2,1)S(1)}, u32[]{:S(2)}, u32[]{:S(2)}) collective-permute-start(bf16[2,64,768]{2,1,0:T(8,128)(2,1)S(1)} %fusion.10), channel_id=1, source_target_pairs={{0,16},{16,0},{1,17},{17,1},{2,18},{18,2},{3,19},{19,3},{4,20},{20... | collective-permute-start | bytes 589832 | tf_op jit(solution)/shard_map/ppermute | solution.py:138
  154.4 1.0 collective-permute-done.13
  155.4 0.5 select_add_fusion
  156.0 26.6 %all_to_all.63 = bf16[8,64,1664]{2,1,0:T(8,128)(2,1)S(1)} all-to-all(bf16[8,64,1664]{2,1,0:T(8,128)(2,1)S(1)} %select_add_fusion), channel_id=1, replica_groups=mesh['y'=4,'xh'=2,'c'=2,'xl'=2,'z'=8] {'y','xh'}, dimensions={0} | all-to-all | bytes 3407872 | tf_op jit(solution)/shard_map/all_to_all | solution.py:152
  182.5 0.2 convert_reduce_fusion
  182.9 0.9 slice_divide_fusion
  (109 shorter events, 2.6 us)
Async XLA Ops:
  0.0 20.7 %copy-start.1 = (bf16[128,1536]{1,0:T(8,128)(2,1)S(1)}, bf16[128,1536]{1,0:T(8,128)(2,1)}, u32[]{:S(2)}) copy-start(bf16[128,1536]{1,0:T(8,128)(2,1)} %param.17) | copy-start | bytes 1179652
  0.0 16.5 %copy-start.11 = (s32[1,2]{1,0:T(1,128)S(1)}, s32[1,2]{1,0:T(1,128)}, u32[]{:S(2)}) copy-start(s32[1,2]{1,0:T(1,128)} %param.20) | copy-start | bytes 28
  0.0 16.6 %copy-start.9 = (s32[1,2]{1,0:T(1,128)S(1)}, s32[1,2]{1,0:T(1,128)}, u32[]{:S(2)}) copy-start(s32[1,2]{1,0:T(1,128)} %param.19) | copy-start | bytes 28
  0.0 16.6 %collective-permute-start = (bf16[128,1536]{1,0:T(8,128)(2,1)}, bf16[128,1536]{1,0:T(8,128)(2,1)S(1)}, u32[]{:S(2)}, u32[]{:S(2)}) collective-permute-start(bf16[128,1536]{1,0:T(8,128)(2,1)} %param.17), channel_id=1, source_target_pairs={{0,1},{1,2},{2,3},{3,4},{4,5},{5,6},{6,7},{7,0},{8,9},{9,10},{10,1... | collective-permute-start | bytes 1179656 | tf_op jit(solution)/shard_map/ppermute | solution.py:37
  2.6 15.3 %collective-permute-start.5 = (bf16[128,1536]{1,0:T(8,128)(2,1)}, bf16[128,1536]{1,0:T(8,128)(2,1)S(1)}, u32[]{:S(2)}, u32[]{:S(2)}) collective-permute-start(bf16[128,1536]{1,0:T(8,128)(2,1)} %param.17), channel_id=1, source_target_pairs={{0,7},{1,0},{2,1},{3,2},{4,3},{5,4},{6,5},{7,6},{8,15},{9,8},{10,9... | collective-permute-start | bytes 1179656 | tf_op jit(solution)/shard_map/ppermute | solution.py:38
  8.8 28.3 %all-to-all-start = ((bf16[8,64,1536]{2,1,0:T(8,128)(2,1)}), bf16[8,64,1536]{2,1,0:T(8,128)(2,1)S(1)}, u32[]{:S(2)}, u32[]{:S(2)}) async-start(bf16[8,64,1536]{2,1,0:T(8,128)(2,1)} %broadcast_in_dim.90), calls=%async_computation | async-start | bytes 3145728 | tf_op jit(solution)/shard_map/all_to_all | solution.py:36
  16.6 7.9 %collective-permute-start.2 = (s32[2]{0:T(128)S(1)}, s32[2]{0:T(128)S(1)}, u32[]{:S(2)}, u32[]{:S(2)}) collective-permute-start(s32[2]{0:T(128)S(1)} %bitcast.147), channel_id=1, source_target_pairs={{0,16},{16,0},{1,17},{17,1},{2,18},{18,2},{3,19},{19,3},{4,20},{20... | collective-permute-start | bytes 32 | tf_op jit(solution)/shard_map/ppermute | solution.py:41
  17.9 11.9 %collective-permute-start.1 = (bf16[128,1536]{1,0:T(8,128)(2,1)S(1)}, bf16[128,1536]{1,0:T(8,128)(2,1)S(1)}, u32[]{:S(2)}, u32[]{:S(2)}) collective-permute-start(bf16[128,1536]{1,0:T(8,128)(2,1)S(1)} %collective-permute-done), channel_id=1, source_target_pairs={{0,1},{1,2},{2,3},{3,4},{4,5},{5,6},{6,7},{7,0},{8,9},{9,10},{10,1... | collective-permute-start | bytes 1179656 | tf_op jit(solution)/shard_map/ppermute | solution.py:42
  17.9 11.9 %collective-permute-start.6 = (bf16[128,1536]{1,0:T(8,128)(2,1)S(1)}, bf16[128,1536]{1,0:T(8,128)(2,1)S(1)}, u32[]{:S(2)}, u32[]{:S(2)}) collective-permute-start(bf16[128,1536]{1,0:T(8,128)(2,1)S(1)} %collective-permute-done.5), channel_id=1, source_target_pairs={{0,7},{1,0},{2,1},{3,2},{4,3},{5,4},{6,5},{7,6},{8,15},{9,8},{10,9... | collective-permute-start | bytes 1179656 | tf_op jit(solution)/shard_map/ppermute | solution.py:43
  24.5 8.0 %copy-start.12 = (s32[2]{0:T(128)}, s32[2]{0:T(128)S(1)}, u32[]{:S(2)}) copy-start(s32[2]{0:T(128)S(1)} %collective-permute-done.2) | copy-start | bytes 28
  29.7 14.0 %collective-permute-start.7 = (bf16[128,1536]{1,0:T(8,128)(2,1)S(1)}, bf16[128,1536]{1,0:T(8,128)(2,1)S(1)}, u32[]{:S(2)}, u32[]{:S(2)}) collective-permute-start(bf16[128,1536]{1,0:T(8,128)(2,1)S(1)} %collective-permute-done.1), channel_id=1, source_target_pairs={{0,1},{1,2},{2,3},{3,4},{4,5},{5,6},{6,7},{7,0},{8,9},{9,10},{10,1... | collective-permute-start | bytes 1179656 | tf_op jit(solution)/shard_map/ppermute | solution.py:46
  29.8 14.0 %collective-permute-start.8 = (bf16[128,1536]{1,0:T(8,128)(2,1)S(1)}, bf16[128,1536]{1,0:T(8,128)(2,1)S(1)}, u32[]{:S(2)}, u32[]{:S(2)}) collective-permute-start(bf16[128,1536]{1,0:T(8,128)(2,1)S(1)} %collective-permute-done.6), channel_id=1, source_target_pairs={{0,7},{1,0},{2,1},{3,2},{4,3},{5,4},{6,5},{7,6},{8,15},{9,8},{10,9... | collective-permute-start | bytes 1179656 | tf_op jit(solution)/shard_map/ppermute | solution.py:47
  38.4 3.9 %collective-permute-start.3 = (bf16[2,64,1536]{2,1,0:T(8,128)(2,1)}, bf16[2,64,1536]{2,1,0:T(8,128)(2,1)}, u32[]{:S(2)}, u32[]{:S(2)}) collective-permute-start(bf16[2,64,1536]{2,1,0:T(8,128)(2,1)} %gather_fusion.1), channel_id=1, source_target_pairs={{0,16},{16,0},{1,17},{17,1},{2,18},{18,2},{3,19},{19,3},{4,20},{20... | collective-permute-start | bytes 1179656 | tf_op jit(solution)/shard_map/ppermute | solution.py:52
  43.4 10.4 %collective-permute-start.4 = (bf16[2,64,1536]{2,1,0:T(8,128)(2,1)S(1)}, bf16[2,64,1536]{2,1,0:T(8,128)(2,1)S(1)}, u32[]{:S(2)}, u32[]{:S(2)}) collective-permute-start(bf16[2,64,1536]{2,1,0:T(8,128)(2,1)S(1)} %broadcast_select_fusion), channel_id=1, source_target_pairs={{0,8},{8,0},{1,9},{9,1},{2,10},{10,2},{3,11},{11,3},{4,12},{12,4},... | collective-permute-start | bytes 1179656 | tf_op jit(solution)/shard_map/ppermute | solution.py:55
  43.8 11.2 %collective-permute-start.9 = (bf16[128,1536]{1,0:T(8,128)(2,1)S(1)}, bf16[128,1536]{1,0:T(8,128)(2,1)S(1)}, u32[]{:S(2)}, u32[]{:S(2)}) collective-permute-start(bf16[128,1536]{1,0:T(8,128)(2,1)S(1)} %collective-permute-done.7), channel_id=1, source_target_pairs={{0,1},{1,2},{2,3},{3,4},{4,5},{5,6},{6,7},{7,0},{8,9},{9,10},{10,1... | collective-permute-start | bytes 1179656 | tf_op jit(solution)/shard_map/ppermute | solution.py:57
  53.9 7.4 %copy-start.10 = (s32[2]{0:T(128)S(1)}, s32[2]{0:T(128)}, u32[]{:S(2)}) copy-start(s32[2]{0:T(128)} %iota_multiply_fusion) | copy-start | bytes 28
  53.9 7.6 %copy-start.2 = (s32[16384]{0:T(1024)S(1)}, s32[16384]{0:T(1024)}, u32[]{:S(2)}) copy-start(s32[16384]{0:T(1024)} %param.21) | copy-start | bytes 196612
  54.0 8.3 %copy-start.13 = (s32[2]{0:T(128)S(1)}, s32[2]{0:T(128)}, u32[]{:S(2)}) copy-start(s32[2]{0:T(128)} %copy-done.12) | copy-start | bytes 28
  54.0 8.3 %copy-start.14 = (s32[8]{0:T(128)S(1)}, s32[8]{0:T(128)}, u32[]{:S(2)}) copy-start(s32[8]{0:T(128)} %multiply_add_fusion) | copy-start | bytes 100
  56.1 12.1 %all-to-all-start.1 = ((f32[8,1,1024]{2,1,0:T(1,128)}), f32[8,1,1024]{2,1,0:T(1,128)S(1)}, u32[]{:S(2)}, u32[]{:S(2)}) async-start(f32[8,1,1024]{2,1,0:T(1,128)} %broadcast_in_dim.166), calls=%async_computation.1 | async-start | bytes 65536 | tf_op jit(solution)/shard_map/all_to_all | solution.py:24
  127.7 10.1 %all-to-all-start.7 = ((f32[8,1,1024]{2,1,0:T(1,128)}), f32[8,1,1024]{2,1,0:T(1,128)S(1)}, u32[]{:S(2)}, u32[]{:S(2)}) async-start(f32[8,1,1024]{2,1,0:T(1,128)} %broadcast_in_dim.174), calls=%async_computation.7 | async-start | bytes 65536 | tf_op jit(solution)/shard_map/all_to_all | solution.py:24
  137.9 2.4 %copy-start = (bf16[8,128,1536]{2,1,0:T(8,128)(2,1)S(1)}, bf16[8,128,1536]{2,1,0:T(8,128)(2,1)}, u32[]{:S(2)}) copy-start(bf16[8,128,1536]{2,1,0:T(8,128)(2,1)} %slice.79) | copy-start | bytes 9437188
  140.2 8.0 %copy-start.6 = (f32[128]{0:T(128)S(1)}, f32[128]{0:T(128)}, u32[]{:S(2)}) copy-start(f32[128]{0:T(128)} %constant.183) | copy-start | bytes 1540
  140.2 8.0 %copy-start.7 = (f32[128]{0:T(128)S(1)}, f32[128]{0:T(128)}, u32[]{:S(2)}) copy-start(f32[128]{0:T(128)} %constant.182) | copy-start | bytes 1540
  140.2 8.0 %copy-start.8 = (f32[128]{0:T(128)S(1)}, f32[128]{0:T(128)}, u32[]{:S(2)}) copy-start(f32[128]{0:T(128)} %constant.181) | copy-start | bytes 1540
  140.2 8.9 %copy-start.3 = (f32[128]{0:T(128)S(1)}, f32[128]{0:T(128)}, u32[]{:S(2)}) copy-start(f32[128]{0:T(128)} %constant.186) | copy-start | bytes 1540
  140.2 8.9 %copy-start.4 = (f32[128]{0:T(128)S(1)}, f32[128]{0:T(128)}, u32[]{:S(2)}) copy-start(f32[128]{0:T(128)} %constant.185) | copy-start | bytes 1540
  140.3 8.9 %copy-start.5 = (f32[128]{0:T(128)S(1)}, f32[128]{0:T(128)}, u32[]{:S(2)}) copy-start(f32[128]{0:T(128)} %constant.184) | copy-start | bytes 1540
  141.1 3.2 %collective-permute-start.12 = (f32[2,64,128]{2,1,0:T(8,128)S(1)}, f32[2,64,128]{2,1,0:T(8,128)S(1)}, u32[]{:S(2)}, u32[]{:S(2)}) collective-permute-start(f32[2,64,128]{2,1,0:T(8,128)S(1)} %dynamic-slice_bitcast_fusion), channel_id=1, source_target_pairs={{0,8},{8,0},{1,9},{9,1},{2,10},{10,2},{3,11},{11,3},{4,12},{12,4},... | collective-permute-start | bytes 196616 | tf_op jit(solution)/shard_map/ppermute | solution.py:111
  141.6 7.6 %collective-permute-start.11 = (bf16[2,64,768]{2,1,0:T(8,128)(2,1)S(1)}, bf16[2,64,768]{2,1,0:T(8,128)(2,1)S(1)}, u32[]{:S(2)}, u32[]{:S(2)}) collective-permute-start(bf16[2,64,768]{2,1,0:T(8,128)(2,1)S(1)} %fusion.12), channel_id=1, source_target_pairs={{0,8},{8,0},{1,9},{9,1},{2,10},{10,2},{3,11},{11,3},{4,12},{12,4},... | collective-permute-start | bytes 589832 | tf_op jit(solution)/shard_map/ppermute | solution.py:136
  142.8 9.4 %collective-permute-start.10 = (bf16[2,64,768]{2,1,0:T(8,128)(2,1)S(1)}, bf16[2,64,768]{2,1,0:T(8,128)(2,1)S(1)}, u32[]{:S(2)}, u32[]{:S(2)}) collective-permute-start(bf16[2,64,768]{2,1,0:T(8,128)(2,1)S(1)} %fusion.11), channel_id=1, source_target_pairs={{0,8},{8,0},{1,9},{9,1},{2,10},{10,2},{3,11},{11,3},{4,12},{12,4},... | collective-permute-start | bytes 589832 | tf_op jit(solution)/shard_map/ppermute | solution.py:136
  144.4 4.8 %collective-permute-start.15 = (f32[2,64,128]{2,1,0:T(8,128)S(1)}, f32[2,64,128]{2,1,0:T(8,128)S(1)}, u32[]{:S(2)}, u32[]{:S(2)}) collective-permute-start(f32[2,64,128]{2,1,0:T(8,128)S(1)} %bitcast_add_fusion.2), channel_id=1, source_target_pairs={{0,16},{16,0},{1,17},{17,1},{2,18},{18,2},{3,19},{19,3},{4,20},{20... | collective-permute-start | bytes 196616 | tf_op jit(solution)/shard_map/ppermute | solution.py:119
  149.2 5.1 %collective-permute-start.14 = (bf16[2,64,768]{2,1,0:T(8,128)(2,1)S(1)}, bf16[2,64,768]{2,1,0:T(8,128)(2,1)S(1)}, u32[]{:S(2)}, u32[]{:S(2)}) collective-permute-start(bf16[2,64,768]{2,1,0:T(8,128)(2,1)S(1)} %fusion.9), channel_id=1, source_target_pairs={{0,16},{16,0},{1,17},{17,1},{2,18},{18,2},{3,19},{19,3},{4,20},{20... | collective-permute-start | bytes 589832 | tf_op jit(solution)/shard_map/ppermute | solution.py:138
  152.3 3.1 %collective-permute-start.13 = (bf16[2,64,768]{2,1,0:T(8,128)(2,1)S(1)}, bf16[2,64,768]{2,1,0:T(8,128)(2,1)S(1)}, u32[]{:S(2)}, u32[]{:S(2)}) collective-permute-start(bf16[2,64,768]{2,1,0:T(8,128)(2,1)S(1)} %fusion.10), channel_id=1, source_target_pairs={{0,16},{16,0},{1,17},{17,1},{2,18},{18,2},{3,19},{19,3},{4,20},{20... | collective-permute-start | bytes 589832 | tf_op jit(solution)/shard_map/ppermute | solution.py:138

commit v7 on v5

--- a/solution.py
+++ b/solution.py
@@ -68,14 +68,11 @@
 
     kt = kernel_of(pts[:NZ].reshape(NZ * rows, width))
     kt = lax.dynamic_update_slice(kt, kernel_of(far), (0, ((z + 4) % NZ) * rows))
-    pts = put(pts, far, z + 4)
 
     def totals_of(match, got):
         return jnp.sum(match[..., None] * got[:, :256].reshape(1, -1, 2, 128), axis=(1, 2))
 
-    rowpart = jnp.sum(kt, axis=0)
-    rowpart, sizes, slots, slots_other = after((rowpart, sizes, slots, slots_other))
-    got = exchange(rowpart, "z", NZ)
+    sizes, slots, slots_other, _ = after((sizes, slots, slots_other, kept))
     ids = jnp.pad(slots.astype(jnp.float32), (0, 126))
     per_row = NB * 8
     pick = (8 * slots[:, None] + 4 * jnp.arange(2, dtype=jnp.int32)[None, :] + z // 2).reshape(4)
@@ -86,12 +83,17 @@
     grid = lax.broadcasted_iota(jnp.int32, (4, NY * NXH), 1) * NC + c
     hits = jnp.concatenate([slots, slots_other])[:, None] == grid
     hits = [hits[i] for i in range(4)]
-    got, ids, target_pair, hits, slots, pts = after((got, ids, target_pair, hits, slots, pts))
-    pts = pts[:NZ].reshape(NZ * rows, width)
+    kt, ids, target_pair, hits, slots = after((kt, ids, target_pair, hits, slots))
 
+    scale_v = jnp.ones((256,), jnp.float32)
     for step in range(ITERS):
-        if step > 0:
-            got = exchange(jnp.sum(kt * scale_v[:, None], axis=0), "z", NZ)
+        rowpart = jnp.sum(kt if step == 0 else kt * scale_v[:, None], axis=0)
+        if step == ITERS - 1:
+            rowpart, pts, far = after((rowpart, pts, far))
+        got = exchange(rowpart, "z", NZ)
+        if step == ITERS - 1:
+            pts = put(pts, far, z + 4)[:NZ].reshape(NZ * rows, width)
+            got, pts = after((got, pts))
         scale_u = 1.0 / jnp.sum(got, axis=0)
         if step < ITERS - 1:
             colpart = jnp.sum(kt * scale_u[None, :], axis=1)
@@ -128,8 +130,11 @@
 
     parts = []
     for k in (0, 1):
+        part = weights[128 * k : 128 * (k + 1)]
+        if k == 1:
+            part, _ = after((part, give))
         sums = lax.dot_general(
-            weights[128 * k : 128 * (k + 1)], pts, (((1,), (0,)), ((), ())), preferred_element_type=jnp.float32
+            part, pts, (((1,), (0,)), ((), ())), preferred_element_type=jnp.float32
         ).reshape(2, 64, width)
         mine = lax.dynamic_index_in_dim(sums, xl, 0, keepdims=False)
         give = lax.dynamic_index_in_dim(sums, 1 - xl, 0, keepdims=False).astype(jnp.bfloat16)

time: 182 us -> 184 us (1.011)
  starting transfers between devices: 41.8 us -> 39.6 us
  matrix products: 2.85 us -> 4.87 us
    ppermute x2, starting transfers between devices: 6.01 us -> 1.05 us  [shards(): pair = (sums, lax.ppermute(sums, 'c', SWAP))]
    ppermute x1, waiting for transfers between devices: 6.3 us -> 2.2 us  [shards(): kept_xl = lax.ppermute(kept, 'xl', SWAP)]
    ppermute x1, waiting for transfers between devices: 0.01 us -> 2.96 us  [halved(): return (mine, lax.ppermute(give, axis_name, SWAP))]
    all_to_all x2, waiting for transfers between devices: 6.63 us -> 9.32 us  [exchange(): lax.all_to_all(jnp.broadcast_to(row[None], (n,) + row.shape), axes, 0, 0)]
    ppermute x1, starting transfers between devices: 2.66 us -> 5.01 us  [shards(): tots = (tots, lax.ppermute(tots, 'c', SWAP))]
    dot_general x2, matrix products: 1.16 us -> 3.2 us  [shards(): lax.dot_general(part, pts, (((1,), (0,)), ((), ())), preferred_element_ty...]
  transfers between devices with their start and end apart: 19 -> 19, of which waited for: 10 -> 10; matrix products, arithmetic and copies ran while one was open for 13% -> 14% of each run, Pallas kernels for 0% -> 0%
where the time goes in v7:
time: 184 us; the launch traced here: 183 us
  blocking collectives  82.7 us (45%)
  starting transfers between devices  39.6 us (22%)
  waiting for transfers between devices  26.4 us (14%)
  local copies, waits for them, and re-layouts  21.9 us (12%)
  other arithmetic  6.34 us (3%)
  matrix products  4.87 us (3%)
    all_to_all x5, blocking collectives, exchange(): lax.all_to_all(jnp.broadcast_to(row[None], (n,) + row.shape), axes, 0, 0)  56.7 us
    all_to_all x1, blocking collectives, shards(): landed = lax.all_to_all(spread, ('y', 'xh'), 0, 0)  26 us
    all_to_all x2, waiting for transfers between devices, exchange(): lax.all_to_all(jnp.broadcast_to(row[None], (n,) + row.shape), axes, 0, 0)  9.32 us
    all_to_all x2, starting transfers between devices, exchange(): lax.all_to_all(jnp.broadcast_to(row[None], (n,) + row.shape), axes, 0, 0)  8.89 us
    all_to_all x1, starting transfers between devices, shards(): allc = lax.all_to_all(spread_cents, ('y', 'xh'), 0, 0)  6.65 us
    dynamic_update_slice x7, local copies, waits for them, and re-layouts, put(): return lax.dynamic_update_slice(buf, part[None], (at % NZ, 0, 0))  5.46 us
    ppermute x1, waiting for transfers between devices, shards(): up2 = lax.ppermute(up1, 'z', UP)  5.25 us
    ppermute x1, starting transfers between devices, shards(): tots = (tots, lax.ppermute(tots, 'c', SWAP))  5.01 us
  transfers between devices with their start and end apart: 19, of which 10 were waited for; matrix products, arithmetic and copies ran while one was open for 14% of the time, Pallas kernels for 0%

profile of v7, /device:TPU:1, one launch (start us, length us, event | category | flops | bytes accessed | tf_op | source)
XLA Modules:
  0.0 183.0 jit_solution(5734639411904204617)
XLA Ops:
  0.0 2.5 %collective-permute-start = (bf16[128,1536]{1,0:T(8,128)(2,1)}, bf16[128,1536]{1,0:T(8,128)(2,1)S(1)}, u32[]{:S(2)}, u32[]{:S(2)}) collective-permute-start(bf16[128,1536]{1,0:T(8,128)(2,1)} %param.17), channel_id=1, source_target_pairs={{0,1},{1,2},{2,3},{3,4},{4,5},{5,6},{6,7},{7,0},{8,9},{9,10},{10,1... | collective-permute-start | bytes 1179656 | tf_op jit(solution)/shard_map/ppermute | solution.py:37
  2.6 4.0 %collective-permute-start.5 = (bf16[128,1536]{1,0:T(8,128)(2,1)}, bf16[128,1536]{1,0:T(8,128)(2,1)S(1)}, u32[]{:S(2)}, u32[]{:S(2)}) collective-permute-start(bf16[128,1536]{1,0:T(8,128)(2,1)} %param.17), channel_id=1, source_target_pairs={{0,7},{1,0},{2,1},{3,2},{4,3},{5,4},{6,5},{7,6},{8,15},{9,8},{10,9... | collective-permute-start | bytes 1179656 | tf_op jit(solution)/shard_map/ppermute | solution.py:38
  6.6 2.2 %broadcast_in_dim.90 = bf16[8,64,1536]{2,1,0:T(8,128)(2,1)} broadcast(bf16[64,1536]{1,0:T(8,128)(2,1)} %param.18), dimensions={1,2} | broadcast | bytes 1769472 | tf_op jit(solution)/shard_map/broadcast_in_dim | solution.py:35
  8.8 6.7 %all-to-all-start = ((bf16[8,64,1536]{2,1,0:T(8,128)(2,1)}), bf16[8,64,1536]{2,1,0:T(8,128)(2,1)S(1)}, u32[]{:S(2)}, u32[]{:S(2)}) async-start(bf16[8,64,1536]{2,1,0:T(8,128)(2,1)} %broadcast_in_dim.90), calls=%async_computation | async-start | bytes 3145728 | tf_op jit(solution)/shard_map/all_to_all | solution.py:36
  15.4 0.5 multiply_add_fusion
  16.1 1.3 collective-permute-start.2
  17.4 2.8 %collective-permute-start.6 = (bf16[128,1536]{1,0:T(8,128)(2,1)S(1)}, bf16[128,1536]{1,0:T(8,128)(2,1)S(1)}, u32[]{:S(2)}, u32[]{:S(2)}) collective-permute-start(bf16[128,1536]{1,0:T(8,128)(2,1)S(1)} %collective-permute-done.5), channel_id=1, source_target_pairs={{0,7},{1,0},{2,1},{3,2},{4,3},{5,4},{6,5},{7,6},{8,15},{9,8},{10,9... | collective-permute-start | bytes 1179656 | tf_op jit(solution)/shard_map/ppermute | solution.py:43
  20.2 2.2 %broadcast_in_dim.159 = bf16[10,128,1536]{2,1,0:T(8,128)(2,1)} broadcast(bf16[128,1536]{1,0:T(8,128)(2,1)S(1)} %copy-done.2), dimensions={1,2} | broadcast | bytes 4325376 | tf_op jit(solution)/shard_map/broadcast_in_dim | solution.py:44
  22.4 0.8 bitcast_dynamic-update-slice_fusion.6
  23.2 0.8 bitcast_dynamic-update-slice_fusion.5
  24.0 5.3 %collective-permute-done.1 = bf16[128,1536]{1,0:T(8,128)(2,1)S(1)} collective-permute-done((bf16[128,1536]{1,0:T(8,128)(2,1)S(1)}, bf16[128,1536]{1,0:T(8,128)(2,1)S(1)}, u32[]{:S(2)}, u32[]{:S(2)}) %collective-permute-start.1) | collective-permute-done | bytes 393248 | tf_op jit(solution)/shard_map/ppermute | solution.py:42
  29.2 2.7 %collective-permute-start.8 = (bf16[128,1536]{1,0:T(8,128)(2,1)S(1)}, bf16[128,1536]{1,0:T(8,128)(2,1)S(1)}, u32[]{:S(2)}, u32[]{:S(2)}) collective-permute-start(bf16[128,1536]{1,0:T(8,128)(2,1)S(1)} %collective-permute-done.6), channel_id=1, source_target_pairs={{0,7},{1,0},{2,1},{3,2},{4,3},{5,4},{6,5},{7,6},{8,15},{9,8},{10,9... | collective-permute-start | bytes 1179656 | tf_op jit(solution)/shard_map/ppermute | solution.py:47
  31.9 0.8 bitcast_dynamic-update-slice_fusion.4
  32.7 4.4 %all-to-all-done = bf16[8,64,1536]{2,1,0:T(8,128)(2,1)S(1)} async-done(((bf16[8,64,1536]{2,1,0:T(8,128)(2,1)}), bf16[8,64,1536]{2,1,0:T(8,128)(2,1)S(1)}, u32[]{:S(2)}, u32[]{:S(2)}) %all-to-all-start) | async-done | bytes 1572896 | tf_op jit(solution)/shard_map/all_to_all | solution.py:36
  37.1 1.3 gather_fusion.1
  38.4 2.2 %collective-permute-start.3 = (bf16[2,64,1536]{2,1,0:T(8,128)(2,1)}, bf16[2,64,1536]{2,1,0:T(8,128)(2,1)}, u32[]{:S(2)}, u32[]{:S(2)}) collective-permute-start(bf16[2,64,1536]{2,1,0:T(8,128)(2,1)} %gather_fusion.1), channel_id=1, source_target_pairs={{0,16},{16,0},{1,17},{17,1},{2,18},{18,2},{3,19},{19,3},{4,20},{20... | collective-permute-start | bytes 1179656 | tf_op jit(solution)/shard_map/ppermute | solution.py:52
  40.6 0.8 bitcast_dynamic-update-slice_fusion.3
  41.4 0.6 gather_fusion
  41.9 0.3 collective-permute-done.3
  42.3 1.1 broadcast_select_fusion
  43.4 0.4 collective-permute-start.4
  43.8 0.8 bitcast_dynamic-update-slice_fusion.2
  44.6 0.8 bitcast_dynamic-update-slice_fusion.1
  45.4 3.8 %slice.70 = bf16[8,128,1536]{2,1,0:T(8,128)(2,1)} slice(bf16[10,128,1536]{2,1,0:T(8,128)(2,1)} %bitcast_dynamic-update-slice_fusion.1), slice={[0:8], [0:128], [0:1536]} | slice | bytes 6291456 | tf_op jit(solution)/shard_map/slice | solution.py:69
  49.4 0.6 convert_reduce_fusion.1
  50.0 0.6 gather_fusion.2
  51.6 2.2 %collective-permute-done.4 = bf16[2,64,1536]{2,1,0:T(8,128)(2,1)S(1)} collective-permute-done((bf16[2,64,1536]{2,1,0:T(8,128)(2,1)S(1)}, bf16[2,64,1536]{2,1,0:T(8,128)(2,1)S(1)}, u32[]{:S(2)}, u32[]{:S(2)}) %collective-permute-start.4) | collective-permute-done | bytes 393248 | tf_op jit(solution)/shard_map/ppermute | solution.py:55
  53.9 1.0 fusion.1
  55.0 0.4 fusion.4
  55.5 11.9 %all_to_all.58 = f32[8,1,1024]{2,1,0:T(1,128)S(1)} all-to-all(f32[8,1,1024]{2,1,0:T(1,128)S(1)} %broadcast_in_dim.167), channel_id=1, replica_groups=mesh['y'=4,'xh'=2,'c'=2,'xl'=2,'z'=8] {'z'}, dimensions={0} | all-to-all | bytes 65536 | tf_op jit(solution)/shard_map/all_to_all | solution.py:24
  67.4 0.2 multiply_reduce_fusion.5
  67.6 14.3 %all_to_all.59 = f32[32,1,384]{2,1,0:T(1,128)S(1)} all-to-all(f32[32,1,384]{2,1,0:T(1,128)S(1)} %broadcast_in_dim.168), channel_id=1, replica_groups=mesh['y'=4,'xh'=2,'c'=2,'xl'=2,'z'=8] {'y','xh','c','xl'}, dimensions={0} | all-to-all | bytes 98304 | tf_op jit(solution)/shard_map/all_to_all | solution.py:24
  82.3 0.2 multiply_reduce_fusion.4
  82.5 9.2 %all_to_all.60 = f32[8,1,1024]{2,1,0:T(1,128)S(1)} all-to-all(f32[8,1,1024]{2,1,0:T(1,128)S(1)} %broadcast_in_dim.169), channel_id=1, replica_groups=mesh['y'=4,'xh'=2,'c'=2,'xl'=2,'z'=8] {'z'}, dimensions={0} | all-to-all | bytes 65536 | tf_op jit(solution)/shard_map/all_to_all | solution.py:24
  91.8 0.2 multiply_reduce_fusion.3
  91.9 12.0 %all_to_all.61 = f32[32,1,256]{2,1,0:T(1,128)S(1)} all-to-all(f32[32,1,256]{2,1,0:T(1,128)S(1)} %broadcast_in_dim.170), channel_id=1, replica_groups=mesh['y'=4,'xh'=2,'c'=2,'xl'=2,'z'=8] {'y','xh','c','xl'}, dimensions={0} | all-to-all | bytes 65536 | tf_op jit(solution)/shard_map/all_to_all | solution.py:24
  104.1 0.2 multiply_reduce_fusion.2
  104.3 9.3 %all_to_all.62 = f32[8,1,1024]{2,1,0:T(1,128)S(1)} all-to-all(f32[8,1,1024]{2,1,0:T(1,128)S(1)} %broadcast_in_dim.171), channel_id=1, replica_groups=mesh['y'=4,'xh'=2,'c'=2,'xl'=2,'z'=8] {'z'}, dimensions={0} | all-to-all | bytes 65536 | tf_op jit(solution)/shard_map/all_to_all | solution.py:24
  113.7 0.6 broadcast_in_dim.172
  114.4 5.5 %all-to-all-start.6 = ((f32[32,1,256]{2,1,0:T(1,128)}), f32[32,1,256]{2,1,0:T(1,128)S(1)}, u32[]{:S(2)}, u32[]{:S(2)}) async-start(f32[32,1,256]{2,1,0:T(1,128)} %broadcast_in_dim.172), calls=%async_computation.6 | async-start | bytes 65536 | tf_op jit(solution)/shard_map/all_to_all | solution.py:24
  119.9 7.1 %all-to-all-done.6 = f32[32,1,256]{2,1,0:T(1,128)S(1)} async-done(((f32[32,1,256]{2,1,0:T(1,128)}), f32[32,1,256]{2,1,0:T(1,128)S(1)}, u32[]{:S(2)}, u32[]{:S(2)}) %all-to-all-start.6) | async-done | bytes 32800 | tf_op jit(solution)/shard_map/all_to_all | solution.py:24
  127.1 0.2 multiply_reduce_fusion
  127.3 0.6 broadcast_in_dim.173
  127.9 3.3 %all-to-all-start.7 = ((f32[8,1,1024]{2,1,0:T(1,128)}), f32[8,1,1024]{2,1,0:T(1,128)S(1)}, u32[]{:S(2)}, u32[]{:S(2)}) async-start(f32[8,1,1024]{2,1,0:T(1,128)} %broadcast_in_dim.173), calls=%async_computation.7 | async-start | bytes 65536 | tf_op jit(solution)/shard_map/all_to_all | solution.py:24
  131.2 0.8 bitcast_dynamic-update-slice_fusion
  132.0 3.8 %slice.72 = bf16[8,128,1536]{2,1,0:T(8,128)(2,1)} slice(bf16[10,128,1536]{2,1,0:T(8,128)(2,1)} %bitcast_dynamic-update-slice_fusion), slice={[0:8], [0:128], [0:1536]} | slice | bytes 6291456 | tf_op jit(solution)/shard_map/slice | solution.py:95
  135.8 2.3 %all-to-all-done.7 = f32[8,1,1024]{2,1,0:T(1,128)S(1)} async-done(((f32[8,1,1024]{2,1,0:T(1,128)}), f32[8,1,1024]{2,1,0:T(1,128)S(1)}, u32[]{:S(2)}, u32[]{:S(2)}) %all-to-all-start.7) | async-done | bytes 32800 | tf_op jit(solution)/shard_map/all_to_all | solution.py:24
  138.3 2.6 %fusion.7 = f32[128,1536]{1,0:T(8,128)S(1)} fusion(bf16[1024,1536]{1,0:T(8,128)(2,1)} %bitcast.111, bf16[256,1024]{1,0:T(8,128)(2,1)S(1)} %multiply_convert_fusion), kind=kOutput, calls=%fused_computation.37 | convolution fusion | flops 402653184 | bytes 4194304 | tf_op jit(solution)/shard_map/dot_general | solution.py:136
  141.0 0.5 collective-permute-start.10
  141.5 0.3 fusion.11
  141.8 1.2 collective-permute-start.11
  142.9 0.6 fusion.36
  143.6 0.5 collective-permute-start.12
  144.0 3.0 %collective-permute-done.11 = f32[2,64,128]{2,1,0:T(8,128)S(1)} collective-permute-done((f32[2,64,128]{2,1,0:T(8,128)S(1)}, f32[2,64,128]{2,1,0:T(8,128)S(1)}, u32[]{:S(2)}, u32[]{:S(2)}) %collective-permute-start.11) | collective-permute-done | bytes 65568 | tf_op jit(solution)/shard_map/ppermute | solution.py:113
  147.0 5.0 %collective-permute-start.14 = (f32[2,64,128]{2,1,0:T(8,128)S(1)}, f32[2,64,128]{2,1,0:T(8,128)S(1)}, u32[]{:S(2)}, u32[]{:S(2)}) collective-permute-start(f32[2,64,128]{2,1,0:T(8,128)S(1)} %bitcast_add_fusion.2), channel_id=1, source_target_pairs={{0,16},{16,0},{1,17},{17,1},{2,18},{18,2},{3,19},{19,3},{4,20},{20... | collective-permute-start | bytes 196616 | tf_op jit(solution)/shard_map/ppermute | solution.py:121
  152.0 0.9 collective-permute-done.14
  153.0 0.4 collective-permute-start.13
  153.5 0.6 collective-permute-start.15
  154.2 0.4 collective-permute-done.13
  154.6 0.7 collective-permute-done.15
  155.2 0.5 select_add_fusion
  155.8 26.0 %all_to_all.63 = bf16[8,64,1664]{2,1,0:T(8,128)(2,1)S(1)} all-to-all(bf16[8,64,1664]{2,1,0:T(8,128)(2,1)S(1)} %select_add_fusion), channel_id=1, replica_groups=mesh['y'=4,'xh'=2,'c'=2,'xl'=2,'z'=8] {'y','xh'}, dimensions={0} | all-to-all | bytes 3407872 | tf_op jit(solution)/shard_map/all_to_all | solution.py:151
  181.8 0.2 convert_reduce_fusion
  182.2 0.9 slice_divide_fusion
  (107 shorter events, 2.5 us)
Async XLA Ops:
  0.0 20.2 %copy-start.2 = (bf16[128,1536]{1,0:T(8,128)(2,1)S(1)}, bf16[128,1536]{1,0:T(8,128)(2,1)}, u32[]{:S(2)}) copy-start(bf16[128,1536]{1,0:T(8,128)(2,1)} %param.17) | copy-start | bytes 1179652
  0.0 16.0 %copy-start.11 = (s32[1,2]{1,0:T(1,128)S(1)}, s32[1,2]{1,0:T(1,128)}, u32[]{:S(2)}) copy-start(s32[1,2]{1,0:T(1,128)} %param.20) | copy-start | bytes 28
  0.0 16.1 %copy-start.4 = (s32[1,2]{1,0:T(1,128)S(1)}, s32[1,2]{1,0:T(1,128)}, u32[]{:S(2)}) copy-start(s32[1,2]{1,0:T(1,128)} %param.19) | copy-start | bytes 28
  0.0 16.1 %collective-permute-start = (bf16[128,1536]{1,0:T(8,128)(2,1)}, bf16[128,1536]{1,0:T(8,128)(2,1)S(1)}, u32[]{:S(2)}, u32[]{:S(2)}) collective-permute-start(bf16[128,1536]{1,0:T(8,128)(2,1)} %param.17), channel_id=1, source_target_pairs={{0,1},{1,2},{2,3},{3,4},{4,5},{5,6},{6,7},{7,0},{8,9},{9,10},{10,1... | collective-permute-start | bytes 1179656 | tf_op jit(solution)/shard_map/ppermute | solution.py:37
  2.6 14.8 %collective-permute-start.5 = (bf16[128,1536]{1,0:T(8,128)(2,1)}, bf16[128,1536]{1,0:T(8,128)(2,1)S(1)}, u32[]{:S(2)}, u32[]{:S(2)}) collective-permute-start(bf16[128,1536]{1,0:T(8,128)(2,1)} %param.17), channel_id=1, source_target_pairs={{0,7},{1,0},{2,1},{3,2},{4,3},{5,4},{6,5},{7,6},{8,15},{9,8},{10,9... | collective-permute-start | bytes 1179656 | tf_op jit(solution)/shard_map/ppermute | solution.py:38
  8.8 28.3 %all-to-all-start = ((bf16[8,64,1536]{2,1,0:T(8,128)(2,1)}), bf16[8,64,1536]{2,1,0:T(8,128)(2,1)S(1)}, u32[]{:S(2)}, u32[]{:S(2)}) async-start(bf16[8,64,1536]{2,1,0:T(8,128)(2,1)} %broadcast_in_dim.90), calls=%async_computation | async-start | bytes 3145728 | tf_op jit(solution)/shard_map/all_to_all | solution.py:36
  16.1 7.9 %collective-permute-start.2 = (s32[2]{0:T(128)S(1)}, s32[2]{0:T(128)S(1)}, u32[]{:S(2)}, u32[]{:S(2)}) collective-permute-start(s32[2]{0:T(128)S(1)} %bitcast.128), channel_id=1, source_target_pairs={{0,16},{16,0},{1,17},{17,1},{2,18},{18,2},{3,19},{19,3},{4,20},{20... | collective-permute-start | bytes 32 | tf_op jit(solution)/shard_map/ppermute | solution.py:41
  17.3 11.9 %collective-permute-start.1 = (bf16[128,1536]{1,0:T(8,128)(2,1)S(1)}, bf16[128,1536]{1,0:T(8,128)(2,1)S(1)}, u32[]{:S(2)}, u32[]{:S(2)}) collective-permute-start(bf16[128,1536]{1,0:T(8,128)(2,1)S(1)} %collective-permute-done), channel_id=1, source_target_pairs={{0,1},{1,2},{2,3},{3,4},{4,5},{5,6},{6,7},{7,0},{8,9},{9,10},{10,1... | collective-permute-start | bytes 1179656 | tf_op jit(solution)/shard_map/ppermute | solution.py:42
  17.4 11.8 %collective-permute-start.6 = (bf16[128,1536]{1,0:T(8,128)(2,1)S(1)}, bf16[128,1536]{1,0:T(8,128)(2,1)S(1)}, u32[]{:S(2)}, u32[]{:S(2)}) collective-permute-start(bf16[128,1536]{1,0:T(8,128)(2,1)S(1)} %collective-permute-done.5), channel_id=1, source_target_pairs={{0,7},{1,0},{2,1},{3,2},{4,3},{5,4},{6,5},{7,6},{8,15},{9,8},{10,9... | collective-permute-start | bytes 1179656 | tf_op jit(solution)/shard_map/ppermute | solution.py:43
  23.9 8.0 %copy-start.12 = (s32[2]{0:T(128)}, s32[2]{0:T(128)S(1)}, u32[]{:S(2)}) copy-start(s32[2]{0:T(128)S(1)} %collective-permute-done.2) | copy-start | bytes 28
  29.2 14.5 %collective-permute-start.7 = (bf16[128,1536]{1,0:T(8,128)(2,1)S(1)}, bf16[128,1536]{1,0:T(8,128)(2,1)S(1)}, u32[]{:S(2)}, u32[]{:S(2)}) collective-permute-start(bf16[128,1536]{1,0:T(8,128)(2,1)S(1)} %collective-permute-done.1), channel_id=1, source_target_pairs={{0,1},{1,2},{2,3},{3,4},{4,5},{5,6},{6,7},{7,0},{8,9},{9,10},{10,1... | collective-permute-start | bytes 1179656 | tf_op jit(solution)/shard_map/ppermute | solution.py:46
  29.2 14.5 %collective-permute-start.8 = (bf16[128,1536]{1,0:T(8,128)(2,1)S(1)}, bf16[128,1536]{1,0:T(8,128)(2,1)S(1)}, u32[]{:S(2)}, u32[]{:S(2)}) collective-permute-start(bf16[128,1536]{1,0:T(8,128)(2,1)S(1)} %collective-permute-done.6), channel_id=1, source_target_pairs={{0,7},{1,0},{2,1},{3,2},{4,3},{5,4},{6,5},{7,6},{8,15},{9,8},{10,9... | collective-permute-start | bytes 1179656 | tf_op jit(solution)/shard_map/ppermute | solution.py:47
  38.4 3.9 %collective-permute-start.3 = (bf16[2,64,1536]{2,1,0:T(8,128)(2,1)}, bf16[2,64,1536]{2,1,0:T(8,128)(2,1)}, u32[]{:S(2)}, u32[]{:S(2)}) collective-permute-start(bf16[2,64,1536]{2,1,0:T(8,128)(2,1)} %gather_fusion.1), channel_id=1, source_target_pairs={{0,16},{16,0},{1,17},{17,1},{2,18},{18,2},{3,19},{19,3},{4,20},{20... | collective-permute-start | bytes 1179656 | tf_op jit(solution)/shard_map/ppermute | solution.py:52
  43.4 10.4 %collective-permute-start.4 = (bf16[2,64,1536]{2,1,0:T(8,128)(2,1)S(1)}, bf16[2,64,1536]{2,1,0:T(8,128)(2,1)S(1)}, u32[]{:S(2)}, u32[]{:S(2)}) collective-permute-start(bf16[2,64,1536]{2,1,0:T(8,128)(2,1)S(1)} %broadcast_select_fusion), channel_id=1, source_target_pairs={{0,8},{8,0},{1,9},{9,1},{2,10},{10,2},{3,11},{11,3},{4,12},{12,4},... | collective-permute-start | bytes 1179656 | tf_op jit(solution)/shard_map/ppermute | solution.py:55
  43.8 11.2 %collective-permute-start.9 = (bf16[128,1536]{1,0:T(8,128)(2,1)S(1)}, bf16[128,1536]{1,0:T(8,128)(2,1)S(1)}, u32[]{:S(2)}, u32[]{:S(2)}) collective-permute-start(bf16[128,1536]{1,0:T(8,128)(2,1)S(1)} %collective-permute-done.7), channel_id=1, source_target_pairs={{0,1},{1,2},{2,3},{3,4},{4,5},{5,6},{6,7},{7,0},{8,9},{9,10},{10,1... | collective-permute-start | bytes 1179656 | tf_op jit(solution)/shard_map/ppermute | solution.py:57
  45.4 4.0 %copy-start.3 = (s32[16384]{0:T(1024)S(1)}, s32[16384]{0:T(1024)}, u32[]{:S(2)}) copy-start(s32[16384]{0:T(1024)} %param.21) | copy-start | bytes 196612
  45.4 6.0 %copy-start.13 = (s32[2]{0:T(128)S(1)}, s32[2]{0:T(128)}, u32[]{:S(2)}) copy-start(s32[2]{0:T(128)} %copy-done.12) | copy-start | bytes 28
  45.4 6.1 %copy-start.14 = (s32[8]{0:T(128)S(1)}, s32[8]{0:T(128)}, u32[]{:S(2)}) copy-start(s32[8]{0:T(128)} %multiply_add_fusion) | copy-start | bytes 100
  51.4 2.5 %copy-start.1 = (bf16[8,128,1536]{2,1,0:T(8,128)(2,1)S(1)}, bf16[8,128,1536]{2,1,0:T(8,128)(2,1)}, u32[]{:S(2)}) copy-start(bf16[8,128,1536]{2,1,0:T(8,128)(2,1)} %slice.70) | copy-start | bytes 9437188
  114.4 12.6 %all-to-all-start.6 = ((f32[32,1,256]{2,1,0:T(1,128)}), f32[32,1,256]{2,1,0:T(1,128)S(1)}, u32[]{:S(2)}, u32[]{:S(2)}) async-start(f32[32,1,256]{2,1,0:T(1,128)} %broadcast_in_dim.172), calls=%async_computation.6 | async-start | bytes 65536 | tf_op jit(solution)/shard_map/all_to_all | solution.py:24
  127.9 10.1 %all-to-all-start.7 = ((f32[8,1,1024]{2,1,0:T(1,128)}), f32[8,1,1024]{2,1,0:T(1,128)S(1)}, u32[]{:S(2)}, u32[]{:S(2)}) async-start(f32[8,1,1024]{2,1,0:T(1,128)} %broadcast_in_dim.173), calls=%async_computation.7 | async-start | bytes 65536 | tf_op jit(solution)/shard_map/all_to_all | solution.py:24
  138.2 4.7 %copy-start = (bf16[8,128,1536]{2,1,0:T(8,128)(2,1)S(1)}, bf16[8,128,1536]{2,1,0:T(8,128)(2,1)}, u32[]{:S(2)}) copy-start(bf16[8,128,1536]{2,1,0:T(8,128)(2,1)} %slice.72) | copy-start | bytes 9437188
  140.9 11.1 %copy-start.8 = (f32[128]{0:T(128)S(1)}, f32[128]{0:T(128)}, u32[]{:S(2)}) copy-start(f32[128]{0:T(128)} %constant.181) | copy-start | bytes 1540
  140.9 11.1 %copy-start.9 = (f32[128]{0:T(128)S(1)}, f32[128]{0:T(128)}, u32[]{:S(2)}) copy-start(f32[128]{0:T(128)} %constant.182) | copy-start | bytes 1540
  140.9 11.1 %copy-start.10 = (f32[128]{0:T(128)S(1)}, f32[128]{0:T(128)}, u32[]{:S(2)}) copy-start(f32[128]{0:T(128)} %constant.183) | copy-start | bytes 1540
  140.9 12.0 %copy-start.5 = (f32[128]{0:T(128)S(1)}, f32[128]{0:T(128)}, u32[]{:S(2)}) copy-start(f32[128]{0:T(128)} %constant.184) | copy-start | bytes 1540
  140.9 12.0 %copy-start.6 = (f32[128]{0:T(128)S(1)}, f32[128]{0:T(128)}, u32[]{:S(2)}) copy-start(f32[128]{0:T(128)} %constant.185) | copy-start | bytes 1540
  140.9 12.0 %copy-start.7 = (f32[128]{0:T(128)S(1)}, f32[128]{0:T(128)}, u32[]{:S(2)}) copy-start(f32[128]{0:T(128)} %constant.186) | copy-start | bytes 1540
  141.0 12.0 %collective-permute-start.10 = (bf16[64,1536]{1,0:T(8,128)(2,1)S(1)}, bf16[64,1536]{1,0:T(8,128)(2,1)S(1)}, u32[]{:S(2)}, u32[]{:S(2)}) collective-permute-start(bf16[64,1536]{1,0:T(8,128)(2,1)S(1)} %fusion.9), channel_id=1, source_target_pairs={{0,8},{8,0},{1,9},{9,1},{2,10},{10,2},{3,11},{11,3},{4,12},{12,4},... | collective-permute-start | bytes 589832 | tf_op jit(solution)/shard_map/ppermute | solution.py:141
  141.8 5.2 %collective-permute-start.11 = (f32[2,64,128]{2,1,0:T(8,128)S(1)}, f32[2,64,128]{2,1,0:T(8,128)S(1)}, u32[]{:S(2)}, u32[]{:S(2)}) collective-permute-start(f32[2,64,128]{2,1,0:T(8,128)S(1)} %dynamic-slice_bitcast_fusion), channel_id=1, source_target_pairs={{0,8},{8,0},{1,9},{9,1},{2,10},{10,2},{3,11},{11,3},{4,12},{12,4},... | collective-permute-start | bytes 196616 | tf_op jit(solution)/shard_map/ppermute | solution.py:113
  143.6 9.9 %collective-permute-start.12 = (bf16[64,1536]{1,0:T(8,128)(2,1)S(1)}, bf16[64,1536]{1,0:T(8,128)(2,1)S(1)}, u32[]{:S(2)}, u32[]{:S(2)}) collective-permute-start(bf16[64,1536]{1,0:T(8,128)(2,1)S(1)} %fusion.10), channel_id=1, source_target_pairs={{0,8},{8,0},{1,9},{9,1},{2,10},{10,2},{3,11},{11,3},{4,12},{12,4},... | collective-permute-start | bytes 589832 | tf_op jit(solution)/shard_map/ppermute | solution.py:141
  147.0 5.9 %collective-permute-start.14 = (f32[2,64,128]{2,1,0:T(8,128)S(1)}, f32[2,64,128]{2,1,0:T(8,128)S(1)}, u32[]{:S(2)}, u32[]{:S(2)}) collective-permute-start(f32[2,64,128]{2,1,0:T(8,128)S(1)} %bitcast_add_fusion.2), channel_id=1, source_target_pairs={{0,16},{16,0},{1,17},{17,1},{2,18},{18,2},{3,19},{19,3},{4,20},{20... | collective-permute-start | bytes 196616 | tf_op jit(solution)/shard_map/ppermute | solution.py:121
  153.0 1.5 collective-permute-start.13
  153.5 1.7 collective-permute-start.15
